TPU v7x, 32 devices: a whole 2x2x4 slice. The times are simulated.
32 devices in a mesh: wide: 8 (over z, x), narrow: 4 (over y, core).
Axes of the slice: x: 2, y: 2, z: 4, core: 2. Of those that a mesh axis runs over, the one named last changes fastest.
Arguments:
- tokens: bfloat16 [32, 448, 768], P('wide'), may hold values from -6 to 6
- lengths: int32 [32], P('wide'), may hold values from 1 to 448, 7168 in all
- memory: bfloat16 [32, 1536, 768], P(None, 'wide'), may hold values from -6 to 6
- gains: float32 [4, 768], replicated, may hold values from 0.5 to 1.5
- self_qkv: bfloat16 [3, 768, 768], P(None, None, 'narrow'), may hold values from -0.21875 to 0.21875
- self_out: bfloat16 [768, 768], P('narrow'), may hold values from -1.5 to 1.5
- cross_q: bfloat16 [768, 768], P(None, 'narrow'), may hold values from -0.21875 to 0.21875
- cross_kv: bfloat16 [2, 768, 768], P(None, None, 'narrow'), may hold values from -0.21875 to 0.21875
- cross_out: bfloat16 [768, 768], P('narrow'), may hold values from -4 to 4
- fc_in: bfloat16 [768, 3072], P(None, 'narrow'), may hold values from -0.21875 to 0.21875
- fc_out: bfloat16 [3072, 768], P('narrow'), may hold values from -0.109375 to 0.109375
- out_grad: bfloat16 [32, 448, 768], P('wide'), may hold values from -6 to 6
Outputs:
- block_out: bfloat16 [32, 448, 768], P('wide')
- tokens_grad: bfloat16 [32, 448, 768], P('wide')
- memory_grad: bfloat16 [32, 1536, 768], P(None, 'wide')
- gains_grad: float32 [4, 768], P(None, 'wide')
- self_qkv_grad: float32 [3, 768, 768], P(None, 'wide', 'narrow')
- self_out_grad: float32 [768, 768], P('narrow', 'wide')
- cross_q_grad: float32 [768, 768], P('wide', 'narrow')
- cross_kv_grad: float32 [2, 768, 768], P(None, 'wide', 'narrow')
- cross_out_grad: float32 [768, 768], P('narrow', 'wide')
- fc_in_grad: float32 [768, 3072], P('wide', 'narrow')
- fc_out_grad: float32 [3072, 768], P('narrow', 'wide')
Inputs may be any that keep to these rules, and one draw needn't show every extreme that they name: `lengths`: some clip has exactly 448 tokens in every draw.
All inputs are finite; a program needn't handle non-finite values. No bound on the sum of `lengths` on one device may be relied on, other than what follows from the above.
Results may differ from a plain program's by a relative error of at most 0.019.
Values may be sent and summed in bfloat16 or wider, within the bound.
No kernel may reach another device: no remote copies, remote signals or barrier semaphores. Data moves between devices by JAX's collectives and lax.ppermute only.
A program may use at most 384 MiB of HBM per device.

v0:
```python
import jax
import jax.numpy as jnp
from jax import lax
from jax.sharding import PartitionSpec as P

HEAD_DIM = 64
AUDIO = 1500


EPSILON = 1e-05
NEG_FILL = -1e30


def norm_rows(values, gain_row):
    center = values - jnp.mean(values, axis=-1, keepdims=True)
    spread = jnp.mean(center * center, axis=-1, keepdims=True)
    return center * lax.rsqrt(spread + EPSILON) * gain_row


def gelu_exact(values):
    return jax.nn.gelu(values, approximate=False)


def rows_dot(left, right):
    return jnp.dot(left, right, preferred_element_type=jnp.float32)


def right_dot(left, right):
    return lax.dot_general(
        left, right, (((1,), (1,)), ((), ())), preferred_element_type=jnp.float32
    )


def outer_sum(left, right):
    return lax.dot_general(
        left, right, (((0,), (0,)), ((), ())), preferred_element_type=jnp.float32
    )


def split_heads(values):
    return values.reshape(values.shape[:-1] + (values.shape[-1] // HEAD_DIM, HEAD_DIM))


def attend(queries, key_rows, value_rows, allowed):
    scores = jnp.einsum(
        "cshd,cthd->chst",
        split_heads(queries),
        split_heads(key_rows),
        preferred_element_type=jnp.float32,
    ) * HEAD_DIM ** (-0.5)
    masked = jnp.where(allowed, scores, NEG_FILL)
    log_total = jax.nn.logsumexp(masked, axis=-1, keepdims=True)
    attn_probs = jnp.exp(masked - log_total).astype(jnp.bfloat16)
    mixture = jnp.einsum(
        "chst,cthd->cshd", attn_probs, split_heads(value_rows), preferred_element_type=jnp.float32
    )
    return (mixture.reshape(queries.shape).astype(jnp.bfloat16), log_total)


def attend_back(queries, key_rows, value_rows, allowed, log_total, grad_mixture):
    inverse_root = HEAD_DIM ** (-0.5)
    query_heads = split_heads(queries)
    key_heads = split_heads(key_rows)
    value_heads = split_heads(value_rows)
    grad_heads = split_heads(grad_mixture)
    scores = (
        jnp.einsum("cshd,cthd->chst", query_heads, key_heads, preferred_element_type=jnp.float32)
        * inverse_root
    )
    masked = jnp.where(allowed, scores, NEG_FILL)
    attn_probs = jnp.exp(masked - log_total)
    grad_probs = jnp.einsum(
        "cshd,cthd->chst", grad_heads, value_heads, preferred_element_type=jnp.float32
    )
    inner_sum = jnp.sum(attn_probs * grad_probs, axis=-1, keepdims=True)
    grad_scores = (attn_probs * (grad_probs - inner_sum)).astype(jnp.bfloat16)
    grad_query = (
        jnp.einsum("chst,cthd->cshd", grad_scores, key_heads, preferred_element_type=jnp.float32)
        * inverse_root
    )
    grad_key = (
        jnp.einsum("chst,cshd->cthd", grad_scores, query_heads, preferred_element_type=jnp.float32)
        * inverse_root
    )
    grad_value = jnp.einsum(
        "chst,cshd->cthd",
        attn_probs.astype(jnp.bfloat16),
        grad_heads,
        preferred_element_type=jnp.float32,
    )
    return (
        grad_query.reshape(queries.shape).astype(jnp.bfloat16),
        grad_key.reshape(key_rows.shape).astype(jnp.bfloat16),
        grad_value.reshape(value_rows.shape).astype(jnp.bfloat16),
    )


def on_device(
    tokens,
    lengths,
    memory,
    gains,
    self_qkv,
    self_out,
    cross_q,
    cross_kv,
    cross_out,
    fc_in,
    fc_out,
    out_grad,
):
    clip_count, seq_len, model_width = tokens.shape
    row_count = clip_count * seq_len
    wide_count = lax.axis_size("wide")
    frame_share = memory.shape[1]
    frames = frame_share * wide_count
    positions = jnp.arange(seq_len)
    live_rows = positions[None, :] < lengths[:, None]
    self_allowed = (positions[None, :] <= positions[:, None])[None, None] & live_rows[
        :, None, None, :
    ]
    cross_allowed = (jnp.arange(frames) < AUDIO)[None, None, None, :]
    encoded_full, encoder_back = jax.vjp(norm_rows, memory.astype(jnp.float32), gains[0])
    encoded = encoded_full.astype(jnp.bfloat16)
    clip_memory = lax.all_to_all(encoded, "wide", split_axis=0, concat_axis=1, tiled=True)
    key_value = jnp.einsum(
        "cfd,kde->kcfe", clip_memory, cross_kv, preferred_element_type=jnp.float32
    ).astype(jnp.bfloat16)
    token_input = tokens.astype(jnp.float32)
    normed_full, back_one = jax.vjp(norm_rows, token_input, gains[1])
    normed_one = normed_full.astype(jnp.bfloat16)
    projected = jnp.einsum(
        "csd,kde->kcse", normed_one, self_qkv, preferred_element_type=jnp.float32
    ).astype(jnp.bfloat16)
    self_mixed, self_total = attend(projected[0], projected[1], projected[2], self_allowed)
    self_part = rows_dot(self_mixed.reshape(row_count, -1), self_out).reshape(
        clip_count, seq_len, model_width
    )
    after_self = token_input + lax.psum(self_part, "narrow")
    normed_full, back_two = jax.vjp(norm_rows, after_self, gains[2])
    normed_two = normed_full.astype(jnp.bfloat16).reshape(row_count, model_width)
    cross_query = (
        rows_dot(normed_two, cross_q).astype(jnp.bfloat16).reshape(clip_count, seq_len, -1)
    )
    cross_mixed, cross_total = attend(cross_query, key_value[0], key_value[1], cross_allowed)
    cross_part = rows_dot(cross_mixed.reshape(row_count, -1), cross_out).reshape(
        clip_count, seq_len, model_width
    )
    after_cross = after_self + lax.psum(cross_part, "narrow")
    normed_full, back_three = jax.vjp(norm_rows, after_cross, gains[3])
    normed_three = normed_full.astype(jnp.bfloat16).reshape(row_count, model_width)
    hidden_pre = rows_dot(normed_three, fc_in)
    activated, gelu_back = jax.vjp(gelu_exact, hidden_pre)
    hidden_low = activated.astype(jnp.bfloat16)
    feed_part = rows_dot(hidden_low, fc_out).reshape(clip_count, seq_len, model_width)
    block_out = after_cross + lax.psum(feed_part.astype(jnp.bfloat16), "narrow").astype(jnp.float32)
    grad_output = out_grad.astype(jnp.float32) * live_rows[:, :, None].astype(jnp.float32)
    grad_three = grad_output.astype(jnp.bfloat16).reshape(row_count, model_width)
    grad_fc_out = outer_sum(hidden_low, grad_three)
    grad_pre = gelu_back(right_dot(grad_three, fc_out))[0].astype(jnp.bfloat16)
    grad_fc_in = outer_sum(normed_three, grad_pre)
    grad_normed = lax.psum(
        right_dot(grad_pre, fc_in).reshape(clip_count, seq_len, model_width), "narrow"
    )
    back_rows, gain_three = back_three(grad_normed)
    grad_cross = grad_output + back_rows
    grad_two = grad_cross.astype(jnp.bfloat16).reshape(row_count, model_width)
    grad_cross_out = outer_sum(cross_mixed.reshape(row_count, -1), grad_two)
    grad_cross_mixed = (
        right_dot(grad_two, cross_out).astype(jnp.bfloat16).reshape(clip_count, seq_len, -1)
    )
    grad_cross_query, grad_keys, grad_values = attend_back(
        cross_query, key_value[0], key_value[1], cross_allowed, cross_total, grad_cross_mixed
    )
    grad_query_rows = grad_cross_query.reshape(row_count, -1)
    grad_cross_q = outer_sum(normed_two, grad_query_rows)
    grad_normed = lax.psum(
        right_dot(grad_query_rows, cross_q).reshape(clip_count, seq_len, model_width), "narrow"
    )
    back_rows, gain_two = back_two(grad_normed)
    grad_self = grad_cross + back_rows
    grad_one = grad_self.astype(jnp.bfloat16).reshape(row_count, model_width)
    grad_self_out = outer_sum(self_mixed.reshape(row_count, -1), grad_one)
    grad_self_mixed = (
        right_dot(grad_one, self_out).astype(jnp.bfloat16).reshape(clip_count, seq_len, -1)
    )
    grad_triple = jnp.stack(
        attend_back(
            projected[0], projected[1], projected[2], self_allowed, self_total, grad_self_mixed
        )
    )
    grad_self_qkv = jnp.einsum(
        "csd,kcse->kde", normed_one, grad_triple, preferred_element_type=jnp.float32
    )
    grad_normed = lax.psum(
        jnp.einsum("kcse,kde->csd", grad_triple, self_qkv, preferred_element_type=jnp.float32),
        "narrow",
    )
    back_rows, gain_one = back_one(grad_normed)
    tokens_grad = (grad_self + back_rows).astype(jnp.bfloat16)
    grad_pair = jnp.stack((grad_keys, grad_values))
    grad_cross_kv = jnp.einsum(
        "cfd,kcfe->kde", clip_memory, grad_pair, preferred_element_type=jnp.float32
    )
    clip_terms = jnp.einsum(
        "kcfe,kde->cfd", grad_pair, cross_kv, preferred_element_type=jnp.float32
    )
    clip_grad = lax.psum(clip_terms, "narrow")
    grad_encoded = lax.all_to_all(
        clip_grad.astype(jnp.bfloat16), "wide", split_axis=1, concat_axis=0, tiled=True
    )
    memory_back, gain_zero = encoder_back(grad_encoded.astype(jnp.float32))
    memory_grad = memory_back.astype(jnp.bfloat16)
    reduced = (
        lax.psum_scatter(
            jnp.stack((gain_zero, gain_one, gain_two, gain_three)),
            "wide",
            scatter_dimension=1,
            tiled=True,
        ),
        lax.psum_scatter(grad_self_qkv, "wide", scatter_dimension=1, tiled=True),
        lax.psum_scatter(grad_self_out, "wide", scatter_dimension=1, tiled=True),
        lax.psum_scatter(grad_cross_q, "wide", scatter_dimension=0, tiled=True),
        lax.psum_scatter(grad_cross_kv, "wide", scatter_dimension=1, tiled=True),
        lax.psum_scatter(grad_cross_out, "wide", scatter_dimension=1, tiled=True),
        lax.psum_scatter(grad_fc_in, "wide", scatter_dimension=0, tiled=True),
        lax.psum_scatter(grad_fc_out, "wide", scatter_dimension=1, tiled=True),
    )
    gains_grad = reduced[0]
    return (
        block_out.astype(jnp.bfloat16),
        tokens_grad,
        memory_grad,
        gains_grad,
        reduced[1],
        reduced[2],
        reduced[3],
        reduced[4],
        reduced[5],
        reduced[6],
        reduced[7],
    )


def solution(mesh):
    placed = (
        P("wide", None, None),
        P("wide"),
        P(None, "wide", None),
        P(),
        P(None, None, "narrow"),
        P("narrow", None),
        P(None, "narrow"),
        P(None, None, "narrow"),
        P("narrow", None),
        P(None, "narrow"),
        P("narrow", None),
        P("wide", None, None),
    )
    return jax.shard_map(
        on_device,
        mesh=mesh,
        in_specs=placed,
        out_specs=(
            P("wide", None, None),
            P("wide", None, None),
            P(None, "wide", None),
            P(None, "wide"),
            P(None, "wide", "narrow"),
            P("narrow", "wide"),
            P("wide", "narrow"),
            P(None, "wide", "narrow"),
            P("narrow", "wide"),
            P("wide", "narrow"),
            P("narrow", "wide"),
        ),
        check_vma=False,
    )
```

profile of v0, /device:TPU:0, one launch (start us, length us, event | category | flops | bytes accessed | tf_op | source)
XLA Modules:
  0.0 1874.5 jit_solution(3459424296826932649)
XLA Ops:
  55.1 108.3 %all-reduce.8.cloned.1.call-done = f32[4,448,768]{2,1,0:T(8,128)} async-done(((f32[4,448,768]{2,1,0:T(8,128)}), f32[4,448,768]{2,1,0:T(8,128)}) %all-reduce.8.cloned.1.call-update) | async-done | bytes 5505040 | tf_op jit(solution)/shard_map/psum | solution.py:139
  174.3 62.6 %all-to-all-done = bf16[32,192,768]{2,1,0:T(8,128)(2,1)} async-done(((bf16[32,192,768]{2,1,0:T(8,128)(2,1)}), bf16[32,192,768]{2,1,0:T(8,128)(2,1)}, u32[]{:S(2)}, u32[]{:S(2)}) %all-to-all-start) | async-done | bytes 9437216 | tf_op jit(solution)/shard_map/all_to_all | solution.py:125
  256.6 13.0 fusion
  269.7 14.7 exponential_reduce_fusion
  285.0 14.8 convolution_convert_fusion.6
  308.2 102.2 %all-reduce.10.cloned.1.call-done = f32[4,448,768]{2,1,0:T(8,128)} async-done(((f32[4,448,768]{2,1,0:T(8,128)}), f32[4,448,768]{2,1,0:T(8,128)}) %all-reduce.10.cloned.1.call-update) | async-done | bytes 5505040 | tf_op jit(solution)/shard_map/psum | solution.py:149
  420.9 15.4 add_convert_fusion.2
  450.5 97.7 %all-reduce.14.cloned.1.call-done = f32[4,448,768]{2,1,0:T(8,128)} async-done(((f32[4,448,768]{2,1,0:T(8,128)}), f32[4,448,768]{2,1,0:T(8,128)}) %all-reduce.14.cloned.1.call-update) | async-done | bytes 5505040 | tf_op jit(solution)/shard_map/psum | solution.py:162
  553.9 59.3 %all-reduce.12.cloned.1.call-done = bf16[4,448,768]{2,1,0:T(8,128)(2,1)} async-done(((bf16[4,448,768]{2,1,0:T(8,128)(2,1)}), bf16[4,448,768]{2,1,0:T(8,128)(2,1)}) %all-reduce.12.cloned.1.call-update) | async-done | bytes 2752528 | tf_op jit(solution)/shard_map/psum | solution.py:156
  629.0 15.4 convolution_convert_fusion
  644.4 26.1 %multiply_reduce_fusion = (f32[4,3,448]{2,1,0:T(4,128)S(1)}, f32[4,3,448,1536]{3,2,1,0:T(8,128)}) fusion(f32[4,3,448,1536]{3,2,1,0:T(8,128)} %get-tuple-element.66, f32[4,3,448]{2,1,0:T(4,128)S(1)} %copy-done.47, pred[1536]{0:T(1024)(128)(4,1)S(1)} %iota_compare_fusion.1, bf16[4,1536,3,64]{1,3,2,0:T(8,128)(2,1)S(1)} %bitcast.193, ...), kind=kOutput, calls=%fused_computation.1 | convolution fusion | flops 1098246912 | bytes 69152256 | tf_op jit(solution)/shard_map/cshd,cthd->chst/dot_general | solution.py:72
  670.5 27.9 %multiply_convert_fusion = bf16[4,3,448,1536]{3,2,1,0:T(8,128)(2,1)} fusion(f32[4,3,448,1536]{3,2,1,0:T(8,128)} %get-tuple-element.68, f32[4,3,448,1536]{3,2,1,0:T(8,128)} %get-tuple-element.66, f32[4,3,448]{2,1,0:T(4,128)S(1)} %get-tuple-element.67, f32[4,3,448]{2,1,0:T(4,128)S(1)} %copy-done.47, pred[1536]{0:T(1024)(128)(4,1)S(1)} %iota_compare_fusion.1), kind=kLoop, calls=%fused_computation | loop fusion | flops 49545216 | bytes 82619904 | tf_op jit(solution)/shard_map/convert_element_type | solution.py:76
  733.2 396.3 %all-reduce.19 = bf16[4,1536,768]{2,1,0:T(8,128)(2,1)} all-reduce(f32[4,1536,768]{2,1,0:T(8,128)} %convolution_bitcast_fusion), channel_id=1, replica_groups=mesh['wide'=8,'narrow'=4] {'narrow'}, use_global_device_ids=true, to_apply=%region_26.27 | all-reduce | flops 4718592 | bytes 28311552 | tf_op jit(solution)/shard_map/psum | solution.py:208
  1129.5 13.5 copy.60
  1232.6 74.2 %all-reduce.18.cloned.1.call-done = f32[4,448,768]{2,1,0:T(8,128)} async-done(((f32[4,448,768]{2,1,0:T(8,128)}), f32[4,448,768]{2,1,0:T(8,128)}) %all-reduce.18.cloned.1.call-update) | async-done | bytes 5505040 | tf_op jit(solution)/shard_map/psum | solution.py:195
  1315.8 45.6 %all-to-all-done.1 = bf16[4,1536,768]{2,0,1:T(4,128)(2,1)} async-done(((bf16[4,1536,768]{2,0,1:T(4,128)(2,1)}), bf16[4,1536,768]{2,0,1:T(4,128)(2,1)}, u32[]{:S(2)}, u32[]{:S(2)}) %all-to-all-start.1) | async-done | bytes 9437216 | tf_op jit(solution)/shard_map/all_to_all | solution.py:209
  1422.1 37.9 %reduce-scatter.31.cloned.1.call-done = f32[96,384]{1,0:T(8,128)} async-done(((f32[768,384]{1,0:T(8,128)}), f32[96,384]{1,0:T(8,128)}) %reduce-scatter.31.cloned.1.call-update) | async-done | bytes 147472
  1461.8 63.3 %reduce-scatter.29.cloned.1.call-done = f32[96,192]{1,0:T(8,128)} async-done(((f32[768,192]{1,0:T(8,128)}), f32[96,192]{1,0:T(8,128)}) %reduce-scatter.29.cloned.1.call-update) | async-done | bytes 73744
  1533.8 60.3 %reduce-scatter.27.cloned.1.call-done = f32[96,576]{1,0:T(8,128)} async-done(((f32[768,576]{1,0:T(8,128)}), f32[96,576]{1,0:T(8,128)}) %reduce-scatter.27.cloned.1.call-update) | async-done | bytes 221200
  1596.0 15.2 add_convert_fusion
  1611.2 46.9 %reduce-scatter.25.cloned.1.call-done = f32[96,4]{1,0:T(8,128)} async-done(((f32[768,4]{1,0:T(8,128)}), f32[96,4]{1,0:T(8,128)}) %reduce-scatter.25.cloned.1.call-update) | async-done | bytes 1552
  1659.5 64.2 %reduce-scatter.19.cloned.1.call-done = f32[96,192]{1,0:T(8,128)} async-done(((f32[768,192]{1,0:T(8,128)}), f32[96,192]{1,0:T(8,128)}) %reduce-scatter.19.cloned.1.call-update) | async-done | bytes 73744 | tf_op jit(solution)/shard_map/reduce_scatter | solution.py:223
  1723.7 72.1 %reduce-scatter.23.cloned.1.call-done = f32[768,96]{0,1:T(8,128)} async-done(((f32[768,768]{0,1:T(8,128)}), f32[768,96]{0,1:T(8,128)}) %reduce-scatter.23.cloned.1.call-update) | async-done | bytes 294928 | tf_op jit(solution)/shard_map/reduce_scatter | solution.py:227
  1795.8 71.9 %reduce-scatter.21.cloned.1.call-done = f32[96,768]{1,0:T(8,128)} async-done(((f32[768,768]{1,0:T(8,128)}), f32[96,768]{1,0:T(8,128)}) %reduce-scatter.21.cloned.1.call-update) | async-done | bytes 294928 | tf_op jit(solution)/shard_map/reduce_scatter | solution.py:226
  (335 shorter events, 340.0 us)
Async XLA Ops:
  7.2 413.6 %copy-start = (bf16[768,768]{1,0:T(8,128)(2,1)S(1)}, bf16[768,768]{1,0:T(8,128)(2,1)}, u32[]{:S(2)}) copy-start(bf16[768,768]{1,0:T(8,128)(2,1)} %param.22) | copy-start | bytes 3538948
  8.2 160.1 %copy-start.67 = (f32[768]{0:T(1024)}, f32[768]{0:T(1024)S(1)}, u32[]{:S(2)}) copy-start(f32[768]{0:T(1024)S(1)} %get-tuple-element.44) | copy-start | bytes 9220
  23.9 213.0 %all-to-all-start = ((bf16[32,192,768]{2,1,0:T(8,128)(2,1)}), bf16[32,192,768]{2,1,0:T(8,128)(2,1)}, u32[]{:S(2)}, u32[]{:S(2)}) async-start(bf16[32,192,768]{2,1,0:T(8,128)(2,1)} %fusion.7), calls=%async_computation | async-start | bytes 18874368 | tf_op jit(solution)/shard_map/all_to_all | solution.py:125
  31.3 132.1 %all-reduce.8.cloned.1.call-start = ((), (), s32[]{:S(2)}) async-start(), calls=%async_computation.10 | async-start | bytes 11010048 | tf_op jit(solution)/shard_map/psum | solution.py:139
  32.0 272.4 %copy-start.63 = (f32[4,448]{1,0:T(4,128)}, f32[4,448]{1,0:T(4,128)S(1)}, u32[]{:S(2)}) copy-start(f32[4,448]{1,0:T(4,128)S(1)} %get-tuple-element.61) | copy-start | bytes 21508
  55.1 355.3 %all-reduce.10.cloned.1.call-start = ((), (), s32[]{:S(2)}) async-start(), calls=%async_computation.11 | async-start | bytes 11010048 | tf_op jit(solution)/shard_map/psum | solution.py:149
  304.3 243.8 %all-reduce.14.cloned.1.call-start = ((), (), s32[]{:S(2)}) async-start(), calls=%async_computation.13 | async-start | bytes 11010048 | tf_op jit(solution)/shard_map/psum | solution.py:162
  441.0 172.2 %all-reduce.12.cloned.1.call-start = ((), (), s32[]{:S(2)}) async-start(), calls=%async_computation.12 | async-start | bytes 5505024 | tf_op jit(solution)/shard_map/psum | solution.py:156
  450.0 103.9 %copy-start.78 = (f32[4,448]{1,0:T(4,128)S(1)}, f32[4,448]{1,0:T(4,128)}, u32[]{:S(2)}) copy-start(f32[4,448]{1,0:T(4,128)} %copy-done.77) | copy-start | bytes 21508
  450.0 163.3 %copy-start.66 = (f32[4,448]{1,0:T(4,128)S(1)}, f32[4,448]{1,0:T(4,128)}, u32[]{:S(2)}) copy-start(f32[4,448]{1,0:T(4,128)} %copy-done.65) | copy-start | bytes 21508
  450.0 699.0 %all-reduce.16.cloned.1.call-start = ((), (), s32[]{:S(2)}) async-start(), calls=%async_computation.14 | async-start | bytes 11010048 | tf_op jit(solution)/shard_map/psum | solution.py:177
  553.9 66.6 %copy-start.64 = (f32[4,448]{1,0:T(4,128)S(1)}, f32[4,448]{1,0:T(4,128)}, u32[]{:S(2)}) copy-start(f32[4,448]{1,0:T(4,128)} %copy-done.63) | copy-start | bytes 21508
  1143.0 218.4 %all-to-all-start.1 = ((bf16[4,1536,768]{2,0,1:T(4,128)(2,1)}), bf16[4,1536,768]{2,0,1:T(4,128)(2,1)}, u32[]{:S(2)}, u32[]{:S(2)}) async-start(bf16[4,1536,768]{2,0,1:T(4,128)(2,1)} %copy.60), calls=%async_computation.1 | async-start | bytes 18874368 | tf_op jit(solution)/shard_map/all_to_all | solution.py:209
  1148.9 157.8 %all-reduce.18.cloned.1.call-start = ((), (), s32[]{:S(2)}) async-start(), calls=%async_computation.15 | async-start | bytes 11010048 | tf_op jit(solution)/shard_map/psum | solution.py:195
  1198.4 222.0 %reduce-scatter.33.cloned.1.call-start = ((), (), s32[]{:S(2)}) async-start(), calls=%async_computation.23 | async-start | bytes 884736
  1203.5 256.5 %reduce-scatter.31.cloned.1.call-start = ((), (), s32[]{:S(2)}) async-start(), calls=%async_computation.22 | async-start | bytes 1327104
  1216.2 308.9 %reduce-scatter.29.cloned.1.call-start = ((), (), s32[]{:S(2)}) async-start(), calls=%async_computation.21 | async-start | bytes 884736
  1220.3 373.9 %reduce-scatter.27.cloned.1.call-start = ((), (), s32[]{:S(2)}) async-start(), calls=%async_computation.20 | async-start | bytes 2211840
  1232.3 79.2 %copy-start.74 = (f32[4,448]{1,0:T(4,128)S(1)}, f32[4,448]{1,0:T(4,128)}, u32[]{:S(2)}) copy-start(f32[4,448]{1,0:T(4,128)} %copy-done.73) | copy-start | bytes 21508
  1232.3 425.7 %reduce-scatter.25.cloned.1.call-start = ((), (), s32[]{:S(2)}) async-start(), calls=%async_computation.19 | async-start | bytes 442368
  1403.3 320.4 %reduce-scatter.19.cloned.1.call-start = ((), (), s32[]{:S(2)}) async-start(), calls=%async_computation.16 | async-start | bytes 884736 | tf_op jit(solution)/shard_map/reduce_scatter | solution.py:223
  1407.1 388.7 %reduce-scatter.23.cloned.1.call-start = ((), (), s32[]{:S(2)}) async-start(), calls=%async_computation.18 | async-start | bytes 2654208 | tf_op jit(solution)/shard_map/reduce_scatter | solution.py:227
  1413.6 454.2 %reduce-scatter.21.cloned.1.call-start = ((), (), s32[]{:S(2)}) async-start(), calls=%async_computation.17 | async-start | bytes 2654208 | tf_op jit(solution)/shard_map/reduce_scatter | solution.py:226
  1596.0 271.7 %copy-start.1 = (bf16[768,768]{1,0:T(8,128)(2,1)S(1)}, bf16[768,768]{1,0:T(8,128)(2,1)}, u32[]{:S(2)}) copy-start(bf16[768,768]{1,0:T(8,128)(2,1)} %param.22) | copy-start | bytes 3538948
  (90 other events, 567.1 us)
Sparse Core Ops, SparseCore 0:
  55.2 108.1 all-reduce.7
  304.5 105.8 all-reduce.9
  441.2 106.9 all-reduce.13
  551.0 62.2 all-reduce.11
  722.1 182.5 all-reduce.15
  1198.5 108.1 all-reduce.17
  1310.0 82.9 reduce-scatter.32
  1396.8 63.1 reduce-scatter.30
  1463.6 61.3 reduce-scatter.28
  1528.4 65.6 reduce-scatter.26
  1597.7 60.3 reduce-scatter.24
  1662.2 61.4 reduce-scatter.18
  1727.8 67.9 reduce-scatter.22
  1799.7 67.9 reduce-scatter.20
where the time goes:
time: 1880 us; the launch traced here: 1870 us
  waiting for transfers between devices  967 us (51%)
  blocking collectives  396 us (21%)
  matrix products  219 us (12%)
  other arithmetic  185 us (10%)
  local copies, waits for them, and re-layouts  76.9 us (4%)
    psum x1, blocking collectives, on_device(): clip_grad = lax.psum(clip_terms, 'narrow')  396 us
    unnamed x19, waiting for transfers between devices  209 us
    psum x1, waiting for transfers between devices, on_device(): after_self = token_input + lax.psum(self_part, 'narrow')  108 us
    psum x1, waiting for transfers between devices, on_device(): after_cross = after_self + lax.psum(cross_part, 'narrow')  102 us
    psum x1, waiting for transfers between devices, on_device(): lax.psum(right_dot(grad_pre, fc_in).reshape(clip_count, seq_len, model_wi...  97.7 us
    psum x1, waiting for transfers between devices, on_device(): lax.psum(jnp.einsum('kcse,kde->csd', grad_triple, self_qkv, preferred_ele...  74.2 us
    reduce_scatter x1, waiting for transfers between devices, on_device(): lax.psum_scatter(grad_fc_out, 'wide', scatter_dimension=1, tiled=True)  72.1 us
    reduce_scatter x1, waiting for transfers between devices, on_device(): lax.psum_scatter(grad_fc_in, 'wide', scatter_dimension=0, tiled=True)  71.9 us
  transfers between devices with their start and end apart: 16, of which 14 were waited for; matrix products, arithmetic and copies ran while one was open for 13% of the time, Pallas kernels for 0%

commit v1 on v0

v1 whole, which is shorter than its diff:
```python
import jax
import jax.numpy as jnp
from jax import lax
from jax.sharding import PartitionSpec as P

HEAD_DIM = 64
AUDIO = 1500
EPSILON = 1e-05
NEG_FILL = -1e30
INV_ROOT = HEAD_DIM**-0.5
F32 = jnp.float32
BF16 = jnp.bfloat16


def dot(left, right, left_dim=1, right_dim=0):
    return lax.dot_general(
        left, right, (((left_dim,), (right_dim,)), ((), ())), preferred_element_type=F32
    )


def norm_stats(values):
    center = values - jnp.mean(values, axis=-1, keepdims=True)
    spread = jnp.mean(center * center, axis=-1, keepdims=True)
    inverse = lax.rsqrt(spread + EPSILON)
    return center * inverse, inverse


def norm_back(unit, inverse, gain_row, grad):
    scaled = grad * gain_row
    first = jnp.mean(scaled, axis=-1, keepdims=True)
    second = jnp.mean(scaled * unit, axis=-1, keepdims=True)
    back = (scaled - first - unit * second) * inverse
    axes = tuple(range(grad.ndim - 1))
    return back, jnp.sum(grad * unit, axis=axes)


def swap(values, axis, bit):
    size = lax.axis_size(axis)
    return lax.ppermute(values, axis, [(i, i ^ bit) for i in range(size)])


def gather_narrow(own):
    core = swap(own, "narrow", 1)
    other = swap(own, "narrow", 2)
    diagonal = swap(other, "narrow", 1)
    return [own, core, other, diagonal]


def scatter_narrow(zero, one, two, three):
    near = swap(jnp.stack((one, three)), "narrow", 1)
    far = swap((two.astype(F32) + near[1].astype(F32)).astype(BF16), "narrow", 2)
    return zero.astype(F32) + near[0].astype(F32) + far.astype(F32)


def scatter_wide(pack):
    size = lax.axis_size("wide")
    index = lax.axis_index("wide")
    bit = 1
    shape = pack.shape[1:]
    pack = pack.astype(F32)
    while bit < size:
        halves = pack.reshape((pack.shape[0] // 2, 2) + shape)
        mine = (index // bit) % 2
        keep = lax.dynamic_index_in_dim(halves, mine, 1, keepdims=False)
        give = lax.dynamic_index_in_dim(halves, 1 - mine, 1, keepdims=False)
        pack = keep + swap(give.astype(BF16), "wide", bit).astype(F32)
        bit *= 2
    return pack[0]


def split_heads(values):
    return values.reshape(values.shape[:-1] + (values.shape[-1] // HEAD_DIM, HEAD_DIM))


def attend(queries, key_rows, value_rows, allowed):
    scores = jnp.einsum(
        "cshd,cthd->chst",
        split_heads(queries),
        split_heads(key_rows),
        preferred_element_type=F32,
    ) * INV_ROOT
    masked = jnp.where(allowed, scores, NEG_FILL)
    log_total = jax.nn.logsumexp(masked, axis=-1, keepdims=True)
    probs = jnp.exp(masked - log_total).astype(BF16)
    mixture = jnp.einsum(
        "chst,cthd->cshd", probs, split_heads(value_rows), preferred_element_type=F32
    )
    return mixture.reshape(queries.shape).astype(BF16), log_total


def attend_back(queries, key_rows, value_rows, allowed, log_total, grad_mixture):
    query_heads = split_heads(queries)
    key_heads = split_heads(key_rows)
    value_heads = split_heads(value_rows)
    grad_heads = split_heads(grad_mixture)
    scores = jnp.einsum("cshd,cthd->chst", query_heads, key_heads, preferred_element_type=F32) * INV_ROOT
    masked = jnp.where(allowed, scores, NEG_FILL)
    probs = jnp.exp(masked - log_total)
    grad_probs = jnp.einsum("cshd,cthd->chst", grad_heads, value_heads, preferred_element_type=F32)
    inner = jnp.sum(probs * grad_probs, axis=-1, keepdims=True)
    grad_scores = (probs * (grad_probs - inner)).astype(BF16)
    grad_query = jnp.einsum("chst,cthd->cshd", grad_scores, key_heads, preferred_element_type=F32) * INV_ROOT
    grad_key = jnp.einsum("chst,cshd->cthd", grad_scores, query_heads, preferred_element_type=F32) * INV_ROOT
    grad_value = jnp.einsum("chst,cshd->cthd", probs.astype(BF16), grad_heads, preferred_element_type=F32)
    return (
        grad_query.reshape(queries.shape).astype(BF16),
        grad_key.reshape(key_rows.shape).astype(BF16),
        grad_value.reshape(value_rows.shape).astype(BF16),
    )


def on_device(
    tokens, lengths, memory, gains, self_qkv, self_out, cross_q, cross_kv, cross_out, fc_in, fc_out, out_grad
):
    clips, seq, width = tokens.shape
    wide = lax.axis_size("wide")
    narrow = lax.axis_size("narrow")
    me = lax.axis_index("narrow")
    share = memory.shape[1]
    frames = share * wide
    heads_width = self_qkv.shape[2]
    take = lambda array, r: lax.dynamic_index_in_dim(array, me ^ r, 0, keepdims=False)
    by_distance = lambda array: jnp.stack([take(array, r) for r in range(narrow)])

    memory_own = lax.dynamic_index_in_dim(
        memory.reshape(wide, narrow, share, width), me, 1, keepdims=False
    ).astype(F32)
    memory_unit, memory_inverse = norm_stats(memory_own)
    encoded_own = (memory_unit * gains[0]).astype(BF16)
    encoded = lax.all_to_all(encoded_own, "wide", 0, 0, tiled=True).reshape(frames, width)

    self_out_all = jnp.concatenate(gather_narrow(self_out), axis=0)
    cross_q_all = jnp.concatenate(gather_narrow(cross_q), axis=1)
    cross_kv_all = jnp.concatenate(gather_narrow(cross_kv), axis=2)
    cross_out_all = jnp.concatenate(gather_narrow(cross_out), axis=0)

    clip_lengths = by_distance(lengths)
    positions = jnp.arange(seq)
    live_rows = positions[None, :] < clip_lengths[:, None]
    self_allowed = (positions[None, :] <= positions[:, None])[None, None] & live_rows[:, None, None, :]
    tokens_by = by_distance(tokens).astype(F32)
    unit_one, inverse_one = norm_stats(tokens_by)
    normed_one = (unit_one * gains[1]).astype(BF16)
    rows_one = normed_one.reshape(clips * seq, width)
    projected = [
        dot(rows_one, self_qkv[i]).astype(BF16).reshape(clips, seq, heads_width) for i in range(3)
    ]
    mixed_heads, self_total = attend(projected[0], projected[1], projected[2], self_allowed)
    near = swap(jnp.stack((mixed_heads[1], mixed_heads[3])), "narrow", 1)
    own_half = jnp.concatenate((mixed_heads[0], near[0]), axis=1)
    far_half = swap(jnp.concatenate((mixed_heads[2], near[1]), axis=1), "narrow", 2)
    self_mixed = jnp.concatenate((own_half, far_half), axis=1)

    after_self = tokens_by[0] + dot(self_mixed, self_out_all)
    unit_two, inverse_two = norm_stats(after_self)
    normed_two = (unit_two * gains[2]).astype(BF16)
    cross_query = dot(normed_two, cross_q_all).astype(BF16)
    keys = dot(encoded, cross_kv_all[0]).astype(BF16)
    values = dot(encoded, cross_kv_all[1]).astype(BF16)
    cross_allowed = (jnp.arange(frames) < AUDIO)[None, None, None, :]
    cross_mixed, cross_total = attend(cross_query[None], keys[None], values[None], cross_allowed)
    cross_mixed = cross_mixed[0]
    after_cross = after_self + dot(cross_mixed, cross_out_all)
    unit_three, inverse_three = norm_stats(after_cross)
    normed_three = (unit_three * gains[3]).astype(BF16)

    rows_three = jnp.concatenate(gather_narrow(normed_three), axis=0)
    hidden_pre = dot(rows_three, fc_in)
    activated, gelu_back = jax.vjp(lambda v: jax.nn.gelu(v, approximate=False), hidden_pre)
    hidden = activated.astype(BF16)
    feed_part = dot(hidden, fc_out).astype(BF16).reshape(clips, seq, width)
    grad_by = by_distance(out_grad).astype(F32) * live_rows[:, :, None].astype(F32)
    grad_three = grad_by.astype(BF16).reshape(clips * seq, width)
    grad_fc_out = dot(grad_three, hidden, 0, 0)
    grad_pre = gelu_back(dot(grad_three, fc_out, 1, 1))[0].astype(BF16)
    grad_fc_in = dot(rows_three, grad_pre, 0, 0)
    part = dot(grad_pre, fc_in, 1, 1).astype(BF16).reshape(clips, seq, width)
    grad_normed = scatter_narrow(part[0], part[1], part[2], part[3])
    feed = scatter_narrow(feed_part[0], feed_part[1], feed_part[2], feed_part[3])
    block_own = (after_cross + feed).astype(BF16)
    block_out = by_distance(jnp.stack(gather_narrow(block_own)))

    back, gain_three = norm_back(unit_three, inverse_three, gains[3], grad_normed)
    grad_cross = grad_by[0] + back
    grad_two = grad_cross.astype(BF16)
    grad_cross_out = dot(cross_mixed, grad_two, 0, 0)
    grad_mixed = dot(grad_two, cross_out_all, 1, 1).astype(BF16)
    grad_query, grad_keys, grad_values = attend_back(
        cross_query[None], keys[None], values[None], cross_allowed, cross_total, grad_mixed[None]
    )
    grad_query, grad_keys, grad_values = grad_query[0], grad_keys[0], grad_values[0]

    grad_encoded = (
        dot(grad_keys, cross_kv_all[0], 1, 1) + dot(grad_values, cross_kv_all[1], 1, 1)
    ).astype(BF16)
    grad_encoded = lax.all_to_all(
        grad_encoded.reshape(wide, share, width), "wide", 0, 0, tiled=True
    ).astype(F32)
    memory_back, gain_zero = norm_back(memory_unit, memory_inverse, gains[0], grad_encoded)
    memory_back = jnp.stack(gather_narrow(memory_back.astype(BF16)))
    memory_grad = by_distance(memory_back).transpose(1, 0, 2, 3).reshape(memory.shape)

    grad_cross_q = dot(normed_two, grad_query, 0, 0)
    grad_cross_k = dot(encoded, grad_keys, 0, 0)
    grad_cross_v = dot(encoded, grad_values, 0, 0)
    back, gain_two = norm_back(unit_two, inverse_two, gains[2], dot(grad_query, cross_q_all, 1, 1))
    grad_self = grad_cross + back
    grad_one = grad_self.astype(BF16)
    grad_self_out = dot(self_mixed, grad_one, 0, 0)
    grad_mixed = dot(grad_one, self_out_all, 1, 1).astype(BF16)
    half = width // 2
    far_half = swap(grad_mixed[:, half:], "narrow", 2)
    near = swap(
        jnp.stack((grad_mixed[:, heads_width:half], far_half[:, heads_width:])), "narrow", 1
    )
    grad_heads = jnp.stack((grad_mixed[:, :heads_width], near[0], far_half[:, :heads_width], near[1]))
    grad_triple = attend_back(
        projected[0], projected[1], projected[2], self_allowed, self_total, grad_heads
    )
    grad_triple = [item.reshape(clips * seq, heads_width) for item in grad_triple]
    grad_qkv = [dot(rows_one, item, 0, 0) for item in grad_triple]
    part = sum(dot(grad_triple[i], self_qkv[i], 1, 1) for i in range(3))
    part = part.astype(BF16).reshape(clips, seq, width)
    grad_normed = scatter_narrow(part[0], part[1], part[2], part[3])
    back, gain_one = norm_back(unit_one[0], inverse_one[0], gains[1], grad_normed)
    tokens_own = (grad_self + back).astype(BF16)
    tokens_grad = by_distance(jnp.stack(gather_narrow(tokens_own)))

    blocks = []
    for r in range(narrow):
        columns = slice(r * heads_width, (r + 1) * heads_width)
        blocks.append(
            jnp.stack(
                (
                    grad_self_out[columns].T,
                    grad_cross_q[:, columns],
                    grad_cross_k[:, columns],
                    grad_cross_v[:, columns],
                    grad_cross_out[columns].T,
                )
            ).astype(BF16)
        )
    shared = scatter_narrow(*blocks)
    gain_terms = jnp.stack((gain_zero, gain_one, gain_two, gain_three))
    gain_terms = gain_terms + swap(gain_terms, "narrow", 1)
    gain_terms = gain_terms + swap(gain_terms, "narrow", 2)
    depth = width // wide

    def cut(matrix):
        return matrix.reshape(wide, -1)

    pieces = [cut(gain_terms.T)]
    pieces += [cut(shared[i]) for i in range(5)]
    pieces += [cut(item) for item in grad_qkv]
    pieces += [cut(grad_fc_in), cut(grad_fc_out)]
    sizes = [piece.shape[1] for piece in pieces]
    total = scatter_wide(jnp.concatenate([p.astype(BF16) for p in pieces], axis=1))
    outs = []
    start = 0
    for size in sizes:
        outs.append(total[start : start + size].reshape(depth, -1))
        start += size
    return (
        block_out,
        tokens_grad,
        memory_grad,
        outs[0].T,
        jnp.stack(outs[6:9]),
        outs[1].T,
        outs[2],
        jnp.stack(outs[3:5]),
        outs[5].T,
        outs[9],
        outs[10].T,
    )


def solution(mesh):
    placed = (
        P("wide", None, None),
        P("wide"),
        P(None, "wide", None),
        P(),
        P(None, None, "narrow"),
        P("narrow", None),
        P(None, "narrow"),
        P(None, None, "narrow"),
        P("narrow", None),
        P(None, "narrow"),
        P("narrow", None),
        P("wide", None, None),
    )
    return jax.shard_map(
        on_device,
        mesh=mesh,
        in_specs=placed,
        out_specs=(
            P("wide", None, None),
            P("wide", None, None),
            P(None, "wide", None),
            P(None, "wide"),
            P(None, "wide", "narrow"),
            P("narrow", "wide"),
            P("wide", "narrow"),
            P(None, "wide", "narrow"),
            P("narrow", "wide"),
            P("wide", "narrow"),
            P("narrow", "wide"),
        ),
        check_vma=False,
    )
```

time: 1880 us -> 751 us (0.40)
  waiting for transfers between devices: 967 us -> 192 us
  blocking collectives: 396 us -> 0 us
  local copies, waits for them, and re-layouts: 76.9 us -> 142 us
  other arithmetic: 185 us -> 153 us
  starting transfers between devices: 15.3 us -> 35.2 us
    psum x6 -> x0, waiting for transfers between devices: 442 us -> none  [the longest x1 108 us: on_device(): after_self = token_input + lax.psum(self_part, 'narrow')]
    psum x1 -> x0, blocking collectives: 396 us -> none  [on_device(): clip_grad = lax.psum(clip_terms, 'narrow')]
    unnamed x19 -> x0, waiting for transfers between devices: 209 us -> none
    reduce_scatter x3 -> x0, waiting for transfers between devices: 208 us -> none  [the longest x1 72.1 us: on_device(): lax.psum_scatter(grad_fc_out, 'wide', scatter_dimension=1, tiled=True)]
    ppermute x0 -> x41, waiting for transfers between devices: none -> 192 us  [swap(): return lax.ppermute(values, axis, [(i, i ^ bit) for i in range(size)])]
    all_to_all x2, waiting for transfers between devices: 108 us -> 0.01 us  [the longest x1 0.01 us: on_device(): lax.all_to_all(grad_encoded.reshape(wide, share, width), 'wide', 0, 0, ti...]
    reduce_sum x16 -> x9, other arithmetic: 71.8 us -> 18.2 us  [the longest x3 9.51 us: norm_back(): return (back, jnp.sum(grad * unit, axis=axes))]
    convert_element_type x13 -> x17, other arithmetic: 94 us -> 63.6 us  [the longest x2 34.2 us: attend_back(): grad_scores = (probs * (grad_probs - inner)).astype(BF16)]
  transfers between devices with their start and end apart: 16 -> 43, of which waited for: 14 -> 14; matrix products, arithmetic and copies ran while one was open for 13% -> 37% of each run, Pallas kernels for 0% -> 0%
where the time goes in v1:
time: 751 us; the launch traced here: 741 us
  matrix products  216 us (29%)
  waiting for transfers between devices  192 us (26%)
  other arithmetic  153 us (20%)
  local copies, waits for them, and re-layouts  142 us (19%)
  starting transfers between devices  35.2 us (5%)
    ppermute x41, waiting for transfers between devices, swap(): return lax.ppermute(values, axis, [(i, i ^ bit) for i in range(size)])  192 us
    dot_general x30, matrix products, dot(): lax.dot_general(left, right, (((left_dim,), (right_dim,)), ((), ())), pre...  95.8 us
    unnamed x248, local copies, waits for them, and re-layouts  52.6 us
    dot_general x2, matrix products, attend_back(): jnp.einsum('cshd,cthd->chst', grad_heads, value_heads, preferred_element_...  36.7 us
    convert_element_type x2, other arithmetic, attend_back(): grad_scores = (probs * (grad_probs - inner)).astype(BF16)  34.2 us
    ppermute x41, starting transfers between devices, swap(): return lax.ppermute(values, axis, [(i, i ^ bit) for i in range(size)])  22.5 us
    dot_general x2, matrix products, attend(): jnp.einsum('chst,cthd->cshd', probs, split_heads(value_rows), preferred_e...  22.2 us
    dot_general x2, matrix products, attend_back(): jnp.einsum('chst,cshd->cthd', probs.astype(BF16), grad_heads, preferred_e...  21.7 us
  transfers between devices with their start and end apart: 43, of which 14 were waited for; matrix products, arithmetic and copies ran while one was open for 37% of the time, Pallas kernels for 0%

profile of v1, /device:TPU:0, one launch (start us, length us, event | category | flops | bytes accessed | tf_op | source)
XLA Modules:
  0.0 740.9 jit_solution(17339985313395118526)
XLA Ops:
  59.7 7.5 %fusion.40 = bf16[4,448,3,64]{1,3,2,0:T(8,128)(2,1)S(1)} fusion(bf16[4,448,3,64]{1,0,3,2:T(4,128)(2,1)} %reshape_reshape.12, f32[4,3,448,448]{2,3,1,0:T(8,128)} %copy-done.2, f32[4,3,448]{2,1,0:T(4,128)S(1)} %log_add_fusion.1, pred[4,448,448]{1,2,0:T(8,128)(4,1)} %copy-done.9), kind=kOutput, calls=%fused_computation.142 | convolution fusion | flops 318259200 | bytes 11834368 | tf_op jit(solution)/shard_map/chst,cthd->cshd/dot_general | solution.py:85
  86.8 7.8 %collective-permute-done.1 = bf16[448,384]{0,1:T(8,128)(2,1)S(1)} collective-permute-done((bf16[448,384]{0,1:T(8,128)(2,1)S(1)}, bf16[448,384]{0,1:T(8,128)(2,1)S(1)}, u32[]{:S(2)}, u32[]{:S(2)}) %collective-permute-start.1) | collective-permute-done | bytes 344096 | tf_op jit(solution)/shard_map/ppermute | solution.py:39
  108.7 13.2 %fusion = (f32[12,448]{1,0:T(8,128)S(1)}, f32[12,448,1536]{2,1,0:T(8,128)}) fusion(pred[1536]{0:T(1024)(128)(4,1)S(1)} %iota_compare_fusion.1, bf16[448,12,64]{0,2,1:T(8,128)(2,1)S(1)} %bitcast.419, bf16[1536,12,64]{0,2,1:T(8,128)(2,1)S(1)} %bitcast.412), kind=kOutput, calls=%fused_computation.5 | convolution fusion | flops 1081731840 | bytes 36100608 | tf_op jit(solution)/shard_map/cshd,cthd->chst/dot_general | solution.py:76
  121.9 14.8 %exponential_reduce_fusion = f32[12,448]{1,0:T(8,128)S(1)} fusion(f32[12,448,1536]{2,1,0:T(8,128)} %get-tuple-element.128, f32[12,448]{1,0:T(8,128)S(1)} %is-finite_select_fusion, pred[1536]{0:T(1024)(128)(4,1)S(1)} %iota_compare_fusion.1), kind=kLoop, calls=%fused_computation.3 | loop fusion | flops 33024768 | bytes 33074688 | tf_op jit(solution)/shard_map/reduce_sum | solution.py:83
  137.4 14.7 %convolution_convert_fusion.17 = bf16[12,64,448]{2,1,0:T(8,128)(2,1)} fusion(bf16[1536,12,64]{0,2,1:T(8,128)(2,1)S(1)} %bitcast.422, f32[12,448,1536]{2,1,0:T(8,128)} %get-tuple-element.128, f32[12,448]{1,0:T(8,128)} %log_add_fusion, pred[1536]{0:T(1024)(128)(4,1)S(1)} %iota_compare_fusion.1), kind=kOutput, calls=%fused_computation.104 | convolution fusion | flops 1090338816 | bytes 36100608 | tf_op jit(solution)/shard_map/chst,cthd->cshd/dot_general | solution.py:85
  156.8 15.2 %collective-permute-done.15 = bf16[448,768]{1,0:T(8,128)(2,1)} collective-permute-done((bf16[448,768]{1,0:T(8,128)(2,1)S(1)}, bf16[448,768]{1,0:T(8,128)(2,1)}, u32[]{:S(2)}, u32[]{:S(2)}) %collective-permute-start.15) | collective-permute-done | bytes 688160 | tf_op jit(solution)/shard_map/ppermute | solution.py:39
  183.0 14.3 %add_convert_fusion.1 = (bf16[1792,768]{1,0:T(8,128)(2,1)S(1)}, f32[1792,768]{1,0:T(8,128)S(1)}) fusion(f32[1792,768]{1,0:T(8,128)S(1)} %fusion.54, bf16[1792,768]{1,0:T(8,128)(2,1)S(1)} %fusion.8, bf16[768,768]{1,0:T(8,128)(2,1)S(1)} %copy-done), kind=kOutput, calls=%fused_computation.28 | convolution fusion | flops 2213019648 | bytes 17694720 | tf_op jit(solution)/shard_map/dot_general | solution.py:16
  218.7 9.1 %collective-permute-done.23 = bf16[448,768]{1,0:T(8,128)(2,1)S(1)} collective-permute-done((bf16[448,768]{1,0:T(8,128)(2,1)S(1)}, bf16[448,768]{1,0:T(8,128)(2,1)S(1)}, u32[]{:S(2)}, u32[]{:S(2)}) %collective-permute-start.23) | collective-permute-done | bytes 688160 | tf_op jit(solution)/shard_map/ppermute | solution.py:39
  230.2 11.9 %collective-permute-done.18 = bf16[448,768]{1,0:T(8,128)(2,1)S(1)} collective-permute-done((bf16[448,768]{1,0:T(8,128)(2,1)S(1)}, bf16[448,768]{1,0:T(8,128)(2,1)S(1)}, u32[]{:S(2)}, u32[]{:S(2)}) %collective-permute-start.18) | collective-permute-done | bytes 688160 | tf_op jit(solution)/shard_map/ppermute | solution.py:39
  250.7 26.4 %multiply_reduce_fusion = (f32[12,448]{1,0:T(8,128)S(1)}, f32[12,448,1536]{2,1,0:T(8,128)}) fusion(f32[12,448,1536]{2,1,0:T(8,128)} %get-tuple-element.128, f32[12,448]{1,0:T(8,128)S(1)} %copy-done.57, pred[1536]{0:T(1024)(128)(4,1)S(1)} %iota_compare_fusion.1, bf16[448,12,64]{0,2,1:T(8,128)(2,1)S(1)} %bitcast.424, bf16[1536,12,64]{0,2,1:T(8,128)(2,1)S(1)} %bitcast.423), kind=kOutput, calls=%fused_computation.1 | convolution fusion | flops 1098246912 | bytes 69152256 | tf_op jit(solution)/shard_map/cshd,cthd->chst/dot_general | solution.py:99
  277.1 27.7 %multiply_convert_fusion = bf16[12,448,1536]{2,1,0:T(8,128)(2,1)} fusion(f32[12,448,1536]{2,1,0:T(8,128)} %get-tuple-element.132, f32[12,448,1536]{2,1,0:T(8,128)} %get-tuple-element.128, f32[12,448]{1,0:T(8,128)S(1)} %get-tuple-element.131, f32[12,448]{1,0:T(8,128)S(1)} %copy-done.57, pred[1536]{0:T(1024)(128)(4,1)S(1)} %iota_compare_fusion.1), kind=kLoop, calls=%fused_computation | loop fusion | flops 49545216 | bytes 82619904 | tf_op jit(solution)/shard_map/convert_element_type | solution.py:101
  304.8 10.4 %multiply_convert_fusion.7 = bf16[12,64,448]{2,1,0:T(8,128)(2,1)S(1)} fusion(bf16[1536,12,64]{0,2,1:T(8,128)(2,1)S(1)} %bitcast.413, bf16[12,448,1536]{2,1,0:T(8,128)(2,1)} %multiply_convert_fusion), kind=kOutput, calls=%fused_computation.90 | convolution fusion | flops 1057652736 | bytes 19562496 | tf_op jit(solution)/shard_map/chst,cthd->cshd/dot_general | solution.py:102
  322.3 8.7 %multiply_convert_fusion.4 = bf16[12,64,1536]{2,1,0:T(8,128)(2,1)S(1)} fusion(bf16[448,12,64]{0,2,1:T(8,128)(2,1)S(1)} %bitcast.420, bf16[12,448,1536]{2,1,0:T(8,128)(2,1)} %multiply_convert_fusion), kind=kOutput, calls=%fused_computation.61 | convolution fusion | flops 1059323904 | bytes 19562496 | tf_op jit(solution)/shard_map/chst,cshd->cthd/dot_general | solution.py:103
  331.0 15.6 %convolution_convert_fusion.4 = bf16[12,64,1536]{2,1,0:T(8,128)(2,1)} fusion(bf16[448,12,64]{0,2,1:T(8,128)(2,1)S(1)} %bitcast.425, f32[12,448,1536]{2,1,0:T(8,128)} %get-tuple-element.128, f32[12,448]{1,0:T(8,128)S(1)} %copy-done.57, pred[1536]{0:T(1024)(128)(4,1)S(1)} %iota_compare_fusion.1), kind=kOutput, calls=%fused_computation.67 | convolution fusion | flops 1091174400 | bytes 36100608 | tf_op jit(solution)/shard_map/chst,cshd->cthd/dot_general | solution.py:104
  365.8 6.8 collective-permute-done.24
  389.7 10.4 %multiply_reduce_fusion.1 = (f32[4,3,448]{2,1,0:T(4,128)S(1)}, f32[4,3,448,448]{2,3,1,0:T(8,128)}) fusion(f32[4,3,448,448]{2,3,1,0:T(8,128)} %copy-done.2, f32[4,3,448]{2,1,0:T(4,128)S(1)} %copy-done.61, pred[4,448,448]{1,2,0:T(8,128)(4,1)S(1)} %copy-done.10, bf16[4,448,3,64]{1,0,3,2:T(4,128)(2,1)S(1)} %copy-done.29, ...), kind=kOutput, calls=%fused_computation.8 | convolution fusion | flops 321350400 | bytes 21489664 | tf_op jit(solution)/shard_map/cshd,cthd->chst/dot_general | solution.py:99
  484.9 26.1 %collective-permute-done.35 = f32[4,768]{1,0:T(4,128)S(1)} collective-permute-done((f32[4,768]{1,0:T(4,128)S(1)}, f32[4,768]{1,0:T(4,128)S(1)}, u32[]{:S(2)}, u32[]{:S(2)}) %collective-permute-start.35) | collective-permute-done | bytes 12320 | tf_op jit(solution)/shard_map/ppermute | solution.py:39
  555.6 14.3 %collective-permute-done.29 = bf16[448,768]{1,0:T(8,128)(2,1)} collective-permute-done((bf16[448,768]{1,0:T(8,128)(2,1)S(1)}, bf16[448,768]{1,0:T(8,128)(2,1)}, u32[]{:S(2)}, u32[]{:S(2)}) %collective-permute-start.29) | collective-permute-done | bytes 688160 | tf_op jit(solution)/shard_map/ppermute | solution.py:39
  581.0 21.6 %collective-permute-done.38 = bf16[4,295296]{1,0:T(4,128)(2,1)} collective-permute-done((bf16[4,295296]{1,0:T(4,128)(2,1)}, bf16[4,295296]{1,0:T(4,128)(2,1)}, u32[]{:S(2)}, u32[]{:S(2)}) %collective-permute-start.38) | collective-permute-done | bytes 2362400 | tf_op jit(solution)/shard_map/ppermute | solution.py:39
  607.8 8.2 %reshape.873 = f32[2,2,295296]{2,1,0:T(2,128)} reshape(f32[4,295296]{1,0:T(4,128)} %bitcast_add_fusion) | data formatting | bytes 9449472 | tf_op jit(solution)/shard_map/reshape | solution.py:62
  627.3 22.4 %collective-permute-done.39 = bf16[2,295296]{1,0:T(2,128)(2,1)S(1)} collective-permute-done((bf16[2,295296]{1,0:T(2,128)(2,1)S(1)}, bf16[2,295296]{1,0:T(2,128)(2,1)S(1)}, u32[]{:S(2)}, u32[]{:S(2)}) %collective-permute-start.39) | collective-permute-done | bytes 1181216 | tf_op jit(solution)/shard_map/ppermute | solution.py:39
  660.0 44.7 %collective-permute-done.40 = bf16[1,295296]{1,0:T(2,128)(2,1)S(1)} collective-permute-done((bf16[1,295296]{1,0:T(2,128)(2,1)S(1)}, bf16[1,295296]{1,0:T(2,128)(2,1)S(1)}, u32[]{:S(2)}, u32[]{:S(2)}) %collective-permute-start.40) | collective-permute-done | bytes 590624 | tf_op jit(solution)/shard_map/ppermute | solution.py:39
  723.9 8.3 %maximum_bitcast_fusion = bf16[8,4,192,768]{3,2,0,1:T(8,128)(2,1)} fusion(bf16[1,8,192,768]{3,2,1,0:T(8,128)(2,1)} %get-tuple-element.51, bf16[1,8,192,768]{3,2,1,0:T(8,128)(2,1)} %get-tuple-element.52, bf16[1,8,192,768]{3,2,1,0:T(8,128)(2,1)} %get-tuple-element.53, bf16[1,8,192,768]{3,2,1,0:T(8,128)(2,1)S(1)} %get-tuple-element.50), kind=kLoop, calls=%fused_computation.13 | loop fusion | flops 14155776 | bytes 18874368 | tf_op jit(solution)/shard_map/transpose | solution.py:201
  732.2 8.5 %copy.64 = bf16[8,4,192,768]{3,2,1,0:T(8,128)(2,1)} copy(bf16[8,4,192,768]{3,2,0,1:T(8,128)(2,1)} %maximum_bitcast_fusion) | data formatting | bytes 18874368 | tf_op jit(solution)/shard_map/transpose | solution.py:201
  (516 shorter events, 369.6 us)
Async XLA Ops:
  0.7 70.9 %collective-permute-start.3 = (bf16[192,768]{1,0:T(8,128)(2,1)}, bf16[192,768]{1,0:T(8,128)(2,1)}, u32[]{:S(2)}, u32[]{:S(2)}) collective-permute-start(bf16[192,768]{1,0:T(8,128)(2,1)} %param.17), channel_id=1, source_target_pairs={{0,2},{1,3},{2,0},{3,1},{4,6},{5,7},{6,4},{7,5},{8,10},{9,11},{10,... | collective-permute-start | bytes 884744 | tf_op jit(solution)/shard_map/ppermute | solution.py:39
  3.7 66.8 %collective-permute-start.2 = (bf16[192,768]{1,0:T(8,128)(2,1)}, bf16[192,768]{1,0:T(8,128)(2,1)}, u32[]{:S(2)}, u32[]{:S(2)}) collective-permute-start(bf16[192,768]{1,0:T(8,128)(2,1)} %param.17), channel_id=1, source_target_pairs={{0,1},{1,0},{2,3},{3,2},{4,5},{5,4},{6,7},{7,6},{8,9},{9,8},{10,11... | collective-permute-start | bytes 884744 | tf_op jit(solution)/shard_map/ppermute | solution.py:39
  3.7 71.0 %collective-permute-start.9 = (bf16[768,192]{0,1:T(8,128)(2,1)}, bf16[768,192]{0,1:T(8,128)(2,1)}, u32[]{:S(2)}, u32[]{:S(2)}) collective-permute-start(bf16[768,192]{0,1:T(8,128)(2,1)} %param.18), channel_id=1, source_target_pairs={{0,2},{1,3},{2,0},{3,1},{4,6},{5,7},{6,4},{7,5},{8,10},{9,11},{10,... | collective-permute-start | bytes 884744 | tf_op jit(solution)/shard_map/ppermute | solution.py:39
  3.9 69.3 %collective-permute-start.8 = (bf16[768,192]{0,1:T(8,128)(2,1)}, bf16[768,192]{0,1:T(8,128)(2,1)}, u32[]{:S(2)}, u32[]{:S(2)}) collective-permute-start(bf16[768,192]{0,1:T(8,128)(2,1)} %param.18), channel_id=1, source_target_pairs={{0,1},{1,0},{2,3},{3,2},{4,5},{5,4},{6,7},{7,6},{8,9},{9,8},{10,11... | collective-permute-start | bytes 884744 | tf_op jit(solution)/shard_map/ppermute | solution.py:39
  13.5 85.1 %all-to-all-start = ((bf16[8,192,768]{2,1,0:T(8,128)(2,1)}), bf16[8,192,768]{2,1,0:T(8,128)(2,1)}, u32[]{:S(2)}, u32[]{:S(2)}) async-start(bf16[8,192,768]{2,1,0:T(8,128)(2,1)} %fusion.19), calls=%async_computation | async-start | bytes 4718592 | tf_op jit(solution)/shard_map/all_to_all | solution.py:130
  19.5 64.5 %collective-permute-start.6 = (bf16[2,768,192]{1,2,0:T(8,128)(2,1)}, bf16[2,768,192]{1,2,0:T(8,128)(2,1)}, u32[]{:S(2)}, u32[]{:S(2)}) collective-permute-start(bf16[2,768,192]{1,2,0:T(8,128)(2,1)} %param.19), channel_id=1, source_target_pairs={{0,2},{1,3},{2,0},{3,1},{4,6},{5,7},{6,4},{7,5},{8,10},{9,11},{10,... | collective-permute-start | bytes 1769480 | tf_op jit(solution)/shard_map/ppermute | solution.py:39
  155.4 16.7 %collective-permute-start.15 = (bf16[448,768]{1,0:T(8,128)(2,1)S(1)}, bf16[448,768]{1,0:T(8,128)(2,1)}, u32[]{:S(2)}, u32[]{:S(2)}) collective-permute-start(bf16[448,768]{1,0:T(8,128)(2,1)S(1)} %multiply_convert_fusion.8), channel_id=1, source_target_pairs={{0,2},{1,3},{2,0},{3,1},{4,6},{5,7},{6,4},{7,5},{8,10},{9,11},{10,... | collective-permute-start | bytes 2064392 | tf_op jit(solution)/shard_map/ppermute | solution.py:39
  156.8 21.3 %collective-permute-start.14 = (bf16[448,768]{1,0:T(8,128)(2,1)S(1)}, bf16[448,768]{1,0:T(8,128)(2,1)}, u32[]{:S(2)}, u32[]{:S(2)}) collective-permute-start(bf16[448,768]{1,0:T(8,128)(2,1)S(1)} %multiply_convert_fusion.8), channel_id=1, source_target_pairs={{0,1},{1,0},{2,3},{3,2},{4,5},{5,4},{6,7},{7,6},{8,9},{9,8},{10,11... | collective-permute-start | bytes 2064392 | tf_op jit(solution)/shard_map/ppermute | solution.py:39
  209.5 18.3 %collective-permute-start.23 = (bf16[448,768]{1,0:T(8,128)(2,1)S(1)}, bf16[448,768]{1,0:T(8,128)(2,1)S(1)}, u32[]{:S(2)}, u32[]{:S(2)}) collective-permute-start(bf16[448,768]{1,0:T(8,128)(2,1)S(1)} %fusion.34), channel_id=1, source_target_pairs={{0,2},{1,3},{2,0},{3,1},{4,6},{5,7},{6,4},{7,5},{8,10},{9,11},{10,... | collective-permute-start | bytes 2064392 | tf_op jit(solution)/shard_map/ppermute | solution.py:39
  217.4 24.8 %collective-permute-start.18 = (bf16[448,768]{1,0:T(8,128)(2,1)S(1)}, bf16[448,768]{1,0:T(8,128)(2,1)S(1)}, u32[]{:S(2)}, u32[]{:S(2)}) collective-permute-start(bf16[448,768]{1,0:T(8,128)(2,1)S(1)} %fusion.36), channel_id=1, source_target_pairs={{0,2},{1,3},{2,0},{3,1},{4,6},{5,7},{6,4},{7,5},{8,10},{9,11},{10,... | collective-permute-start | bytes 2064392 | tf_op jit(solution)/shard_map/ppermute | solution.py:39
  365.7 108.0 %collective-permute-start.36 = (bf16[2,5,768,192]{2,3,1,0:T(8,128)(2,1)}, bf16[2,5,768,192]{2,3,1,0:T(8,128)(2,1)}, u32[]{:S(2)}, u32[]{:S(2)}) collective-permute-start(bf16[2,5,768,192]{2,3,1,0:T(8,128)(2,1)} %pad_maximum_fusion.1), channel_id=1, source_target_pairs={{0,1},{1,0},{2,3},{3,2},{4,5},{5,4},{6,7},{7,6},{8,9},{9,8},{10,11... | collective-permute-start | bytes 8847368 | tf_op jit(solution)/shard_map/ppermute | solution.py:39
  376.4 101.1 %all-to-all-start.1 = ((bf16[8,192,768]{2,1,0:T(8,128)(2,1)}), bf16[8,192,768]{2,1,0:T(8,128)(2,1)}, u32[]{:S(2)}, u32[]{:S(2)}) async-start(bf16[8,192,768]{2,1,0:T(8,128)(2,1)} %bitcast.437), calls=%async_computation.1 | async-start | bytes 4718592 | tf_op jit(solution)/shard_map/all_to_all | solution.py:196
  430.3 16.3 %collective-permute-start.26 = (bf16[2,448,768]{2,1,0:T(8,128)(2,1)}, bf16[2,448,768]{2,1,0:T(8,128)(2,1)}, u32[]{:S(2)}, u32[]{:S(2)}) collective-permute-start(bf16[2,448,768]{2,1,0:T(8,128)(2,1)} %pad_maximum_fusion.10), channel_id=1, source_target_pairs={{0,1},{1,0},{2,3},{3,2},{4,5},{5,4},{6,7},{7,6},{8,9},{9,8},{10,11... | collective-permute-start | bytes 4128776 | tf_op jit(solution)/shard_map/ppermute | solution.py:39
  438.4 116.7 %collective-permute-start.20 = (bf16[448,768]{1,0:T(8,128)(2,1)}, bf16[448,768]{1,0:T(8,128)(2,1)}, u32[]{:S(2)}, u32[]{:S(2)}) collective-permute-start(bf16[448,768]{1,0:T(8,128)(2,1)} %get-tuple-element.84), channel_id=1, source_target_pairs={{0,2},{1,3},{2,0},{3,1},{4,6},{5,7},{6,4},{7,5},{8,10},{9,11},{10,... | collective-permute-start | bytes 2064392 | tf_op jit(solution)/shard_map/ppermute | solution.py:39
  448.9 22.2 %collective-permute-start.27 = (bf16[448,768]{1,0:T(8,128)(2,1)}, bf16[448,768]{1,0:T(8,128)(2,1)}, u32[]{:S(2)}, u32[]{:S(2)}) collective-permute-start(bf16[448,768]{1,0:T(8,128)(2,1)} %fusion.32), channel_id=1, source_target_pairs={{0,2},{1,3},{2,0},{3,1},{4,6},{5,7},{6,4},{7,5},{8,10},{9,11},{10,... | collective-permute-start | bytes 2064392 | tf_op jit(solution)/shard_map/ppermute | solution.py:39
  477.0 35.1 %collective-permute-start.37 = (bf16[5,768,192]{1,2,0:T(8,128)(2,1)}, bf16[5,768,192]{1,2,0:T(8,128)(2,1)}, u32[]{:S(2)}, u32[]{:S(2)}) collective-permute-start(bf16[5,768,192]{1,2,0:T(8,128)(2,1)} %fusion.26), channel_id=1, source_target_pairs={{0,2},{1,3},{2,0},{3,1},{4,6},{5,7},{6,4},{7,5},{8,10},{9,11},{10,... | collective-permute-start | bytes 4423688 | tf_op jit(solution)/shard_map/ppermute | solution.py:39
  483.3 27.7 %collective-permute-start.35 = (f32[4,768]{1,0:T(4,128)S(1)}, f32[4,768]{1,0:T(4,128)S(1)}, u32[]{:S(2)}, u32[]{:S(2)}) collective-permute-start(f32[4,768]{1,0:T(4,128)S(1)} %fusion.107), channel_id=1, source_target_pairs={{0,2},{1,3},{2,0},{3,1},{4,6},{5,7},{6,4},{7,5},{8,10},{9,11},{10,... | collective-permute-start | bytes 36872 | tf_op jit(solution)/shard_map/ppermute | solution.py:39
  550.4 52.1 %collective-permute-start.38 = (bf16[4,295296]{1,0:T(4,128)(2,1)}, bf16[4,295296]{1,0:T(4,128)(2,1)}, u32[]{:S(2)}, u32[]{:S(2)}) collective-permute-start(bf16[4,295296]{1,0:T(4,128)(2,1)} %fusion.29), channel_id=1, source_target_pairs={{0,4},{4,0},{8,12},{12,8},{16,20},{20,16},{24,28},{28,24},{1,5},{5... | collective-permute-start | bytes 7087112 | tf_op jit(solution)/shard_map/ppermute | solution.py:39
  555.6 17.5 %collective-permute-start.28 = (bf16[448,768]{1,0:T(8,128)(2,1)S(1)}, bf16[448,768]{1,0:T(8,128)(2,1)}, u32[]{:S(2)}, u32[]{:S(2)}) collective-permute-start(bf16[448,768]{1,0:T(8,128)(2,1)S(1)} %add_convert_fusion.3), channel_id=1, source_target_pairs={{0,1},{1,0},{2,3},{3,2},{4,5},{5,4},{6,7},{7,6},{8,9},{9,8},{10,11... | collective-permute-start | bytes 2064392 | tf_op jit(solution)/shard_map/ppermute | solution.py:39
  580.5 79.0 %collective-permute-start.32 = (bf16[8,192,768]{2,1,0:T(8,128)(2,1)}, bf16[8,192,768]{2,1,0:T(8,128)(2,1)}, u32[]{:S(2)}, u32[]{:S(2)}) collective-permute-start(bf16[8,192,768]{2,1,0:T(8,128)(2,1)} %fusion.22), channel_id=1, source_target_pairs={{0,2},{1,3},{2,0},{3,1},{4,6},{5,7},{6,4},{7,5},{8,10},{9,11},{10,... | collective-permute-start | bytes 7077896 | tf_op jit(solution)/shard_map/ppermute | solution.py:39
  624.0 25.6 %collective-permute-start.39 = (bf16[2,295296]{1,0:T(2,128)(2,1)S(1)}, bf16[2,295296]{1,0:T(2,128)(2,1)S(1)}, u32[]{:S(2)}, u32[]{:S(2)}) collective-permute-start(bf16[2,295296]{1,0:T(2,128)(2,1)S(1)} %bitcast.438), channel_id=1, source_target_pairs={{0,8},{4,12},{8,0},{12,4},{16,24},{20,28},{24,16},{28,20},{1,9},{5... | collective-permute-start | bytes 3543560 | tf_op jit(solution)/shard_map/ppermute | solution.py:39
  653.9 50.8 %collective-permute-start.40 = (bf16[1,295296]{1,0:T(2,128)(2,1)S(1)}, bf16[1,295296]{1,0:T(2,128)(2,1)S(1)}, u32[]{:S(2)}, u32[]{:S(2)}) collective-permute-start(bf16[1,295296]{1,0:T(2,128)(2,1)S(1)} %dynamic-slice_convert_fusion.1), channel_id=1, source_target_pairs={{0,16},{4,20},{8,24},{12,28},{16,0},{20,4},{24,8},{28,12},{1,17},{... | collective-permute-start | bytes 1771784 | tf_op jit(solution)/shard_map/ppermute | solution.py:39
  659.5 56.7 %collective-permute-start.31 = (bf16[8,192,768]{2,1,0:T(8,128)(2,1)}, bf16[8,192,768]{2,1,0:T(8,128)(2,1)}, u32[]{:S(2)}, u32[]{:S(2)}) collective-permute-start(bf16[8,192,768]{2,1,0:T(8,128)(2,1)} %fusion.22), channel_id=1, source_target_pairs={{0,1},{1,0},{2,3},{3,2},{4,5},{5,4},{6,7},{7,6},{8,9},{9,8},{10,11... | collective-permute-start | bytes 7077896 | tf_op jit(solution)/shard_map/ppermute | solution.py:39
  659.5 56.7 %collective-permute-start.33 = (bf16[8,192,768]{2,1,0:T(8,128)(2,1)}, bf16[8,192,768]{2,1,0:T(8,128)(2,1)}, u32[]{:S(2)}, u32[]{:S(2)}) collective-permute-start(bf16[8,192,768]{2,1,0:T(8,128)(2,1)} %collective-permute-done.32), channel_id=1, source_target_pairs={{0,1},{1,0},{2,3},{3,2},{4,5},{5,4},{6,7},{7,6},{8,9},{9,8},{10,11... | collective-permute-start | bytes 7077896 | tf_op jit(solution)/shard_map/ppermute | solution.py:39
  (127 other events, 1318.2 us)

commit v2 on v1

v2 whole, which is shorter than its diff:
```python
import functools

import jax
import jax.numpy as jnp
from jax import lax
from jax.experimental import pallas as pl
from jax.experimental.pallas import tpu as pltpu
from jax.sharding import PartitionSpec as P

HEAD_DIM = 64
AUDIO = 1500
EPSILON = 1e-05
NEG_FILL = -1e30
INV_ROOT = HEAD_DIM**-0.5
F32 = jnp.float32
BF16 = jnp.bfloat16
VMEM_LIMIT = 56 << 20
COST_SCALE = 1.0


def dot(left, right, left_dim=1, right_dim=0):
    return lax.dot_general(
        left, right, (((left_dim,), (right_dim,)), ((), ())), preferred_element_type=F32
    )


def call(body, grid, in_specs, out_specs, out_shape, name, estimate, prefetch=0, scratch=()):
    return pl.pallas_call(
        body,
        grid_spec=pltpu.PrefetchScalarGridSpec(
            num_scalar_prefetch=prefetch,
            grid=grid,
            in_specs=in_specs,
            out_specs=out_specs,
            scratch_shapes=list(scratch),
        ),
        out_shape=out_shape,
        compiler_params=pltpu.CompilerParams(vmem_limit_bytes=VMEM_LIMIT),
        cost_estimate=estimate,
        name=name,
    )


def shape(dims, dtype=BF16):
    return jax.ShapeDtypeStruct(dims, dtype)


def cost(flops, moved, exps=0):
    scale = COST_SCALE
    return pl.CostEstimate(
        flops=int(flops * scale), bytes_accessed=int(moved * scale), transcendentals=int(exps * scale)
    )


def whole(shape):
    return pl.BlockSpec(shape, lambda *_: (0,) * len(shape))


def norm_stats(values):
    center = values - jnp.mean(values, axis=-1, keepdims=True)
    spread = jnp.mean(center * center, axis=-1, keepdims=True)
    inverse = lax.rsqrt(spread + EPSILON)
    return center * inverse, inverse


def norm_back(unit, inverse, gain_row, grad):
    scaled = grad * gain_row
    first = jnp.mean(scaled, axis=-1, keepdims=True)
    second = jnp.mean(scaled * unit, axis=-1, keepdims=True)
    return (scaled - first - unit * second) * inverse


def swap(values, axis, bit):
    size = lax.axis_size(axis)
    return lax.ppermute(values, axis, [(i, i ^ bit) for i in range(size)])


def gather_narrow(own):
    other = swap(own, "narrow", 2)
    return [own, swap(own, "narrow", 1), other]


def finish(blocks, then):
    return blocks + [swap(then(blocks[2]), "narrow", 1)]


class Order:
    def __init__(self):
        self.last = None

    def __call__(self, item, *named):
        named = named if self.last is None else named + (self.last,)
        if named:
            item, _ = lax.optimization_barrier((item, named))
        return item


def encode_body(order, memory_ref, gain_ref, out_ref):
    unit, _ = norm_stats(memory_ref[:, 0].astype(F32))
    out_ref[...] = (unit * gain_ref[...]).astype(BF16)


def encode(order, memory, gain_row, start, size):
    wide, _, _, width = memory.shape
    group = min(4, wide)
    return call(
        encode_body,
        (wide // group,),
        [
            pl.BlockSpec((group, 1, size, width), lambda i, order: (i, order[0], start // size, 0)),
            whole((1, width)),
        ],
        pl.BlockSpec((group, size, width), lambda i, *_: (i, 0, 0)),
        shape((wide, size, width)),
        "encode",
        cost(0, 4 * wide * size * width),
        prefetch=1,
    )(order, memory, gain_row)


def memory_back_body(order, memory_ref, gain_ref, grad_ref, out_ref, gain_out):
    unit, inverse = norm_stats(memory_ref[:, 0].astype(F32))
    grad = grad_ref[...].astype(F32)
    out_ref[...] = norm_back(unit, inverse, gain_ref[...], grad).astype(BF16)

    @pl.when(pl.program_id(0) == 0)
    def _():
        gain_out[...] = jnp.zeros_like(gain_out)

    gain_out[...] += jnp.sum(jnp.sum(grad * unit, axis=0), axis=0, keepdims=True)


def memory_back(order, memory, gain_row, grad, start):
    wide, _, _, width = memory.shape
    size = grad.shape[1]
    group = min(4, wide)
    rows = pl.BlockSpec((group, size, width), lambda i, *_: (i, 0, 0))
    return call(
        memory_back_body,
        (wide // group,),
        [
            pl.BlockSpec((group, 1, size, width), lambda i, order: (i, order[0], start // size, 0)),
            whole((1, width)),
            rows,
        ],
        [rows, whole((1, width))],
        [shape((wide, size, width)), shape((1, width), F32)],
        "memory_back",
        cost(0, 6 * wide * size * width),
        prefetch=1,
    )(order, memory, gain_row, grad)


def self_fwd_body(order, lengths, token_ref, gain_ref, weight_ref, normed_ref, qkv_ref, first_ref, second_ref, lse_ref):
    seq = token_ref.shape[1]
    heads = weight_ref.shape[1] // HEAD_DIM
    step = pl.program_id(0)
    length = lengths[order[step]]
    unit, _ = norm_stats(token_ref[0].astype(F32))
    normed = (unit * gain_ref[...]).astype(BF16)
    normed_ref[0] = normed
    for i in range(3):
        qkv_ref[0, i] = dot(normed, weight_ref[i], 1, 1).astype(BF16)
    cut = 256 if seq > 256 else seq
    mixed = []
    for h in range(heads):
        columns = slice(h * HEAD_DIM, (h + 1) * HEAD_DIM)
        parts = []
        for start, stop in ((0, cut), (cut, seq)):
            if start == stop:
                continue
            queries = qkv_ref[0, 0, start:stop, columns] * jnp.asarray(INV_ROOT, BF16)
            scores = dot(qkv_ref[0, 1, :stop, columns], queries, 1, 1)
            key = lax.broadcasted_iota(jnp.int32, scores.shape, 0)
            query = lax.broadcasted_iota(jnp.int32, scores.shape, 1) + start
            scores = jnp.where((key <= query) & (key < length), scores, NEG_FILL)
            top = jnp.max(scores, axis=0, keepdims=True)
            probs = jnp.exp(scores - top)
            total = jnp.sum(probs, axis=0, keepdims=True)
            out = dot(qkv_ref[0, 2, :stop, columns], probs.astype(BF16), 0, 0) / total
            parts.append(out.T)
            lse_ref[0, h : h + 1, start:stop] = top + jnp.log(total)
        mixed.append(jnp.concatenate(parts, axis=0))
    mixed = jnp.concatenate(mixed, axis=1).astype(BF16)

    @pl.when(step == 0)
    def _():
        first_ref[...] = mixed

    @pl.when(step == 1)
    def _():
        second_ref[...] = mixed


def self_fwd(order, lengths, tokens, gain_row, weights):
    _, seq, width = tokens.shape
    local = weights.shape[1]
    heads = local // HEAD_DIM
    return call(
        self_fwd_body,
        (2,),
        [
            pl.BlockSpec((1, seq, width), lambda i, order, lengths: (order[i], 0, 0)),
            whole((1, width)),
            whole((3, local, width)),
        ],
        [
            pl.BlockSpec((1, seq, width), lambda i, *_: (i, 0, 0)),
            pl.BlockSpec((1, 3, seq, local), lambda i, *_: (i, 0, 0, 0)),
            whole((seq, local)),
            whole((seq, local)),
            pl.BlockSpec((1, heads, seq), lambda i, *_: (i, 0, 0)),
        ],
        [
            shape((2, seq, width)),
            shape((2, 3, seq, local)),
            shape((seq, local)),
            shape((seq, local)),
            shape((2, heads, seq), F32),
        ],
        "self_forward",
        cost(2 * (6 * seq * width * local + 8 * seq * seq * local), 2 * seq * width * 8, 2 * heads * seq * seq),
        prefetch=2,
    )(order, lengths, tokens, gain_row, weights)


def self_bwd_body(order, lengths, qkv_ref, mixed0_ref, mixed1_ref, lse_ref, grad0_ref, grad1_ref, weight_ref, dqkv_ref, first_ref, second_ref):
    seq = qkv_ref.shape[2]
    heads = weight_ref.shape[1] // HEAD_DIM
    step = pl.program_id(0)
    length = lengths[order[step]]
    grad = jnp.where(step == 0, grad0_ref[...], grad1_ref[...])
    mixed = jnp.where(step == 0, mixed0_ref[...], mixed1_ref[...])
    inner = (grad.astype(F32) * mixed.astype(F32)).T
    cut = 256 if seq > 256 else seq
    for h in range(heads):
        columns = slice(h * HEAD_DIM, (h + 1) * HEAD_DIM)
        keys = qkv_ref[0, 1, :, columns]
        values = qkv_ref[0, 2, :, columns]
        dq_parts = []
        dk = jnp.zeros((seq, HEAD_DIM), F32)
        dv = jnp.zeros((seq, HEAD_DIM), F32)
        for start, stop in ((0, cut), (cut, seq)):
            if start == stop:
                continue
            queries = qkv_ref[0, 0, start:stop, columns] * jnp.asarray(INV_ROOT, BF16)
            grads = grad[start:stop, columns]
            scores = dot(keys[:stop], queries, 1, 1)
            key = lax.broadcasted_iota(jnp.int32, scores.shape, 0)
            query = lax.broadcasted_iota(jnp.int32, scores.shape, 1) + start
            allowed = (key <= query) & (key < length)
            probs = jnp.exp(jnp.where(allowed, scores, NEG_FILL) - lse_ref[0, h : h + 1, start:stop])
            dp = dot(values[:stop], grads, 1, 1)
            centre = jnp.sum(inner[columns, start:stop], axis=0, keepdims=True)
            ds = (probs * (dp - centre)).astype(BF16)
            dk_now = dot(ds, queries)
            dv_now = dot(probs.astype(BF16), grads)
            if stop < seq:
                pad = jnp.zeros((seq - stop, HEAD_DIM), F32)
                dk_now = jnp.concatenate((dk_now, pad), axis=0)
                dv_now = jnp.concatenate((dv_now, pad), axis=0)
            dk, dv = dk + dk_now, dv + dv_now
            dq_parts.append((dot(keys[:stop], ds, 0, 0) * INV_ROOT).T)
        dqkv_ref[0, 0, :, columns] = jnp.concatenate(dq_parts, axis=0).astype(BF16)
        dqkv_ref[0, 1, :, columns] = dk.astype(BF16)
        dqkv_ref[0, 2, :, columns] = dv.astype(BF16)
    total = dot(dqkv_ref[0, 0], weight_ref[0])
    total = total + dot(dqkv_ref[0, 1], weight_ref[1])
    total = (total + dot(dqkv_ref[0, 2], weight_ref[2])).astype(BF16)

    @pl.when(step == 0)
    def _():
        first_ref[...] = total

    @pl.when(step == 1)
    def _():
        second_ref[...] = total


def self_bwd(order, lengths, qkv, mixed0, mixed1, lse, grad0, grad1, weights):
    _, _, seq, local = qkv.shape
    width = weights.shape[2]
    heads = local // HEAD_DIM
    return call(
        self_bwd_body,
        (2,),
        [
            pl.BlockSpec((1, 3, seq, local), lambda i, *_: (i, 0, 0, 0)),
            whole((seq, local)),
            whole((seq, local)),
            pl.BlockSpec((1, heads, seq), lambda i, *_: (i, 0, 0)),
            whole((seq, local)),
            whole((seq, local)),
            whole((3, local, width)),
        ],
        [
            pl.BlockSpec((1, 3, seq, local), lambda i, *_: (i, 0, 0, 0)),
            whole((seq, width)),
            whole((seq, width)),
        ],
        [shape((2, 3, seq, local)), shape((seq, width)), shape((seq, width))],
        "self_backward",
        cost(2 * (6 * seq * width * local + 20 * seq * seq * local), 2 * seq * width * 8, 2 * heads * seq * seq),
        prefetch=2,
    )(order, lengths, qkv, mixed0, mixed1, lse, grad0, grad1, weights)


def to_query_body(order, token_ref, m0, m1, m2, m3, p0, p1, p2, p3, gain_ref, after_ref, normed_ref, query_ref):
    local = m0.shape[1]
    rows = token_ref[0].astype(F32)
    for mixed, pack in ((m0, p0), (m1, p1), (m2, p2), (m3, p3)):
        rows = rows + dot(mixed[...], pack[:local])
    after_ref[...] = rows
    unit, _ = norm_stats(rows)
    normed = (unit * gain_ref[...]).astype(BF16)
    normed_ref[...] = normed
    for r, pack in enumerate((p0, p1, p2, p3)):
        query = dot(normed, pack[local:], 1, 1).astype(BF16)
        query_ref[r // 2, :, (r % 2) * local : (r % 2 + 1) * local] = query


def to_query(order, tokens, mixes, packs, gain_row):
    _, seq, width = tokens.shape
    local = mixes[0].shape[1]
    tile = seq // 2
    return call(
        to_query_body,
        (2,),
        [pl.BlockSpec((1, tile, width), lambda i, order: (order[0], i, 0))]
        + [pl.BlockSpec((tile, local), lambda i, *_: (i, 0))] * 4
        + [whole((2 * local, width))] * 4
        + [whole((1, width))],
        [
            pl.BlockSpec((tile, width), lambda i, *_: (i, 0)),
            pl.BlockSpec((tile, width), lambda i, *_: (i, 0)),
            pl.BlockSpec((2, tile, 2 * local), lambda i, *_: (0, i, 0)),
        ],
        [shape((seq, width), F32), shape((seq, width)), shape((2, seq, 2 * local))],
        "self_out_to_query",
        cost(4 * seq * width * width, seq * width * 12 + 4 * width * width),
        prefetch=1,
    )(order, tokens, *mixes, *packs, gain_row)


def head_places(local):
    for r in range(2):
        for h in range(local // HEAD_DIM):
            at = r * local + h * HEAD_DIM
            key = 2 * r * local + h * HEAD_DIM
            yield (
                at // HEAD_DIM,
                slice(at, at + HEAD_DIM),
                slice(key, key + HEAD_DIM),
                slice(key + local, key + local + HEAD_DIM),
            )


def cross_first_body(query_ref, encoded_ref, w0, w1, w2, w3, kv_ref, acc_ref, top_ref, total_ref, *, valid):
    make_keys_values(encoded_ref, (w0, w1, w2, w3), kv_ref)
    frames = kv_ref.shape[0]
    for head, columns, key, value in head_places(query_ref.shape[2] // 2):
        queries = query_ref[0, :, columns] * jnp.asarray(INV_ROOT, BF16)
        scores = dot(kv_ref[:, key], queries, 1, 1)
        if valid < frames:
            frame = lax.broadcasted_iota(jnp.int32, scores.shape, 0)
            scores = jnp.where(frame < valid, scores, NEG_FILL)
        top = jnp.max(scores, axis=0, keepdims=True)
        probs = jnp.exp(scores - top)
        acc_ref[0, columns, :] = dot(kv_ref[:, value], probs.astype(BF16), 0, 0)
        top_ref[0, head : head + 1, :] = top
        total_ref[0, head : head + 1, :] = jnp.sum(probs, axis=0, keepdims=True)


def make_keys_values(encoded_ref, weights, kv_ref):
    pair = weights[0].shape[0]
    for step in range(2):

        @pl.when(pl.program_id(0) == step)
        def _():
            for r in range(2):
                kv = dot(encoded_ref[...], weights[2 * step + r][...], 1, 1)
                kv_ref[:, r * pair : (r + 1) * pair] = kv.astype(BF16)


def cross_second_body(
    query_ref, encoded_ref, w0, w1, w2, w3, acc_in, top_in, total_in, after_ref, o0, o1, o2, o3, gain_ref,
    kv_ref, mixed_ref, lse_ref, next_ref, normed_ref, *, valid,
):
    make_keys_values(encoded_ref, (w0, w1, w2, w3), kv_ref)
    frames = kv_ref.shape[0]
    local = o0.shape[0]
    for head, columns, key, value in head_places(local):
        queries = query_ref[0, :, columns] * jnp.asarray(INV_ROOT, BF16)
        scores = dot(kv_ref[:, key], queries, 1, 1)
        if valid < frames:
            frame = lax.broadcasted_iota(jnp.int32, scores.shape, 0)
            scores = jnp.where(frame < valid, scores, NEG_FILL)
        before = top_in[0, head : head + 1, :]
        top = jnp.maximum(jnp.max(scores, axis=0, keepdims=True), before)
        probs = jnp.exp(scores - top)
        fade = jnp.exp(before - top)
        total = jnp.sum(probs, axis=0, keepdims=True) + total_in[0, head : head + 1, :] * fade
        out = dot(kv_ref[:, value], probs.astype(BF16), 0, 0) + acc_in[0, columns, :] * fade
        mixed_ref[0, :, columns] = (out / total).T.astype(BF16)
        lse_ref[0, head : head + 1, :] = top + jnp.log(total)
    outs = (o0, o1, o2, o3)
    for step in range(2):

        @pl.when(pl.program_id(0) == step)
        def _():
            rows = after_ref[...] if step == 0 else next_ref[...]
            for r in range(2):
                rows = rows + dot(mixed_ref[0, :, r * local : (r + 1) * local], outs[2 * step + r][...])
            next_ref[...] = rows
            if step == 1:
                unit, _ = norm_stats(rows)
                normed_ref[...] = (unit * gain_ref[...]).astype(BF16)


def pack_specs(packs, rows, index):
    width = packs[0].shape[1]
    return [pl.BlockSpec((rows, width), lambda *_: (index, 0))] * 4


def cross_first(query, encoded, packs, valid):
    _, seq, pair = query.shape
    frames, width = encoded.shape
    heads = pair // HEAD_DIM
    stats = pl.BlockSpec((1, heads, seq), lambda i: (i, 0, 0))
    return call(
        functools.partial(cross_first_body, valid=valid),
        (2,),
        [pl.BlockSpec((1, seq, pair), lambda i: (i, 0, 0)), whole((frames, width))] + pack_specs(packs, pair, 0),
        [
            pl.BlockSpec((frames, 2 * pair), lambda i: (0, i)),
            pl.BlockSpec((1, pair, seq), lambda i: (i, 0, 0)),
            stats,
            stats,
        ],
        [
            shape((frames, 4 * pair)),
            shape((2, pair, seq), F32),
            shape((2, heads, seq), F32),
            shape((2, heads, seq), F32),
        ],
        "cross_first",
        cost(4 * frames * width * width + 40 * seq * frames * pair, 8 * frames * width, 2 * heads * seq * frames),
    )(query, encoded, *packs)


def cross_second(query, encoded, packs, packs_out, valid, before, after, gain_row):
    _, seq, pair = query.shape
    frames, width = encoded.shape
    heads = pair // HEAD_DIM
    rows = pl.BlockSpec((1, seq, pair), lambda i: (i, 0, 0))
    stats = pl.BlockSpec((1, heads, seq), lambda i: (i, 0, 0))
    acc = pl.BlockSpec((1, pair, seq), lambda i: (i, 0, 0))
    return call(
        functools.partial(cross_second_body, valid=valid),
        (2,),
        [rows, whole((frames, width))]
        + pack_specs(packs, pair, 0)
        + [acc, stats, stats, whole((seq, width))]
        + pack_specs(packs_out, pair // 2, 0)
        + [whole((1, width))],
        [pl.BlockSpec((frames, 2 * pair), lambda i: (0, i)), rows, stats, whole((seq, width)), whole((seq, width))],
        [
            shape((frames, 4 * pair)),
            shape((2, seq, pair)),
            shape((2, heads, seq), F32),
            shape((seq, width), F32),
            shape((seq, width)),
        ],
        "cross_second",
        cost(4 * frames * width * width + 40 * seq * frames * pair, 10 * frames * width, 2 * heads * seq * frames),
    )(query, encoded, *packs, *before, after, *packs_out, gain_row)


def feed_body(order, lengths, *refs, count):
    row_refs, (grad_ref, in_ref, out_ref, hidden_ref, pre_ref, live_ref) = refs[:count], refs[count : count + 6]
    outs = refs[count + 6 :]
    step = pl.program_id(0)
    tile = grad_ref.shape[1]
    rows = row_refs[0][...]
    if count == 2:
        rows = jnp.where(step == 0, rows, row_refs[1][...])
    place = lax.broadcasted_iota(jnp.int32, grad_ref.shape[1:], 0) + pl.program_id(1) * tile
    grads = jnp.where(place < lengths[order[step]], grad_ref[0], jnp.zeros((), BF16))
    live_ref[0] = grads
    pre = dot(rows, in_ref[...])
    half = 0.5 * (1.0 + lax.erf(pre * (0.5**0.5)))
    hidden = (pre * half).astype(BF16)
    slope = half + pre * jnp.exp(-0.5 * pre * pre) * 0.3989422804014327
    hidden_ref[0] = hidden
    grad_pre = (dot(grads, out_ref[...], 1, 1) * slope).astype(BF16)
    pre_ref[0] = grad_pre
    part = dot(grad_pre, in_ref[...], 1, 1).astype(BF16)
    feed = dot(hidden, out_ref[...]).astype(BF16)
    for i in range(count):

        @pl.when(step == i)
        def _():
            outs[2 * i][...] = part
            outs[2 * i + 1][...] = feed


def feed_forward(order, lengths, rows, out_grad, fc_in, fc_out):
    count = len(rows)
    seq, width = rows[0].shape
    units = fc_in.shape[1]
    tiles = 2
    tile = seq // tiles
    block = lambda last: pl.BlockSpec((1, tile, last), lambda i, j, *_: (i, j, 0))
    single = [
        pl.BlockSpec((tile, width), lambda i, j, *_: (jnp.where(i == 0, j, tiles - 1), 0)),
        pl.BlockSpec((tile, width), lambda i, j, *_: (jnp.where(i == 0, 0, j), 0)),
    ]
    if count == 1:
        single = [pl.BlockSpec((tile, width), lambda i, j, *_: (j, 0))]
    return call(
        functools.partial(feed_body, count=count),
        (count, tiles),
        single
        + [
            pl.BlockSpec((1, tile, width), lambda i, j, order, lengths: (order[i], j, 0)),
            whole((width, units)),
            whole((units, width)),
        ],
        [block(units), block(units), block(width)] + [spec for spec in single for _ in range(2)],
        [shape((count, seq, units)), shape((count, seq, units)), shape((count, seq, width))]
        + [shape((seq, width))] * (2 * count),
        "feed_forward",
        cost(8 * count * seq * width * units, count * seq * width * 14, 2 * count * seq * units),
        prefetch=2,
    )(order, lengths, *rows, out_grad, fc_in, fc_out)


def add_gain(gain_out, term):
    @pl.when(pl.program_id(0) == 0)
    def _():
        gain_out[...] = jnp.zeros_like(gain_out)

    gain_out[...] += term


def cross_back(queries_ref, kv_ref, grads_ref, mixed_ref, lse_ref, dkv_ref, local, valid, store):
    frames = kv_ref.shape[0]
    inner = (grads_ref.astype(F32) * mixed_ref[0].astype(F32)).T
    for head, columns, key, value in head_places(local):
        queries = queries_ref[0, :, columns] * jnp.asarray(INV_ROOT, BF16)
        grads = grads_ref[:, columns]
        centre = jnp.sum(inner[columns, :], axis=0, keepdims=True)
        keys = kv_ref[:, key]
        probs = jnp.exp(dot(keys, queries, 1, 1) - lse_ref[0, head : head + 1, :])
        if valid < frames:
            frame = lax.broadcasted_iota(jnp.int32, probs.shape, 0)
            probs = jnp.where(frame < valid, probs, 0.0)
        dp = dot(kv_ref[:, value], grads, 1, 1)
        ds = (probs * (dp - centre)).astype(BF16)
        dkv_ref[:, value] = dot(probs.astype(BF16), grads).astype(BF16)
        dkv_ref[:, key] = dot(ds, queries).astype(BF16)
        store(columns, dot(keys, ds, 0, 0))


def encoded_back(dkv_ref, weights, out_ref, acc):
    pair = weights[0].shape[0]
    for step in range(2):

        @pl.when(pl.program_id(0) == step)
        def _():
            total = dot(dkv_ref[:, :pair], weights[2 * step][...]) + dot(dkv_ref[:, pair:], weights[2 * step + 1][...])
            if step == 0:
                acc[...] = total
            else:
                out_ref[...] = (acc[...] + total).astype(BF16)


def cross_first_back_body(
    order, lengths, grad_ref, own_ref, near_ref, far_ref, after_ref, gain_ref, o0, o1, o2, o3,
    query_ref, kv_ref, mixed_ref, lse_ref, w0, w1, w2, w3,
    cross_ref, two_ref, grads_ref, gain_out, dq_ref, dkv_ref, encoded_ref, acc, *, valid,
):
    local = o0.shape[0]
    step = pl.program_id(0)

    @pl.when(step == 0)
    def _():
        place = lax.broadcasted_iota(jnp.int32, own_ref.shape, 0)
        grads = jnp.where(place < lengths[order[0]], grad_ref[0].astype(F32), 0.0)
        normed_grad = own_ref[...].astype(F32) + near_ref[...].astype(F32) + far_ref[...].astype(F32)
        unit, inverse = norm_stats(after_ref[...])
        total = grads + norm_back(unit, inverse, gain_ref[...], normed_grad)
        cross_ref[...] = total
        low = total.astype(BF16)
        two_ref[...] = low
        for r, weight in enumerate((o0, o1, o2, o3)):
            mixed = dot(low, weight[...], 1, 1).astype(BF16)
            grads_ref[r // 2, :, (r % 2) * local : (r % 2 + 1) * local] = mixed
        gain_out[...] = jnp.sum(normed_grad * unit, axis=0, keepdims=True)

    def store(columns, dq):
        dq_ref[0, columns, :] = dq

    cross_back(query_ref, kv_ref, grads_ref[step], mixed_ref, lse_ref, dkv_ref, local, valid, store)
    encoded_back(dkv_ref, (w0, w1, w2, w3), encoded_ref, acc)


def cross_first_back(order, lengths, out_grad, parts, after, gain_row, packs, packs_out, query, kv, mixed, lse, valid):
    seq, width = after.shape
    frames = kv.shape[0]
    pair = query.shape[2]
    heads = pair // HEAD_DIM
    rows = whole((seq, width))
    head_rows = pl.BlockSpec((1, seq, pair), lambda i, *_: (i, 0, 0))
    both = pl.BlockSpec((frames, 2 * pair), lambda i, *_: (0, i))
    return call(
        functools.partial(cross_first_back_body, valid=valid),
        (2,),
        [pl.BlockSpec((1, seq, width), lambda i, order, lengths: (order[0], 0, 0)), rows, rows, rows, rows]
        + [whole((1, width))]
        + pack_specs(packs_out, pair // 2, 0)
        + [head_rows, both, head_rows, pl.BlockSpec((1, heads, seq), lambda i, *_: (i, 0, 0))]
        + pack_specs(packs, pair, 0),
        [
            rows,
            rows,
            whole((2, seq, pair)),
            whole((1, width)),
            pl.BlockSpec((1, pair, seq), lambda i, *_: (i, 0, 0)),
            both,
            whole((frames, width)),
        ],
        [
            shape((seq, width), F32),
            shape((seq, width)),
            shape((2, seq, pair)),
            shape((1, width), F32),
            shape((2, pair, seq), F32),
            shape((frames, 2 * width)),
            shape((frames, width)),
        ],
        "cross_first_back",
        cost(4 * frames * width * width + 120 * seq * frames * pair, 20 * frames * width, 2 * heads * seq * frames),
        prefetch=2,
        scratch=[pltpu.VMEM((frames, width), F32)],
    )(order, lengths, out_grad, *parts, after, gain_row, *packs_out, query, kv, mixed, lse, *packs)


def cross_second_back_body(
    query_ref, kv_ref, grads_ref, mixed_ref, lse_ref, dq_in, w0, w1, w2, w3,
    p0, p1, p2, p3, after_ref, gain_ref, cross_ref,
    dq_ref, dkv_ref, encoded_ref, self_ref, one_ref, h0, h1, h2, h3, gain_out, acc, *, valid,
):
    local = h0.shape[1]
    step = pl.program_id(0)

    def store(columns, dq):
        dq_ref[step, :, columns] = ((dq + dq_in[0, columns, :]) * INV_ROOT).T.astype(BF16)

    cross_back(query_ref, kv_ref, grads_ref[0], mixed_ref, lse_ref, dkv_ref, local, valid, store)
    encoded_back(dkv_ref, (w0, w1, w2, w3), encoded_ref, acc)

    @pl.when(step == 1)
    def _():
        packs = (p0, p1, p2, p3)
        normed_grad = 0.0
        for r, pack in enumerate(packs):
            normed_grad = normed_grad + dot(dq_ref[r // 2, :, (r % 2) * local : (r % 2 + 1) * local], pack[local:])
        unit, inverse = norm_stats(after_ref[...])
        total = cross_ref[...] + norm_back(unit, inverse, gain_ref[...], normed_grad)
        self_ref[...] = total
        low = total.astype(BF16)
        one_ref[...] = low
        for out, pack in zip((h0, h1, h2, h3), packs):
            out[...] = dot(low, pack[:local], 1, 1).astype(BF16)
        gain_out[...] = jnp.sum(normed_grad * unit, axis=0, keepdims=True)


def cross_second_back(query, kv, grads, mixed, lse, dq, packs_two, packs_one, after, gain_row, cross, valid):
    seq, width = after.shape
    frames = kv.shape[0]
    pair = query.shape[2]
    local = pair // 2
    heads = pair // HEAD_DIM
    rows = whole((seq, width))
    head_rows = pl.BlockSpec((1, seq, pair), lambda i: (i, 0, 0))
    both = pl.BlockSpec((frames, 2 * pair), lambda i: (0, i))
    return call(
        functools.partial(cross_second_back_body, valid=valid),
        (2,),
        [head_rows, both, head_rows, head_rows, pl.BlockSpec((1, heads, seq), lambda i: (i, 0, 0))]
        + [pl.BlockSpec((1, pair, seq), lambda i: (i, 0, 0))]
        + pack_specs(packs_two, pair, 0)
        + pack_specs(packs_one, pair, 0)
        + [rows, whole((1, width)), rows],
        [whole((2, seq, pair)), both, whole((frames, width)), rows, rows]
        + [whole((seq, local))] * 4
        + [whole((1, width))],
        [
            shape((2, seq, pair)),
            shape((frames, 2 * width)),
            shape((frames, width)),
            shape((seq, width), F32),
            shape((seq, width)),
        ]
        + [shape((seq, local))] * 4
        + [shape((1, width), F32)],
        "cross_second_back",
        cost(4 * frames * width * width + 120 * seq * frames * pair, 20 * frames * width, 2 * heads * seq * frames),
        scratch=[pltpu.VMEM((frames, width), F32)],
    )(query, kv, grads, mixed, lse, dq, *packs_two, *packs_one, after, gain_row, cross)


def add_gain(gain_out, term):
    @pl.when(pl.program_id(0) == 0)
    def _():
        gain_out[...] = jnp.zeros_like(gain_out)

    gain_out[...] += term

def to_tokens_grad_body(order, token_ref, own_ref, near_ref, far_ref, self_ref, gain_ref, out_ref, gain_out):
    normed_grad = own_ref[...].astype(F32) + near_ref[...].astype(F32) + far_ref[...].astype(F32)
    unit, inverse = norm_stats(token_ref[0].astype(F32))
    out_ref[...] = (self_ref[...] + norm_back(unit, inverse, gain_ref[...], normed_grad)).astype(BF16)
    add_gain(gain_out, jnp.sum(normed_grad * unit, axis=0, keepdims=True))


def to_tokens_grad(order, tokens, own, near, far, grad_self, gain_row):
    _, seq, width = tokens.shape
    tile = seq // 2
    rows = pl.BlockSpec((tile, width), lambda i, *_: (i, 0))
    return call(
        to_tokens_grad_body,
        (2,),
        [pl.BlockSpec((1, tile, width), lambda i, order: (order[0], i, 0)), rows, rows, rows, rows, whole((1, width))],
        [rows, whole((1, width))],
        [shape((seq, width)), shape((1, width), F32)],
        "norm_one_back",
        cost(0, seq * width * 14),
        prefetch=1,
    )(order, tokens, own, near, far, grad_self, gain_row)


def split_store(total, mine, keep_ref, give_ref, scratch, lead=()):
    scratch[...] = total
    parts, depth = keep_ref.shape[-3], keep_ref.shape[-2]
    for j in range(parts):
        at = pl.multiple_of((2 * j + mine) * depth, 8)
        keep_ref[lead + (j,)] = scratch[pl.ds(at, depth), :].astype(BF16)
        at = pl.multiple_of((2 * j + 1 - mine) * depth, 8)
        give_ref[lead + (j,)] = scratch[pl.ds(at, depth), :].astype(BF16)


def feed_weights_body(bits, *refs):
    rows, pres, lives, hiddens = refs[:4], refs[4:7], refs[7:10], refs[10:13]
    keep_ref, give_ref, scratch = refs[13:]
    three = lambda items: (items[0][0], items[0][1], items[1][0], items[2][0])
    total = 0.0
    for left, right in zip(rows, three(pres)):
        total = total + dot(left[...], right, 0, 0)
    split_store(total, bits[0], keep_ref, give_ref, scratch, (0,))
    total = 0.0
    for left, right in zip(three(lives), three(hiddens)):
        total = total + dot(left, right, 0, 0)
    split_store(total, bits[0], keep_ref, give_ref, scratch, (1,))


def feed_weights(bits, rows, pres, lives, hiddens, wide):
    seq, width = rows[0].shape
    units = pres[0].shape[2]
    tile = width // 2
    depth = width // wide
    column = lambda count: pl.BlockSpec((count, seq, tile), lambda i, *_: (0, 0, i))
    full = lambda count: whole((count, seq, units))
    out = pl.BlockSpec((2, wide // 4, depth, units), lambda i, *_: (0, i, 0, 0))
    return call(
        feed_weights_body,
        (2,),
        [pl.BlockSpec((seq, tile), lambda i, *_: (0, i))] * 4
        + [full(2), full(1), full(1), column(2), column(1), column(1), full(2), full(1), full(1)],
        [out, out],
        [shape((2, wide // 2, depth, units))] * 2,
        "feed_weight_grads",
        cost(16 * seq * width * units, 24 * seq * width),
        prefetch=1,
        scratch=[pltpu.VMEM((tile, units), F32)],
    )(bits, *rows, *pres, *lives, *hiddens)


def head_weights_body(*refs):
    enc0, enc1, dkv0, dkv1, two, dq_ref, one, grad_two, cross_mixed = refs[:9]
    mixes = refs[9:13]
    keep_ref, give_ref, self_keep, self_give = refs[13:]
    local = mixes[0].shape[1]
    for r in range(4):
        out = (keep_ref, give_ref)[r % 2]
        columns = slice((r % 2) * local, (r % 2 + 1) * local)
        pair = slice(2 * r * local, 2 * (r + 1) * local)
        kv = dot(enc0[...], dkv0[:, pair], 0, 0) + dot(enc1[...], dkv1[:, pair], 0, 0)
        out[r // 2, :, : 2 * local] = kv.astype(BF16)
        query = dot(two[...], dq_ref[r // 2, :, columns], 0, 0)
        cross = dot(grad_two[...], cross_mixed[r // 2, :, columns], 0, 0)
        out[r // 2, :, 2 * local :] = jnp.concatenate((query, cross), axis=1).astype(BF16)
        (self_keep, self_give)[r % 2][r // 2] = dot(mixes[r][...], one[...], 0, 0).astype(BF16)


def head_weights(encs, dkvs, normed_two, dq, grad_one, grad_two, cross_mixed, mixes):
    seq, width = normed_two.shape
    local = mixes[0].shape[1]
    tile = width // 2
    rows = pl.BlockSpec((seq, tile), lambda i: (0, i))
    out = pl.BlockSpec((2, tile, width), lambda i: (0, i, 0))
    turned = pl.BlockSpec((2, local, tile), lambda i: (0, 0, i))
    frames = encs[0].shape[0] + encs[1].shape[0]
    return call(
        head_weights_body,
        (2,),
        [pl.BlockSpec((item.shape[0], tile), lambda i: (0, i)) for item in encs]
        + [whole(item.shape) for item in dkvs]
        + [rows, whole(dq.shape), rows, rows, whole(cross_mixed.shape)]
        + [whole(item.shape) for item in mixes],
        [out, out, turned, turned],
        [shape((2, width, width))] * 2 + [shape((2, local, width))] * 2,
        "head_weight_grads",
        cost(4 * frames * width * width + 6 * seq * width * width, 6 * frames * width),
    )(*encs, *dkvs, normed_two, dq, grad_one, grad_two, cross_mixed, *mixes)


def self_weights_body(bits, near, far, dnear, dfar, own, core, other, keep_ref, give_ref, scratch):
    totals = []
    for i in range(3):
        total = 0.0
        for c in range(2):
            total = total + dot(near[c], dnear[c, i], 0, 0) + dot(far[c], dfar[c, i], 0, 0)
        totals.append(total)
    totals.append((own[0].astype(F32) + core[0].astype(F32) + other[...].astype(F32)).T)
    split_store(jnp.concatenate(totals, axis=1), bits[0], keep_ref, give_ref, scratch)


def self_weights(bits, near, far, dnear, dfar, own, core, other, wide):
    _, seq, width = near.shape
    local = dnear.shape[3]
    tile = width // 2
    depth = width // wide
    rows = pl.BlockSpec((2, seq, tile), lambda i, *_: (0, 0, i))
    turned = pl.BlockSpec((1, local, tile), lambda i, *_: (0, 0, i))
    out = pl.BlockSpec((wide // 4, depth, 4 * local), lambda i, *_: (i, 0, 0))
    return call(
        self_weights_body,
        (2,),
        [rows, rows, whole(dnear.shape), whole(dfar.shape), turned, turned]
        + [pl.BlockSpec((local, tile), lambda i, *_: (0, i))],
        [out, out],
        [shape((wide // 2, depth, 4 * local))] * 2,
        "self_weight_grads",
        cost(24 * seq * width * local, 16 * seq * width),
        prefetch=1,
        scratch=[pltpu.VMEM((tile, 4 * local), F32)],
    )(bits, near, far, dnear, dfar, own, core, other)


def merge_body(bits, keep_in, got_in, keep_out, give_out, *, which):
    mine = bits[which] if which >= 0 else 0
    keep_out[:, 0] = (keep_in[:, mine].astype(F32) + got_in[:, mine].astype(F32)).astype(BF16)
    give_out[:, 0] = (keep_in[:, 1 - mine].astype(F32) + got_in[:, 1 - mine].astype(F32)).astype(BF16)


def merge(bits, keep, got, which):
    groups, _, rows, columns = keep.shape
    tile = rows // 2 if rows % 32 == 0 else rows
    both = pl.BlockSpec((groups, 2, tile, columns), lambda i, *_: (0, 0, i, 0))
    out = pl.BlockSpec((groups, 1, tile, columns), lambda i, *_: (0, 0, i, 0))
    return call(
        functools.partial(merge_body, which=which),
        (rows // tile,),
        [both, both],
        [out, out],
        [shape((groups, 1, rows, columns))] * 2,
        "merge",
        cost(0, 12 * groups * rows * columns),
        prefetch=1,
    )(bits, keep, got)


def scatter_wide(bits, then, keep, give, which, got):
    dims = keep.shape[-2:]
    parts = lax.axis_size("wide") >> which
    lead = keep.size // (parts * dims[0] * dims[1])
    while parts > 1:
        parts //= 2
        view = (lead * parts, 2) + dims
        keep, give = merge(then(bits), keep.reshape(view), got.reshape(view), which)
        then.last = keep
        which += 1
        got = swap(give, "wide", 1 << (which - 1))
    view = (lead,) + dims
    return keep.reshape(view).astype(F32) + got.reshape(view).astype(F32)


def place_body(order, a, b, c, d, *refs, start):
    out, held, reads, writes = refs[-4:]
    blocks = (a, b, c, d)
    loads = [pltpu.make_async_copy(item, held.at[r], reads.at[r]) for r, item in enumerate(blocks)]
    for item in loads:
        item.start()
    stores = []
    for r, item in enumerate(loads):
        item.wait()
        if start is None:
            target = out.at[order[r]]
        else:
            target = out.at[:, order[r], pl.ds(start, held.shape[2])]
        stores.append(pltpu.make_async_copy(held.at[r], target, writes.at[r]))
        stores[-1].start()
    for item in stores:
        item.wait()


def place_blocks(order, blocks, dims, start=None, before=None):
    anywhere = pl.BlockSpec(memory_space=pl.ANY)
    extra = () if before is None else (before,)
    return pl.pallas_call(
        functools.partial(place_body, start=start),
        grid_spec=pltpu.PrefetchScalarGridSpec(
            num_scalar_prefetch=1,
            grid=(1,),
            in_specs=[anywhere] * (4 + len(extra)),
            out_specs=anywhere,
            scratch_shapes=[
                pltpu.VMEM((4,) + blocks[0].shape, BF16),
                pltpu.SemaphoreType.DMA((4,)),
                pltpu.SemaphoreType.DMA((4,)),
            ],
        ),
        out_shape=shape(dims),
        input_output_aliases={5: 0} if extra else {},
        compiler_params=pltpu.CompilerParams(vmem_limit_bytes=VMEM_LIMIT),
        cost_estimate=cost(0, 16 * blocks[0].size),
        name="place_blocks",
    )(order, *blocks, *extra)


def on_device(
    tokens, lengths, memory, gains, self_qkv, self_out, cross_q, cross_kv, cross_out, fc_in, fc_out, out_grad
):
    clips, seq, width = tokens.shape
    wide = lax.axis_size("wide")
    narrow = lax.axis_size("narrow")
    me = lax.axis_index("narrow")
    place = lax.axis_index("wide")
    bits = ((place >> jnp.arange(8)) & 1).astype(jnp.int32)
    share = memory.shape[1]
    local = self_qkv.shape[2]
    depth = width // wide
    order = (me ^ jnp.arange(4)).astype(jnp.int32)
    near_order = (me ^ jnp.array([1, 0])).astype(jnp.int32)
    far_order = (me ^ jnp.array([3, 2])).astype(jnp.int32)
    gain_row = [gains[i : i + 1] for i in range(4)]
    then = Order()

    by_clip = memory.reshape(wide, narrow, share, width)
    sizes = (-(-share // 32) * 16, share - -(-share // 32) * 16)
    starts = (0, sizes[0])
    last = AUDIO - (wide - 1) * share
    valid = [(wide - 1) * size + min(max(last - start, 0), size) for start, size in zip(starts, sizes)]

    def encoder_rows(part, *named):
        block = encode(then(order, *named), by_clip, gain_row[0], starts[part], sizes[part])
        then.last = block
        block = lax.all_to_all(block, "wide", 0, 0, tiled=True)
        return block.reshape(wide * sizes[part], width)

    encoded_first = encoder_rows(0)
    self_qkv = self_qkv.transpose(0, 2, 1)
    pack_kv = cross_kv.transpose(0, 2, 1).reshape(2 * local, width)
    packs_one = gather_narrow(jnp.concatenate((self_out, then(cross_q).T)))

    normed_far, qkv_far, mixed_three, mixed_two, lse_far = self_fwd(
        then(far_order), lengths, tokens, gain_row[1], self_qkv
    )
    then.last = mixed_two
    mix_two = swap(mixed_two, "narrow", 2)
    crossing = swap(mixed_three, "narrow", 1)
    normed_near, qkv_near, mixed_one, mixed_zero, lse_near = self_fwd(
        then(near_order), lengths, tokens, gain_row[1], self_qkv
    )
    then.last = mixed_zero
    mix_three = swap(then(crossing), "narrow", 2)
    packs_kv = gather_narrow(then(pack_kv))
    mixes = [mixed_zero, swap(mixed_one, "narrow", 1), mix_two, mix_three]
    packs_one = finish(packs_one, then)
    encoded_second = encoder_rows(1, mix_two, packs_one[2])
    encoded = (encoded_first, encoded_second)
    after_self, normed_two, query = to_query(then(order), tokens, mixes, packs_one, gain_row[2])
    then.last = query
    packs_kv = finish(packs_kv, then)
    packs_out = gather_narrow(then(cross_out))
    kv_first, *before = cross_first(then(query), encoded_first, packs_kv, valid[0])
    then.last = kv_first
    packs_out = finish(packs_out, then)
    kv_second, cross_mixed, cross_lse, after_cross, normed_three = cross_second(
        query, encoded_second, packs_kv, packs_out, valid[1], before, after_self, gain_row[3]
    )
    then.last = normed_three

    rows = gather_narrow(normed_three)
    hidden_a, pre_a, live_a, part_zero, feed_zero, part_one, feed_one = feed_forward(
        order[:2], lengths, rows[:2], out_grad, fc_in, fc_out
    )
    then.last = part_one
    rows = finish(rows, then)
    part_near = swap(part_one, "narrow", 1)
    feed_near = swap(feed_one, "narrow", 1)
    hidden_c, pre_c, live_c, part_three, feed_three = feed_forward(
        order[3:], lengths, rows[3:], out_grad, fc_in, fc_out
    )
    then.last = part_three
    part_cross = swap(part_three, "narrow", 1)
    feed_cross = swap(feed_three, "narrow", 1)
    hidden_b, pre_b, live_b, part_two, feed_two = feed_forward(
        then(order[2:3]), lengths, rows[2:3], out_grad, fc_in, fc_out
    )
    part_far = (part_two.astype(F32) + part_cross.astype(F32)).astype(BF16)
    then.last = part_far
    part_far = swap(part_far, "narrow", 2)
    feed_keep, feed_give = feed_weights(
        then(bits, part_near, feed_near, feed_cross),
        rows, (pre_a, pre_b, pre_c), (live_a, live_b, live_c), (hidden_a, hidden_b, hidden_c), wide,
    )
    then.last = feed_give
    feed_far = (then(feed_two).astype(F32) + feed_cross.astype(F32)).astype(BF16)
    then.last = feed_far
    feed_far = swap(then(feed_far, part_far), "narrow", 2)
    feed_got = swap(feed_give, "wide", 1)

    grad_cross, grad_two, grad_mixed, gain_three, dq, dkv_first, frames_first = cross_first_back(
        then(order), lengths, out_grad, (part_zero, part_near, part_far), after_cross, gain_row[3],
        packs_kv, packs_out, query, kv_first, cross_mixed, cross_lse, valid[0],
    )
    then.last = dkv_first

    def frames_sent(block, part):
        block = block.reshape(wide, sizes[part], width)
        return lax.all_to_all(block, "wide", 0, 0, tiled=True)

    frames_first = frames_sent(frames_first, 0)
    block_own = (
        then(after_cross) + (feed_zero.astype(F32) + feed_near.astype(F32) + feed_far.astype(F32))
    ).astype(BF16)
    then.last = block_own
    block_all = gather_narrow(block_own)
    view = (2 * (wide // 4), 2, depth, width)
    feed_keep, feed_give = merge(then(bits), feed_keep.reshape(view), feed_got.reshape(view), 1)
    then.last = feed_keep
    feed_got = swap(feed_give, "wide", 2)
    dq, dkv_second, frames_second, grad_self, grad_one, head0, head1, head2, head3, gain_two = cross_second_back(
        query, kv_second, grad_mixed, cross_mixed, cross_lse, dq, packs_kv, packs_one, after_self,
        then(gain_row[2]), grad_cross, valid[1],
    )
    then.last = dq
    heads_one = swap(head1, "narrow", 1)
    heads_two = swap(head2, "narrow", 2)
    head3 = swap(head3, "narrow", 2)
    frames_second = frames_sent(frames_second, 1)
    block_all = finish(block_all, then)

    back_first, gain_first = memory_back(then(order), by_clip, gain_row[0], frames_first, starts[0])
    then.last = back_first
    dqkv_near, part_one, part_zero = self_bwd(
        then(near_order, heads_two, head3), lengths, qkv_near, mixed_one, mixed_zero, lse_near, heads_one, head0,
        self_qkv,
    )
    then.last = part_one
    heads_three = swap(then(head3), "narrow", 1)
    back_first = gather_narrow(back_first)
    part_near = swap(part_one, "narrow", 1)
    feed_grads = scatter_wide(bits, then, feed_keep, feed_give, 2, feed_got)
    dqkv_far, part_three, part_two = self_bwd(
        then(far_order), lengths, qkv_far, mixed_three, mixed_two, lse_far, heads_three, heads_two, self_qkv
    )
    then.last = part_three
    part_cross = swap(part_three, "narrow", 1)
    block_out = place_blocks(then(order), block_all, (clips, seq, width))
    then.last = block_out
    part_far = (then(part_two).astype(F32) + part_cross.astype(F32)).astype(BF16)
    then.last = part_far
    part_far = swap(part_far, "narrow", 2)
    keep, give, self_keep, self_give = head_weights(
        encoded, (dkv_first, dkv_second), then(normed_two), dq, grad_one, grad_two, cross_mixed, mixes
    )
    then.last = keep
    got = swap(give, "narrow", 1)
    self_got = swap(self_give, "narrow", 1)
    back_second, gain_second = memory_back(then(order), by_clip, gain_row[0], frames_second, starts[1])
    then.last = back_second
    self_other = (self_keep[1].astype(F32) + self_got[1].astype(F32)).astype(BF16)
    then.last = self_other
    self_other = swap(self_other, "narrow", 2)
    view = (wide, 2, depth, width)
    keep, give = merge(then(bits), keep.reshape(view), got.reshape(view), 0)
    then.last = keep
    got = swap(give, "wide", 1)
    tokens_own, gain_one = to_tokens_grad(
        then(order), tokens, part_zero, part_near, part_far, grad_self, gain_row[1]
    )
    then.last = tokens_own
    tokens_all = gather_narrow(tokens_own)
    self_keep, self_give = self_weights(
        then(bits), normed_near, normed_far, dqkv_near, dqkv_far, self_keep, self_got, self_other, wide
    )
    then.last = self_keep
    self_got = swap(self_give, "wide", 1)
    back_second = gather_narrow(back_second)
    back_first = finish(back_first, then)
    view = (2 * (wide // 4), 2, depth, width)
    keep, give = merge(then(bits), keep.reshape(view), got.reshape(view), 1)
    then.last = keep
    got = swap(give, "wide", 2)
    memory_grad = place_blocks(then(order), back_first, (wide, narrow, share, width), starts[0])
    then.last = memory_grad
    view = (wide // 4, 2, depth, width)
    self_keep, self_give = merge(then(bits), self_keep.reshape(view), self_got.reshape(view), 1)
    then.last = self_keep
    self_got = swap(self_give, "wide", 2)
    tokens_all = finish(tokens_all, then)
    keep = scatter_wide(bits, then, keep, give, 2, got).astype(BF16)
    then.last = keep
    other = swap(keep[1], "narrow", 2)
    tokens_grad = place_blocks(then(order), tokens_all, (clips, seq, width))
    then.last = tokens_grad
    self_grads = scatter_wide(bits, then, self_keep, self_give, 2, self_got)[0]
    back_second = finish(back_second, then)
    head_grads = keep[0].astype(F32) + other.astype(F32)
    memory_grad = place_blocks(
        then(order), back_second, (wide, narrow, share, width), starts[1], memory_grad
    ).reshape(memory.shape)

    gain_terms = jnp.concatenate((gain_first + gain_second, gain_one, gain_two, gain_three))
    gain_terms = gain_terms + swap(gain_terms, "narrow", 1)
    gain_terms = gain_terms + swap(gain_terms, "narrow", 2)
    gain_terms = gain_terms.reshape(4, wide, depth).transpose(1, 0, 2)
    gains_grad = jnp.sum(lax.all_to_all(gain_terms, "wide", 0, 0, tiled=True), axis=0)

    heads = lambda i: head_grads[:, i * local : (i + 1) * local]
    own = lambda i: self_grads[:, i * local : (i + 1) * local]
    return (
        block_out,
        tokens_grad,
        memory_grad,
        gains_grad,
        jnp.stack([own(i) for i in range(3)]),
        own(3).T,
        heads(2),
        jnp.stack((heads(0), heads(1))),
        heads(3).T,
        feed_grads[0],
        feed_grads[1].T,
    )


def solution(mesh):
    placed = (
        P("wide", None, None),
        P("wide"),
        P(None, "wide", None),
        P(),
        P(None, None, "narrow"),
        P("narrow", None),
        P(None, "narrow"),
        P(None, None, "narrow"),
        P("narrow", None),
        P(None, "narrow"),
        P("narrow", None),
        P("wide", None, None),
    )
    return jax.shard_map(
        on_device,
        mesh=mesh,
        in_specs=placed,
        out_specs=(
            P("wide", None, None),
            P("wide", None, None),
            P(None, "wide", None),
            P(None, "wide"),
            P(None, "wide", "narrow"),
            P("narrow", "wide"),
            P("wide", "narrow"),
            P(None, "wide", "narrow"),
            P("narrow", "wide"),
            P("wide", "narrow"),
            P("narrow", "wide"),
        ),
        check_vma=False,
    )
```

time: 751 us -> 445 us (0.59)
  Pallas kernels: 0 us -> 238 us
  matrix products: 216 us -> 0 us
  other arithmetic: 153 us -> 11.8 us
  local copies, waits for them, and re-layouts: 142 us -> 22.5 us
  waiting for transfers between devices: 192 us -> 99.2 us
  starting transfers between devices: 35.2 us -> 65.7 us
    pallas_call x0 -> x31, Pallas kernels: none -> 238 us  [the longest x1 25.1 us: cross_second_back(): call(functools.partial(cross_second_back_body, valid=valid), (2,), [head_...]
    dot_general x42 -> x0, matrix products: 216 us -> none  [the longest x30 95.8 us: dot(): lax.dot_general(left, right, (((left_dim,), (right_dim,)), ((), ())), pre...]
    ppermute x41 -> x56, waiting for transfers between devices: 192 us -> 99.2 us  [swap(): return lax.ppermute(values, axis, [(i, i ^ bit) for i in range(size)])]
    convert_element_type x17 -> x6, other arithmetic: 63.6 us -> 6.28 us  [the longest x1 1.8 us: on_device(): block_own = (then(after_cross) + (feed_zero.astype(F32) + feed_near.astyp...]
    reduce_sum x11 -> x1, other arithmetic: 35.5 us -> 0.6 us  [on_device(): jnp.sum(lax.all_to_all(gain_terms, 'wide', 0, 0, tiled=True), axis=0)]
    unnamed x248 -> x110, local copies, waits for them, and re-layouts: 52.6 us -> 18 us
    convert_element_type x26 -> x0, local copies, waits for them, and re-layouts: 31.5 us -> none  [the longest x15 16.6 us: on_device(): p.astype(BF16)]
    another operation x16 -> x2, other arithmetic: 27.1 us -> 1.42 us  [the longest x1 0.73 us: on_device(): jnp.stack([own(i) for i in range(3)])]
  transfers between devices with their start and end apart: 43 -> 61, of which waited for: 14 -> 19; matrix products, arithmetic and copies ran while one was open for 37% -> 3% of each run, Pallas kernels for 0% -> 44%
where the time goes in v2:
time: 445 us; the launch traced here: 439 us
  Pallas kernels  238 us (53%)
  waiting for transfers between devices  99.2 us (22%)
  starting transfers between devices  65.7 us (15%)
  local copies, waits for them, and re-layouts  22.5 us (5%)
  other arithmetic  11.8 us (3%)
    ppermute x56, waiting for transfers between devices, swap(): return lax.ppermute(values, axis, [(i, i ^ bit) for i in range(size)])  99.2 us
    ppermute x56, starting transfers between devices, swap(): return lax.ppermute(values, axis, [(i, i ^ bit) for i in range(size)])  36.3 us
    pallas_call x1, Pallas kernels, cross_second_back(): call(functools.partial(cross_second_back_body, valid=valid), (2,), [head_...  25.1 us
    pallas_call x1, Pallas kernels, cross_first_back(): call(functools.partial(cross_first_back_body, valid=valid), (2,), [pl.Blo...  24.4 us
    pallas_call x3, Pallas kernels, feed_forward(): call(functools.partial(feed_body, count=count), (count, tiles), single +...  23.6 us
    pallas_call x7, Pallas kernels, merge(): call(functools.partial(merge_body, which=which), (rows // tile,), [both,...  21.6 us
    pallas_call x1, Pallas kernels, cross_second(): call(functools.partial(cross_second_body, valid=valid), (2,), [rows, whol...  18.8 us
    pallas_call x2, Pallas kernels, self_bwd(): call(self_bwd_body, (2,), [pl.BlockSpec((1, 3, seq, local), lambda i, *_:...  18.3 us
  transfers between devices with their start and end apart: 61, of which 19 were waited for; matrix products, arithmetic and copies ran while one was open for 3% of the time, Pallas kernels for 44%

profile of v2, /device:TPU:0, one launch (start us, length us, event | category | flops | bytes accessed | tf_op | source)
XLA Modules:
  0.0 438.8 jit_solution(11999776841165416156)
XLA Ops:
  6.0 7.4 %all-to-all-start.1 = ((bf16[8,96,768]{2,1,0:T(8,128)(2,1)}), bf16[8,96,768]{2,1,0:T(8,128)(2,1)S(1)}, u32[]{:S(2)}, u32[]{:S(2)}) async-start(bf16[8,96,768]{2,1,0:T(8,128)(2,1)} %encode.2), calls=%async_computation.1 | async-start | bytes 2359296 | tf_op jit(solution)/shard_map/all_to_all | solution.py:970
  15.6 8.9 %self_forward.2 = (bf16[2,448,768]{2,1,0:T(8,128)(2,1)}, bf16[2,3,448,192]{3,2,1,0:T(8,128)(2,1)}, bf16[448,192]{1,0:T(8,128)(2,1)}, bf16[448,192]{1,0:T(8,128)(2,1)}, f32[2,3,448]{2,1,0:T(4,128)}) custom-call(s32[2]{0:T(128)} %get-tuple-element.219.order, s32[4]{0:T(128)} %lengths.15, bf16[4,448,768]{2,1,0:T(8,128)(2,1)} %token_ref.7, ...), custom_call_target="tpu_custom_call" | custom-call | flops 1409286144 | bytes 5505024 | tf_op jit(solution)/shard_map/self_forward/pallas_call | solution.py:199
  24.6 9.1 %self_forward.3 = (bf16[2,448,768]{2,1,0:T(8,128)(2,1)}, bf16[2,3,448,192]{3,2,1,0:T(8,128)(2,1)}, bf16[448,192]{1,0:T(8,128)(2,1)}, bf16[448,192]{1,0:T(8,128)(2,1)}, f32[2,3,448]{2,1,0:T(4,128)}) custom-call(s32[2]{0:T(128)} %get-tuple-element.210.order, s32[4]{0:T(128)} %lengths.15, bf16[4,448,768]{2,1,0:T(8,128)(2,1)} %token_ref.7, ...), custom_call_target="tpu_custom_call" | custom-call | flops 1409286144 | bytes 5505024 | tf_op jit(solution)/shard_map/self_forward/pallas_call | solution.py:199
  36.2 6.4 %collective-permute-done.m2.refs_11_ = bf16[448,192]{1,0:T(8,128)(2,1)S(1)} collective-permute-done((bf16[448,192]{1,0:T(8,128)(2,1)S(1)}, bf16[448,192]{1,0:T(8,128)(2,1)S(1)}, u32[]{:S(2)}, u32[]{:S(2)}) %collective-permute-start) | collective-permute-done | bytes 172064 | tf_op jit(solution)/shard_map/ppermute | solution.py:75
  46.0 6.3 %all-to-all-start = ((bf16[8,96,768]{2,1,0:T(8,128)(2,1)}), bf16[8,96,768]{2,1,0:T(8,128)(2,1)S(1)}, u32[]{:S(2)}, u32[]{:S(2)}) async-start(bf16[8,96,768]{2,1,0:T(8,128)(2,1)} %encode.3), calls=%async_computation | async-start | bytes 2359296 | tf_op jit(solution)/shard_map/all_to_all | solution.py:970
  54.7 7.1 %collective-permute-done.4.m3.refs_12_ = bf16[448,192]{1,0:T(8,128)(2,1)S(1)} collective-permute-done((bf16[448,192]{1,0:T(8,128)(2,1)S(1)}, bf16[448,192]{1,0:T(8,128)(2,1)S(1)}, u32[]{:S(2)}, u32[]{:S(2)}) %collective-permute-start.4) | collective-permute-done | bytes 172064 | tf_op jit(solution)/shard_map/ppermute | solution.py:75
  62.5 6.9 %self_out_to_query.1 = (f32[448,768]{1,0:T(8,128)}, bf16[448,768]{1,0:T(8,128)(2,1)}, bf16[2,448,384]{2,1,0:T(8,128)(2,1)}) custom-call(s32[4]{0:T(128)} %iota_xor_fusion.order, bf16[4,448,768]{2,1,0:T(8,128)(2,1)} %token_ref.7, bf16[448,192]{1,0:T(8,128)(2,1)} %get-tuple-element.148.m0.mixed1_ref.refs_9_, bf16[448,192]{1,0:T(8,128)(2,1)} %copy-done.31, ...), custom_call_target="tpu_custom_call" | custom-call | flops 1056964608 | bytes 6488064 | tf_op jit(solution)/shard_map/self_out_to_query/pallas_call | solution.py:326
  72.5 14.1 %cross_first.1 = (bf16[768,1536]{1,0:T(8,128)(2,1)}, f32[2,384,448]{2,1,0:T(8,128)}, f32[2,6,448]{2,1,0:T(8,128)}, f32[2,6,448]{2,1,0:T(8,128)}) custom-call(bf16[2,448,384]{2,1,0:T(8,128)(2,1)} %get-tuple-element.158.query_ref, bf16[768,768]{1,0:T(8,128)(2,1)} %bitcast.70, bf16[384,768]{1,0:T(8,128)(2,1)} %bitcast.5.w0, bf16[384,768]{1,0:T(8,128)(2,1)} %copy-done.45, ...), custom_call_target="tpu_custom_call" | custom-call | flops 7096762368 | bytes 4718592 | tf_op jit(solution)/shard_map/cross_first/pallas_call | solution.py:430
  89.5 18.8 %cross_second.1 = (bf16[768,1536]{1,0:T(8,128)(2,1)}, bf16[2,448,384]{2,1,0:T(8,128)(2,1)}, f32[2,6,448]{2,1,0:T(8,128)}, f32[448,768]{1,0:T(8,128)}, bf16[448,768]{1,0:T(8,128)(2,1)}) custom-call(bf16[2,448,384]{2,1,0:T(8,128)(2,1)} %get-tuple-element.158.query_ref, bf16[768,768]{1,0:T(8,128)(2,1)} %bitcast.72, bf16[384,768]{1,0:T(8,128)(2,1)} %bitcast.5.w0, ...), custom_call_target="tpu_custom_call" | custom-call | flops 7096762368 | bytes 5898240 | tf_op jit(solution)/shard_map/cross_second/pallas_call | solution.py:458
  111.5 10.2 %feed_forward.3 = (bf16[2,448,768]{2,1,0:T(8,128)(2,1)}, bf16[2,448,768]{2,1,0:T(8,128)(2,1)}, bf16[2,448,768]{2,1,0:T(8,128)(2,1)}, bf16[448,768]{1,0:T(8,128)(...) custom-call(s32[2]{0:T(128)} %bitcast.84, s32[4]{0:T(128)} %lengths.15, ...), custom_call_target="tpu_custom_call" | custom-call | flops 4227858432 | bytes 9633792 | tf_op jit(solution)/shard_map/feed_forward/pallas_call | solution.py:520
  129.4 6.7 %feed_forward.4 = (bf16[1,448,768]{2,1,0:T(8,128)(2,1)}, bf16[1,448,768]{2,1,0:T(8,128)(2,1)}, bf16[1,448,768]{2,1,0:T(8,128)(2,1)}, bf16[448,768]{1,0:T(8,128)(2,1)}, bf16[448,768]{1,0:T(8,128)(2,1)}) custom-call(s32[1]{0:T(128)} %get-tuple-element.314.order, s32[4]{0:T(128)} %lengths.15, bf16[448,768]{1,0:T(8,128)(2,1)} %copy-done.43, ...), custom_call_target="tpu_custom_call" | custom-call | flops 2113929216 | bytes 4816896 | tf_op jit(solution)/shard_map/feed_forward/pallas_call | solution.py:520
  137.2 6.7 %feed_forward.5 = (bf16[1,448,768]{2,1,0:T(8,128)(2,1)}, bf16[1,448,768]{2,1,0:T(8,128)(2,1)}, bf16[1,448,768]{2,1,0:T(8,128)(2,1)}, bf16[448,768]{1,0:T(8,128)(2,1)}, bf16[448,768]{1,0:T(8,128)(2,1)}) custom-call(s32[1]{0:T(128)} %get-tuple-element.171.order, s32[4]{0:T(128)} %lengths.15, bf16[448,768]{1,0:T(8,128)(2,1)} %copy-done.42, ...), custom_call_target="tpu_custom_call" | custom-call | flops 2113929216 | bytes 4816896 | tf_op jit(solution)/shard_map/feed_forward/pallas_call | solution.py:520
  146.4 11.3 %feed_weight_grads.1 = (bf16[2,4,96,768]{3,2,1,0:T(8,128)(2,1)}, bf16[2,4,96,768]{3,2,1,0:T(8,128)(2,1)}) custom-call(s32[8]{0:T(128)} %shift-right-arithmetic_and_fusion.bits, bf16[448,768]{1,0:T(8,128)(2,1)} %get-tuple-element.167.refs_0_, bf16[448,768]{1,0:T(8,128)(2,1)} %copy-done.40, bf16[448,768]{1,0:T(8,128)(2,1)} %copy-done.42, ...), custom_call_target="tpu_custom_call" | custom-call | flops 4227858432 | bytes 8257536 | tf_op jit(solution)/shard_map/feed_weight_grads/pallas_call | solution.py:776
  163.6 24.4 %cross_first_back.1 = (f32[448,768]{1,0:T(8,128)}, bf16[448,768]{1,0:T(8,128)(2,1)}, bf16[2,448,384]{2,1,0:T(8,128)(2,1)}, f32[1,768]{1,0:T(1,128)}, f32[2,384,4...) custom-call(s32[4]{0:T(128)} %iota_xor_fusion.order, s32[4]{0:T(128)} %lengths.15, ...), custom_call_target="tpu_custom_call" | custom-call | flops 17666408448 | bytes 11796480 | tf_op jit(solution)/shard_map/cross_first_back/pallas_call | solution.py:616
  188.0 6.4 %all-to-all-start.2 = ((bf16[8,96,768]{2,1,0:T(8,128)(2,1)}), bf16[8,96,768]{2,1,0:T(8,128)(2,1)S(1)}, u32[]{:S(2)}, u32[]{:S(2)}) async-start(bf16[8,96,768]{2,1,0:T(8,128)(2,1)} %bitcast.75), calls=%async_computation.2 | async-start | bytes 2359296 | tf_op jit(solution)/shard_map/all_to_all | solution.py:1044
  203.6 25.1 %cross_second_back.1 = (bf16[2,448,384]{2,1,0:T(8,128)(2,1)}, bf16[768,1536]{1,0:T(8,128)(2,1)}, bf16[768,768]{1,0:T(8,128)(2,1)}, f32[448,768]{1,0:T(8,128)}, b...) custom-call(bf16[2,448,384]{2,1,0:T(8,128)(2,1)} %get-tuple-element., ...), custom_call_target="tpu_custom_call" | custom-call | flops 17666408448 | bytes 11796480 | tf_op jit(solution)/shard_map/cross_second_back/pallas_call | solution.py:688
  239.5 9.1 %self_backward.2 = (bf16[2,3,448,192]{3,2,1,0:T(8,128)(2,1)}, bf16[448,768]{1,0:T(8,128)(2,1)}, bf16[448,768]{1,0:T(8,128)(2,1)}) custom-call(s32[2]{0:T(128)} %get-tuple-element.210.order, s32[4]{0:T(128)} %lengths.15, bf16[2,3,448,192]{3,2,1,0:T(8,128)(2,1)} %get-tuple-element.211.qkv_ref, bf16[448,192]{1,0:T(8,128)(2,1)} %get-tuple-element.151.mixed0_ref, ...), custom_call_target="tpu_custom_call" | custom-call | flops 2334130176 | bytes 5505024 | tf_op jit(solution)/shard_map/self_backward/pallas_call | solution.py:284
  253.7 9.1 %self_backward.3 = (bf16[2,3,448,192]{3,2,1,0:T(8,128)(2,1)}, bf16[448,768]{1,0:T(8,128)(2,1)}, bf16[448,768]{1,0:T(8,128)(2,1)}) custom-call(s32[2]{0:T(128)} %get-tuple-element.219.order, s32[4]{0:T(128)} %lengths.15, bf16[2,3,448,192]{3,2,1,0:T(8,128)(2,1)} %get-tuple-element.220.qkv_ref, bf16[448,192]{1,0:T(8,128)(2,1)} %get-tuple-element.152.mixed0_ref, ...), custom_call_target="tpu_custom_call" | custom-call | flops 2334130176 | bytes 5505024 | tf_op jit(solution)/shard_map/self_backward/pallas_call | solution.py:284
  269.3 13.3 %head_weight_grads.1 = (bf16[2,768,768]{2,1,0:T(8,128)(2,1)}, bf16[2,768,768]{2,1,0:T(8,128)(2,1)}, bf16[2,192,768]{2,1,0:T(8,128)(2,1)}, bf16[2,192,768]{2,1,0:T(8,128)(2,1)}) custom-call(bf16[768,768]{1,0:T(8,128)(2,1)} %bitcast.71, bf16[768,768]{1,0:T(8,128)(2,1)} %bitcast.73, bf16[768,1536]{1,0:T(8,128)(2,1)} %get-tuple-element.195.refs_2_, ...), custom_call_target="tpu_custom_call" | custom-call | flops 5209325568 | bytes 7077888 | tf_op jit(solution)/shard_map/head_weight_grads/pallas_call | solution.py:815
  298.3 28.7 %collective-permute-done.35.far_ref = bf16[448,768]{1,0:T(8,128)(2,1)S(1)} collective-permute-done((bf16[448,768]{1,0:T(8,128)(2,1)}, bf16[448,768]{1,0:T(8,128)(2,1)S(1)}, u32[]{:S(2)}, u32[]{:S(2)}) %collective-permute-start.35) | collective-permute-done | bytes 688160 | tf_op jit(solution)/shard_map/ppermute | solution.py:75
  333.3 7.1 %self_weight_grads.1 = (bf16[4,96,768]{2,1,0:T(8,128)(2,1)}, bf16[4,96,768]{2,1,0:T(8,128)(2,1)}) custom-call(s32[8]{0:T(128)} %shift-right-arithmetic_and_fusion.bits, bf16[2,448,768]{2,1,0:T(8,128)(2,1)} %get-tuple-element.244.near, bf16[2,448,768]{2,1,0:T(8,128)(2,1)} %get-tuple-element.245.far, bf16[2,3,448,192]{3,2,1,0:T(8,128)(2,1)} %get-tuple-element.246.dnear, ...), custom_call_target="tpu_custom_call" | custom-call | flops 1585446912 | bytes 5505024 | tf_op jit(solution)/shard_map/self_weight_grads/pallas_call | solution.py:848
  353.3 16.3 %collective-permute-done.39 = bf16[8,1,96,768]{3,2,1,0:T(8,128)(2,1)} collective-permute-done((bf16[8,1,96,768]{3,2,1,0:T(8,128)(2,1)}, bf16[8,1,96,768]{3,2,1,0:T(8,128)(2,1)}, u32[]{:S(2)}, u32[]{:S(2)}) %collective-permute-start.39) | collective-permute-done | bytes 1179680 | tf_op jit(solution)/shard_map/ppermute | solution.py:75
  396.5 5.4 %collective-permute-done.52 = bf16[4,1,96,768]{3,2,1,0:T(8,128)(2,1)S(1)} collective-permute-done((bf16[4,1,96,768]{3,2,1,0:T(8,128)(2,1)}, bf16[4,1,96,768]{3,2,1,0:T(8,128)(2,1)S(1)}, u32[]{:S(2)}, u32[]{:S(2)}) %collective-permute-start.52) | collective-permute-done | bytes 589856 | tf_op jit(solution)/shard_map/ppermute | solution.py:75
  417.1 8.6 %collective-permute-done.51 = bf16[1,1,96,768]{3,2,1,0:T(8,128)(2,1)} collective-permute-done((bf16[1,1,96,768]{3,2,1,0:T(8,128)(2,1)}, bf16[1,1,96,768]{3,2,1,0:T(8,128)(2,1)}, u32[]{:S(2)}, u32[]{:S(2)}) %collective-permute-start.51) | collective-permute-done | bytes 147488 | tf_op jit(solution)/shard_map/ppermute | solution.py:75
  (267 shorter events, 163.7 us)
Async XLA Ops:
  6.0 40.0 %all-to-all-start.1 = ((bf16[8,96,768]{2,1,0:T(8,128)(2,1)}), bf16[8,96,768]{2,1,0:T(8,128)(2,1)S(1)}, u32[]{:S(2)}, u32[]{:S(2)}) async-start(bf16[8,96,768]{2,1,0:T(8,128)(2,1)} %encode.2), calls=%async_computation.1 | async-start | bytes 2359296 | tf_op jit(solution)/shard_map/all_to_all | solution.py:970
  15.0 46.8 %collective-permute-start.5 = (bf16[384,768]{1,0:T(8,128)(2,1)S(1)}, bf16[384,768]{1,0:T(8,128)(2,1)}, u32[]{:S(2)}, u32[]{:S(2)}) collective-permute-start(bf16[384,768]{1,0:T(8,128)(2,1)S(1)} %pad_maximum_fusion.p0), channel_id=1, source_target_pairs={{0,1},{1,0},{2,3},{3,2},{4,5},{5,4},{6,7},{7,6},{8,9},{9,8},{10,11... | collective-permute-start | bytes 1769480 | tf_op jit(solution)/shard_map/ppermute | solution.py:75
  33.7 28.1 %collective-permute-start.6 = (bf16[384,768]{1,0:T(8,128)(2,1)S(1)}, bf16[384,768]{1,0:T(8,128)(2,1)}, u32[]{:S(2)}, u32[]{:S(2)}) collective-permute-start(bf16[384,768]{1,0:T(8,128)(2,1)S(1)} %collective-permute-done.1.p2), channel_id=1, source_target_pairs={{0,1},{1,0},{2,3},{3,2},{4,5},{5,4},{6,7},{7,6},{8,9},{9,8},{10,11... | collective-permute-start | bytes 1769480 | tf_op jit(solution)/shard_map/ppermute | solution.py:75
  34.7 34.6 %collective-permute-start.8 = (bf16[384,768]{1,0:T(8,128)(2,1)}, bf16[384,768]{1,0:T(8,128)(2,1)}, u32[]{:S(2)}, u32[]{:S(2)}) collective-permute-start(bf16[384,768]{1,0:T(8,128)(2,1)} %bitcast.5.w0), channel_id=1, source_target_pairs={{0,2},{1,3},{2,0},{3,1},{4,6},{5,7},{6,4},{7,5},{8,10},{9,11},{10,... | collective-permute-start | bytes 1769480 | tf_op jit(solution)/shard_map/ppermute | solution.py:75
  46.0 42.2 %all-to-all-start = ((bf16[8,96,768]{2,1,0:T(8,128)(2,1)}), bf16[8,96,768]{2,1,0:T(8,128)(2,1)S(1)}, u32[]{:S(2)}, u32[]{:S(2)}) async-start(bf16[8,96,768]{2,1,0:T(8,128)(2,1)} %encode.3), calls=%async_computation | async-start | bytes 2359296 | tf_op jit(solution)/shard_map/all_to_all | solution.py:970
  157.7 40.6 %collective-permute-start.22 = (bf16[2,4,96,768]{3,2,1,0:T(8,128)(2,1)}, bf16[2,4,96,768]{3,2,1,0:T(8,128)(2,1)}, u32[]{:S(2)}, u32[]{:S(2)}) collective-permute-start(bf16[2,4,96,768]{3,2,1,0:T(8,128)(2,1)} %get-tuple-element.186), channel_id=1, source_target_pairs={{0,4},{4,0},{8,12},{12,8},{16,20},{20,16},{24,28},{28,24},{1,5},{5... | collective-permute-start | bytes 3538952 | tf_op jit(solution)/shard_map/ppermute | solution.py:75
  162.7 31.6 %collective-permute-start.21 = (bf16[448,768]{1,0:T(8,128)(2,1)}, bf16[448,768]{1,0:T(8,128)(2,1)S(1)}, u32[]{:S(2)}, u32[]{:S(2)}) collective-permute-start(bf16[448,768]{1,0:T(8,128)(2,1)} %add_convert_fusion.2), channel_id=1, source_target_pairs={{0,2},{1,3},{2,0},{3,1},{4,6},{5,7},{6,4},{7,5},{8,10},{9,11},{10,... | collective-permute-start | bytes 2064392 | tf_op jit(solution)/shard_map/ppermute | solution.py:75
  188.0 42.8 %all-to-all-start.2 = ((bf16[8,96,768]{2,1,0:T(8,128)(2,1)}), bf16[8,96,768]{2,1,0:T(8,128)(2,1)S(1)}, u32[]{:S(2)}, u32[]{:S(2)}) async-start(bf16[8,96,768]{2,1,0:T(8,128)(2,1)} %bitcast.75), calls=%async_computation.2 | async-start | bytes 2359296 | tf_op jit(solution)/shard_map/all_to_all | solution.py:1044
  197.1 52.2 %collective-permute-start.29 = (bf16[448,768]{1,0:T(8,128)(2,1)S(1)}, bf16[448,768]{1,0:T(8,128)(2,1)S(1)}, u32[]{:S(2)}, u32[]{:S(2)}) collective-permute-start(bf16[448,768]{1,0:T(8,128)(2,1)S(1)} %add_convert_fusion.1.a), channel_id=1, source_target_pairs={{0,2},{1,3},{2,0},{3,1},{4,6},{5,7},{6,4},{7,5},{8,10},{9,11},{10,... | collective-permute-start | bytes 2064392 | tf_op jit(solution)/shard_map/ppermute | solution.py:75
  201.5 47.8 %collective-permute-start.26 = (bf16[4,1,96,768]{3,2,1,0:T(8,128)(2,1)}, bf16[4,1,96,768]{3,2,1,0:T(8,128)(2,1)S(1)}, u32[]{:S(2)}, u32[]{:S(2)}) collective-permute-start(bf16[4,1,96,768]{3,2,1,0:T(8,128)(2,1)} %get-tuple-element.217), channel_id=1, source_target_pairs={{0,8},{4,12},{8,0},{12,4},{16,24},{20,28},{24,16},{28,20},{1,9},{5... | collective-permute-start | bytes 1769480 | tf_op jit(solution)/shard_map/ppermute | solution.py:75
  283.2 57.2 %collective-permute-start.41 = (bf16[8,96,768]{2,1,0:T(8,128)(2,1)}, bf16[8,96,768]{2,1,0:T(8,128)(2,1)}, u32[]{:S(2)}, u32[]{:S(2)}) collective-permute-start(bf16[8,96,768]{2,1,0:T(8,128)(2,1)} %get-tuple-element.209.a), channel_id=1, source_target_pairs={{0,2},{1,3},{2,0},{3,1},{4,6},{5,7},{6,4},{7,5},{8,10},{9,11},{10,... | collective-permute-start | bytes 3538952 | tf_op jit(solution)/shard_map/ppermute | solution.py:75
  284.4 59.5 %all-to-all-start.3 = ((bf16[8,96,768]{2,1,0:T(8,128)(2,1)}), bf16[8,96,768]{2,1,0:T(8,128)(2,1)S(1)}, u32[]{:S(2)}, u32[]{:S(2)}) async-start(bf16[8,96,768]{2,1,0:T(8,128)(2,1)} %bitcast.74), calls=%async_computation.3 | async-start | bytes 2359296 | tf_op jit(solution)/shard_map/all_to_all | solution.py:1044
  289.2 37.8 %collective-permute-start.35 = (bf16[448,768]{1,0:T(8,128)(2,1)}, bf16[448,768]{1,0:T(8,128)(2,1)S(1)}, u32[]{:S(2)}, u32[]{:S(2)}) collective-permute-start(bf16[448,768]{1,0:T(8,128)(2,1)} %add_convert_fusion), channel_id=1, source_target_pairs={{0,2},{1,3},{2,0},{3,1},{4,6},{5,7},{6,4},{7,5},{8,10},{9,11},{10,... | collective-permute-start | bytes 2064392 | tf_op jit(solution)/shard_map/ppermute | solution.py:75
  291.3 41.3 %collective-permute-start.38 = (bf16[192,768]{1,0:T(8,128)(2,1)S(1)}, bf16[192,768]{1,0:T(8,128)(2,1)S(1)}, u32[]{:S(2)}, u32[]{:S(2)}) collective-permute-start(bf16[192,768]{1,0:T(8,128)(2,1)S(1)} %fusion), channel_id=1, source_target_pairs={{0,2},{1,3},{2,0},{3,1},{4,6},{5,7},{6,4},{7,5},{8,10},{9,11},{10,... | collective-permute-start | bytes 884744 | tf_op jit(solution)/shard_map/ppermute | solution.py:75
  292.5 56.8 %collective-permute-start.40 = (bf16[8,96,768]{2,1,0:T(8,128)(2,1)}, bf16[8,96,768]{2,1,0:T(8,128)(2,1)}, u32[]{:S(2)}, u32[]{:S(2)}) collective-permute-start(bf16[8,96,768]{2,1,0:T(8,128)(2,1)} %get-tuple-element.209.a), channel_id=1, source_target_pairs={{0,1},{1,0},{2,3},{3,2},{4,5},{5,4},{6,7},{7,6},{8,9},{9,8},{10,11... | collective-permute-start | bytes 3538952 | tf_op jit(solution)/shard_map/ppermute | solution.py:75
  340.5 29.1 %collective-permute-start.39 = (bf16[8,1,96,768]{3,2,1,0:T(8,128)(2,1)}, bf16[8,1,96,768]{3,2,1,0:T(8,128)(2,1)}, u32[]{:S(2)}, u32[]{:S(2)}) collective-permute-start(bf16[8,1,96,768]{3,2,1,0:T(8,128)(2,1)} %get-tuple-element.250), channel_id=1, source_target_pairs={{0,4},{4,0},{8,12},{12,8},{16,20},{20,16},{24,28},{28,24},{1,5},{5... | collective-permute-start | bytes 3538952 | tf_op jit(solution)/shard_map/ppermute | solution.py:75
  342.0 43.2 %collective-permute-start.37 = (bf16[448,768]{1,0:T(8,128)(2,1)}, bf16[448,768]{1,0:T(8,128)(2,1)}, u32[]{:S(2)}, u32[]{:S(2)}) collective-permute-start(bf16[448,768]{1,0:T(8,128)(2,1)} %get-tuple-element.242.a), channel_id=1, source_target_pairs={{0,2},{1,3},{2,0},{3,1},{4,6},{5,7},{6,4},{7,5},{8,10},{9,11},{10,... | collective-permute-start | bytes 2064392 | tf_op jit(solution)/shard_map/ppermute | solution.py:75
  343.2 38.5 %collective-permute-start.43 = (bf16[4,96,768]{2,1,0:T(8,128)(2,1)}, bf16[4,96,768]{2,1,0:T(8,128)(2,1)S(1)}, u32[]{:S(2)}, u32[]{:S(2)}) collective-permute-start(bf16[4,96,768]{2,1,0:T(8,128)(2,1)} %get-tuple-element.255), channel_id=1, source_target_pairs={{0,4},{4,0},{8,12},{12,8},{16,20},{20,16},{24,28},{28,24},{1,5},{5... | collective-permute-start | bytes 1769480 | tf_op jit(solution)/shard_map/ppermute | solution.py:75
  349.3 67.3 %collective-permute-start.47 = (bf16[8,96,768]{2,1,0:T(8,128)(2,1)}, bf16[8,96,768]{2,1,0:T(8,128)(2,1)S(1)}, u32[]{:S(2)}, u32[]{:S(2)}) collective-permute-start(bf16[8,96,768]{2,1,0:T(8,128)(2,1)} %get-tuple-element.264.a), channel_id=1, source_target_pairs={{0,2},{1,3},{2,0},{3,1},{4,6},{5,7},{6,4},{7,5},{8,10},{9,11},{10,... | collective-permute-start | bytes 3538952 | tf_op jit(solution)/shard_map/ppermute | solution.py:75
  350.9 34.7 %collective-permute-start.55 = (bf16[2,1,96,768]{3,2,1,0:T(8,128)(2,1)}, bf16[2,1,96,768]{3,2,1,0:T(8,128)(2,1)S(1)}, u32[]{:S(2)}, u32[]{:S(2)}) collective-permute-start(bf16[2,1,96,768]{3,2,1,0:T(8,128)(2,1)} %get-tuple-element.276), channel_id=1, source_target_pairs={{0,16},{4,20},{8,24},{12,28},{16,0},{20,4},{24,8},{28,12},{1,17},{... | collective-permute-start | bytes 884744 | tf_op jit(solution)/shard_map/ppermute | solution.py:75
  381.8 25.9 %collective-permute-start.36 = (bf16[448,768]{1,0:T(8,128)(2,1)}, bf16[448,768]{1,0:T(8,128)(2,1)S(1)}, u32[]{:S(2)}, u32[]{:S(2)}) collective-permute-start(bf16[448,768]{1,0:T(8,128)(2,1)} %get-tuple-element.242.a), channel_id=1, source_target_pairs={{0,1},{1,0},{2,3},{3,2},{4,5},{5,4},{6,7},{7,6},{8,9},{9,8},{10,11... | collective-permute-start | bytes 2064392 | tf_op jit(solution)/shard_map/ppermute | solution.py:75
  385.6 22.0 %collective-permute-start.44 = (bf16[448,768]{1,0:T(8,128)(2,1)}, bf16[448,768]{1,0:T(8,128)(2,1)}, u32[]{:S(2)}, u32[]{:S(2)}) collective-permute-start(bf16[448,768]{1,0:T(8,128)(2,1)} %collective-permute-done.37.c), channel_id=1, source_target_pairs={{0,1},{1,0},{2,3},{3,2},{4,5},{5,4},{6,7},{7,6},{8,9},{9,8},{10,11... | collective-permute-start | bytes 2064392 | tf_op jit(solution)/shard_map/ppermute | solution.py:75
  389.4 22.5 %collective-permute-start.45 = (bf16[2,1,96,768]{3,2,0,1:T(8,128)(2,1)}, bf16[2,1,96,768]{3,2,0,1:T(8,128)(2,1)}, u32[]{:S(2)}, u32[]{:S(2)}) collective-permute-start(bf16[2,1,96,768]{3,2,0,1:T(8,128)(2,1)} %bitcast.89), channel_id=1, source_target_pairs={{0,8},{4,12},{8,0},{12,4},{16,24},{20,28},{24,16},{28,20},{1,9},{5... | collective-permute-start | bytes 884744 | tf_op jit(solution)/shard_map/ppermute | solution.py:75
  391.9 24.1 %all-to-all-start.4 = ((f32[8,4,96]{2,1,0:T(4,128)}), f32[8,4,96]{2,1,0:T(4,128)S(1)}, u32[]{:S(2)}, u32[]{:S(2)}) async-start(f32[8,4,96]{2,1,0:T(4,128)} %bitcast.59), calls=%async_computation.4 | async-start | bytes 32768 | tf_op jit(solution)/shard_map/all_to_all | solution.py:1142
  (91 other events, 795.2 us)

commit v3 on v2

--- a/solution.py
+++ b/solution.py
@@ -16,6 +16,9 @@
 BF16 = jnp.bfloat16
 VMEM_LIMIT = 56 << 20
 COST_SCALE = 1.0
+LONG = 50.0
+SHORT = 1e-6
+SPLIT = 32
 
 
 def dot(left, right, left_dim=1, right_dim=0):
@@ -45,8 +48,8 @@
     return jax.ShapeDtypeStruct(dims, dtype)
 
 
-def cost(flops, moved, exps=0):
-    scale = COST_SCALE
+def cost(flops, moved, exps=0, scale=None):
+    scale = COST_SCALE if scale is None else scale
     return pl.CostEstimate(
         flops=int(flops * scale), bytes_accessed=int(moved * scale), transcendentals=int(exps * scale)
     )
@@ -63,8 +66,8 @@
     return center * inverse, inverse
 
 
-def norm_back(unit, inverse, gain_row, grad):
-    scaled = grad * gain_row
+def norm_back(unit, inverse, gains_all, grad):
+    scaled = grad * gains_all
     first = jnp.mean(scaled, axis=-1, keepdims=True)
     second = jnp.mean(scaled * unit, axis=-1, keepdims=True)
     return (scaled - first - unit * second) * inverse
@@ -94,13 +97,18 @@
             item, _ = lax.optimization_barrier((item, named))
         return item
 
+    def join(self, *items):
+        items = lax.optimization_barrier(items)
+        self.last = items[0]
+        return items
+
 
 def encode_body(order, memory_ref, gain_ref, out_ref):
     unit, _ = norm_stats(memory_ref[:, 0].astype(F32))
-    out_ref[...] = (unit * gain_ref[...]).astype(BF16)
-
-
-def encode(order, memory, gain_row, start, size):
+    out_ref[...] = (unit * gain_ref[0 : 1]).astype(BF16)
+
+
+def encode(order, memory, gains_all, start, size):
     wide, _, _, width = memory.shape
     group = min(4, wide)
     return call(
@@ -108,20 +116,20 @@
         (wide // group,),
         [
             pl.BlockSpec((group, 1, size, width), lambda i, order: (i, order[0], start // size, 0)),
-            whole((1, width)),
+            whole(gains_all.shape),
         ],
         pl.BlockSpec((group, size, width), lambda i, *_: (i, 0, 0)),
         shape((wide, size, width)),
         "encode",
         cost(0, 4 * wide * size * width),
         prefetch=1,
-    )(order, memory, gain_row)
+    )(order, memory, gains_all)
 
 
 def memory_back_body(order, memory_ref, gain_ref, grad_ref, out_ref, gain_out):
     unit, inverse = norm_stats(memory_ref[:, 0].astype(F32))
     grad = grad_ref[...].astype(F32)
-    out_ref[...] = norm_back(unit, inverse, gain_ref[...], grad).astype(BF16)
+    out_ref[...] = norm_back(unit, inverse, gain_ref[0 : 1], grad).astype(BF16)
 
     @pl.when(pl.program_id(0) == 0)
     def _():
@@ -130,7 +138,7 @@
     gain_out[...] += jnp.sum(jnp.sum(grad * unit, axis=0), axis=0, keepdims=True)
 
 
-def memory_back(order, memory, gain_row, grad, start):
+def memory_back(order, memory, gains_all, grad, start, scale):
     wide, _, _, width = memory.shape
     size = grad.shape[1]
     group = min(4, wide)
@@ -140,15 +148,15 @@
         (wide // group,),
         [
             pl.BlockSpec((group, 1, size, width), lambda i, order: (i, order[0], start // size, 0)),
-            whole((1, width)),
+            whole(gains_all.shape),
             rows,
         ],
         [rows, whole((1, width))],
         [shape((wide, size, width)), shape((1, width), F32)],
         "memory_back",
-        cost(0, 6 * wide * size * width),
+        cost(0, 6 * wide * size * width, scale=scale),
         prefetch=1,
-    )(order, memory, gain_row, grad)
+    )(order, memory, gains_all, grad)
 
 
 def self_fwd_body(order, lengths, token_ref, gain_ref, weight_ref, normed_ref, qkv_ref, first_ref, second_ref, lse_ref):
@@ -157,7 +165,7 @@
     step = pl.program_id(0)
     length = lengths[order[step]]
     unit, _ = norm_stats(token_ref[0].astype(F32))
-    normed = (unit * gain_ref[...]).astype(BF16)
+    normed = (unit * gain_ref[1 : 2]).astype(BF16)
     normed_ref[0] = normed
     for i in range(3):
         qkv_ref[0, i] = dot(normed, weight_ref[i], 1, 1).astype(BF16)
@@ -192,7 +200,7 @@
         second_ref[...] = mixed
 
 
-def self_fwd(order, lengths, tokens, gain_row, weights):
+def self_fwd(order, lengths, tokens, gains_all, weights):
     _, seq, width = tokens.shape
     local = weights.shape[1]
     heads = local // HEAD_DIM
@@ -201,7 +209,7 @@
         (2,),
         [
             pl.BlockSpec((1, seq, width), lambda i, order, lengths: (order[i], 0, 0)),
-            whole((1, width)),
+            whole(gains_all.shape),
             whole((3, local, width)),
         ],
         [
@@ -221,7 +229,7 @@
         "self_forward",
         cost(2 * (6 * seq * width * local + 8 * seq * seq * local), 2 * seq * width * 8, 2 * heads * seq * seq),
         prefetch=2,
-    )(order, lengths, tokens, gain_row, weights)
+    )(order, lengths, tokens, gains_all, weights)
 
 
 def self_bwd_body(order, lengths, qkv_ref, mixed0_ref, mixed1_ref, lse_ref, grad0_ref, grad1_ref, weight_ref, dqkv_ref, first_ref, second_ref):
@@ -277,7 +285,7 @@
         second_ref[...] = total
 
 
-def self_bwd(order, lengths, qkv, mixed0, mixed1, lse, grad0, grad1, weights):
+def self_bwd(order, lengths, qkv, mixed0, mixed1, lse, grad0, grad1, weights, scale):
     _, _, seq, local = qkv.shape
     width = weights.shape[2]
     heads = local // HEAD_DIM
@@ -300,7 +308,7 @@
         ],
         [shape((2, 3, seq, local)), shape((seq, width)), shape((seq, width))],
         "self_backward",
-        cost(2 * (6 * seq * width * local + 20 * seq * seq * local), 2 * seq * width * 8, 2 * heads * seq * seq),
+        cost(2 * (6 * seq * width * local + 20 * seq * seq * local), 2 * seq * width * 8, 2 * heads * seq * seq, scale=scale),
         prefetch=2,
     )(order, lengths, qkv, mixed0, mixed1, lse, grad0, grad1, weights)
 
@@ -312,14 +320,14 @@
         rows = rows + dot(mixed[...], pack[:local])
     after_ref[...] = rows
     unit, _ = norm_stats(rows)
-    normed = (unit * gain_ref[...]).astype(BF16)
+    normed = (unit * gain_ref[2 : 3]).astype(BF16)
     normed_ref[...] = normed
     for r, pack in enumerate((p0, p1, p2, p3)):
         query = dot(normed, pack[local:], 1, 1).astype(BF16)
         query_ref[r // 2, :, (r % 2) * local : (r % 2 + 1) * local] = query
 
 
-def to_query(order, tokens, mixes, packs, gain_row):
+def to_query(order, tokens, mixes, packs, gains_all):
     _, seq, width = tokens.shape
     local = mixes[0].shape[1]
     tile = seq // 2
@@ -329,7 +337,7 @@
         [pl.BlockSpec((1, tile, width), lambda i, order: (order[0], i, 0))]
         + [pl.BlockSpec((tile, local), lambda i, *_: (i, 0))] * 4
         + [whole((2 * local, width))] * 4
-        + [whole((1, width))],
+        + [whole(gains_all.shape)],
         [
             pl.BlockSpec((tile, width), lambda i, *_: (i, 0)),
             pl.BlockSpec((tile, width), lambda i, *_: (i, 0)),
@@ -339,7 +347,7 @@
         "self_out_to_query",
         cost(4 * seq * width * width, seq * width * 12 + 4 * width * width),
         prefetch=1,
-    )(order, tokens, *mixes, *packs, gain_row)
+    )(order, tokens, *mixes, *packs, gains_all)
 
 
 def head_places(local):
@@ -414,7 +422,7 @@
             next_ref[...] = rows
             if step == 1:
                 unit, _ = norm_stats(rows)
-                normed_ref[...] = (unit * gain_ref[...]).astype(BF16)
+                normed_ref[...] = (unit * gain_ref[3 : 4]).astype(BF16)
 
 
 def pack_specs(packs, rows, index):
@@ -448,7 +456,7 @@
     )(query, encoded, *packs)
 
 
-def cross_second(query, encoded, packs, packs_out, valid, before, after, gain_row):
+def cross_second(query, encoded, packs, packs_out, valid, before, after, gains_all):
     _, seq, pair = query.shape
     frames, width = encoded.shape
     heads = pair // HEAD_DIM
@@ -462,7 +470,7 @@
         + pack_specs(packs, pair, 0)
         + [acc, stats, stats, whole((seq, width))]
         + pack_specs(packs_out, pair // 2, 0)
-        + [whole((1, width))],
+        + [whole(gains_all.shape)],
         [pl.BlockSpec((frames, 2 * pair), lambda i: (0, i)), rows, stats, whole((seq, width)), whole((seq, width))],
         [
             shape((frames, 4 * pair)),
@@ -473,7 +481,7 @@
         ],
         "cross_second",
         cost(4 * frames * width * width + 40 * seq * frames * pair, 10 * frames * width, 2 * heads * seq * frames),
-    )(query, encoded, *packs, *before, after, *packs_out, gain_row)
+    )(query, encoded, *packs, *before, after, *packs_out, gains_all)
 
 
 def feed_body(order, lengths, *refs, count):
@@ -589,7 +597,7 @@
         grads = jnp.where(place < lengths[order[0]], grad_ref[0].astype(F32), 0.0)
         normed_grad = own_ref[...].astype(F32) + near_ref[...].astype(F32) + far_ref[...].astype(F32)
         unit, inverse = norm_stats(after_ref[...])
-        total = grads + norm_back(unit, inverse, gain_ref[...], normed_grad)
+        total = grads + norm_back(unit, inverse, gain_ref[3 : 4], normed_grad)
         cross_ref[...] = total
         low = total.astype(BF16)
         two_ref[...] = low
@@ -605,7 +613,7 @@
     encoded_back(dkv_ref, (w0, w1, w2, w3), encoded_ref, acc)
 
 
-def cross_first_back(order, lengths, out_grad, parts, after, gain_row, packs, packs_out, query, kv, mixed, lse, valid):
+def cross_first_back(order, lengths, out_grad, parts, after, gains_all, packs, packs_out, query, kv, mixed, lse, valid):
     seq, width = after.shape
     frames = kv.shape[0]
     pair = query.shape[2]
@@ -617,7 +625,7 @@
         functools.partial(cross_first_back_body, valid=valid),
         (2,),
         [pl.BlockSpec((1, seq, width), lambda i, order, lengths: (order[0], 0, 0)), rows, rows, rows, rows]
-        + [whole((1, width))]
+        + [whole(gains_all.shape)]
         + pack_specs(packs_out, pair // 2, 0)
         + [head_rows, both, head_rows, pl.BlockSpec((1, heads, seq), lambda i, *_: (i, 0, 0))]
         + pack_specs(packs, pair, 0),
@@ -643,7 +651,7 @@
         cost(4 * frames * width * width + 120 * seq * frames * pair, 20 * frames * width, 2 * heads * seq * frames),
         prefetch=2,
         scratch=[pltpu.VMEM((frames, width), F32)],
-    )(order, lengths, out_grad, *parts, after, gain_row, *packs_out, query, kv, mixed, lse, *packs)
+    )(order, lengths, out_grad, *parts, after, gains_all, *packs_out, query, kv, mixed, lse, *packs)
 
 
 def cross_second_back_body(
@@ -667,7 +675,7 @@
         for r, pack in enumerate(packs):
             normed_grad = normed_grad + dot(dq_ref[r // 2, :, (r % 2) * local : (r % 2 + 1) * local], pack[local:])
         unit, inverse = norm_stats(after_ref[...])
-        total = cross_ref[...] + norm_back(unit, inverse, gain_ref[...], normed_grad)
+        total = cross_ref[...] + norm_back(unit, inverse, gain_ref[2 : 3], normed_grad)
         self_ref[...] = total
         low = total.astype(BF16)
         one_ref[...] = low
@@ -676,7 +684,7 @@
         gain_out[...] = jnp.sum(normed_grad * unit, axis=0, keepdims=True)
 
 
-def cross_second_back(query, kv, grads, mixed, lse, dq, packs_two, packs_one, after, gain_row, cross, valid):
+def cross_second_back(query, kv, grads, mixed, lse, dq, packs_two, packs_one, after, gains_all, cross, valid):
     seq, width = after.shape
     frames = kv.shape[0]
     pair = query.shape[2]
@@ -692,7 +700,7 @@
         + [pl.BlockSpec((1, pair, seq), lambda i: (i, 0, 0))]
         + pack_specs(packs_two, pair, 0)
         + pack_specs(packs_one, pair, 0)
-        + [rows, whole((1, width)), rows],
+        + [rows, whole(gains_all.shape), rows],
         [whole((2, seq, pair)), both, whole((frames, width)), rows, rows]
         + [whole((seq, local))] * 4
         + [whole((1, width))],
@@ -708,7 +716,7 @@
         "cross_second_back",
         cost(4 * frames * width * width + 120 * seq * frames * pair, 20 * frames * width, 2 * heads * seq * frames),
         scratch=[pltpu.VMEM((frames, width), F32)],
-    )(query, kv, grads, mixed, lse, dq, *packs_two, *packs_one, after, gain_row, cross)
+    )(query, kv, grads, mixed, lse, dq, *packs_two, *packs_one, after, gains_all, cross)
 
 
 def add_gain(gain_out, term):
@@ -721,24 +729,24 @@
 def to_tokens_grad_body(order, token_ref, own_ref, near_ref, far_ref, self_ref, gain_ref, out_ref, gain_out):
     normed_grad = own_ref[...].astype(F32) + near_ref[...].astype(F32) + far_ref[...].astype(F32)
     unit, inverse = norm_stats(token_ref[0].astype(F32))
-    out_ref[...] = (self_ref[...] + norm_back(unit, inverse, gain_ref[...], normed_grad)).astype(BF16)
+    out_ref[...] = (self_ref[...] + norm_back(unit, inverse, gain_ref[1 : 2], normed_grad)).astype(BF16)
     add_gain(gain_out, jnp.sum(normed_grad * unit, axis=0, keepdims=True))
 
 
-def to_tokens_grad(order, tokens, own, near, far, grad_self, gain_row):
+def to_tokens_grad(order, tokens, own, near, far, grad_self, gains_all, scale):
     _, seq, width = tokens.shape
     tile = seq // 2
     rows = pl.BlockSpec((tile, width), lambda i, *_: (i, 0))
     return call(
         to_tokens_grad_body,
         (2,),
-        [pl.BlockSpec((1, tile, width), lambda i, order: (order[0], i, 0)), rows, rows, rows, rows, whole((1, width))],
+        [pl.BlockSpec((1, tile, width), lambda i, order: (order[0], i, 0)), rows, rows, rows, rows, whole(gains_all.shape)],
         [rows, whole((1, width))],
         [shape((seq, width)), shape((1, width), F32)],
         "norm_one_back",
-        cost(0, seq * width * 14),
+        cost(0, seq * width * 14, scale=scale),
         prefetch=1,
-    )(order, tokens, own, near, far, grad_self, gain_row)
+    )(order, tokens, own, near, far, grad_self, gains_all)
 
 
 def split_store(total, mine, keep_ref, give_ref, scratch, lead=()):
@@ -787,11 +795,8 @@
     )(bits, *rows, *pres, *lives, *hiddens)
 
 
-def head_weights_body(*refs):
-    enc0, enc1, dkv0, dkv1, two, dq_ref, one, grad_two, cross_mixed = refs[:9]
-    mixes = refs[9:13]
-    keep_ref, give_ref, self_keep, self_give = refs[13:]
-    local = mixes[0].shape[1]
+def head_weights_body(enc0, enc1, dkv0, dkv1, two, dq_ref, grad_two, cross_mixed, keep_ref, give_ref):
+    local = dq_ref.shape[2] // 2
     for r in range(4):
         out = (keep_ref, give_ref)[r % 2]
         columns = slice((r % 2) * local, (r % 2 + 1) * local)
@@ -801,29 +806,44 @@
         query = dot(two[...], dq_ref[r // 2, :, columns], 0, 0)
         cross = dot(grad_two[...], cross_mixed[r // 2, :, columns], 0, 0)
         out[r // 2, :, 2 * local :] = jnp.concatenate((query, cross), axis=1).astype(BF16)
-        (self_keep, self_give)[r % 2][r // 2] = dot(mixes[r][...], one[...], 0, 0).astype(BF16)
-
-
-def head_weights(encs, dkvs, normed_two, dq, grad_one, grad_two, cross_mixed, mixes):
+
+
+def head_weights(encs, dkvs, normed_two, dq, grad_two, cross_mixed, scale):
     seq, width = normed_two.shape
-    local = mixes[0].shape[1]
     tile = width // 2
     rows = pl.BlockSpec((seq, tile), lambda i: (0, i))
     out = pl.BlockSpec((2, tile, width), lambda i: (0, i, 0))
-    turned = pl.BlockSpec((2, local, tile), lambda i: (0, 0, i))
     frames = encs[0].shape[0] + encs[1].shape[0]
     return call(
         head_weights_body,
         (2,),
         [pl.BlockSpec((item.shape[0], tile), lambda i: (0, i)) for item in encs]
         + [whole(item.shape) for item in dkvs]
-        + [rows, whole(dq.shape), rows, rows, whole(cross_mixed.shape)]
-        + [whole(item.shape) for item in mixes],
-        [out, out, turned, turned],
-        [shape((2, width, width))] * 2 + [shape((2, local, width))] * 2,
+        + [rows, whole(dq.shape), rows, whole(cross_mixed.shape)],
+        [out, out],
+        [shape((2, width, width))] * 2,
         "head_weight_grads",
-        cost(4 * frames * width * width + 6 * seq * width * width, 6 * frames * width),
-    )(*encs, *dkvs, normed_two, dq, grad_one, grad_two, cross_mixed, *mixes)
+        cost(4 * frames * width * width + 4 * seq * width * width, 6 * frames * width, scale=scale),
+    )(*encs, *dkvs, normed_two, dq, grad_two, cross_mixed)
+
+
+def out_weights_body(one, m0, m1, m2, m3, keep_ref, give_ref):
+    for r, mixed in enumerate((m0, m1, m2, m3)):
+        (keep_ref, give_ref)[r % 2][r // 2] = dot(mixed[...], one[...], 0, 0).astype(BF16)
+
+
+def out_weights(grad_one, mixes, scale):
+    seq, width = grad_one.shape
+    local = mixes[0].shape[1]
+    return call(
+        out_weights_body,
+        (1,),
+        [whole(item.shape) for item in (grad_one, *mixes)],
+        [whole((2, local, width))] * 2,
+        [shape((2, local, width))] * 2,
+        "out_weight_grads",
+        cost(2 * seq * width * width, 8 * seq * width, scale=scale),
+    )(grad_one, *mixes)
 
 
 def self_weights_body(bits, near, far, dnear, dfar, own, core, other, keep_ref, give_ref, scratch):
@@ -837,7 +857,7 @@
     split_store(jnp.concatenate(totals, axis=1), bits[0], keep_ref, give_ref, scratch)
 
 
-def self_weights(bits, near, far, dnear, dfar, own, core, other, wide):
+def self_weights(bits, near, far, dnear, dfar, own, core, other, wide, scale):
     _, seq, width = near.shape
     local = dnear.shape[3]
     tile = width // 2
@@ -853,31 +873,73 @@
         [out, out],
         [shape((wide // 2, depth, 4 * local))] * 2,
         "self_weight_grads",
-        cost(24 * seq * width * local, 16 * seq * width),
+        cost(24 * seq * width * local, 16 * seq * width, scale=scale),
         prefetch=1,
         scratch=[pltpu.VMEM((tile, 4 * local), F32)],
     )(bits, near, far, dnear, dfar, own, core, other)
 
 
-def merge_body(bits, keep_in, got_in, keep_out, give_out, *, which):
-    mine = bits[which] if which >= 0 else 0
-    keep_out[:, 0] = (keep_in[:, mine].astype(F32) + got_in[:, mine].astype(F32)).astype(BF16)
-    give_out[:, 0] = (keep_in[:, 1 - mine].astype(F32) + got_in[:, 1 - mine].astype(F32)).astype(BF16)
-
-
-def merge(bits, keep, got, which):
-    groups, _, rows, columns = keep.shape
+def add_low(keep, got):
+    return (keep.astype(F32) + got.astype(F32)).astype(BF16)
+
+
+def merge_body(bits, *refs, which, joined):
+    ins, outs = refs[: 2 * len(which)], refs[2 * len(which) :]
+    at = 0
+    for i, bit in enumerate(which):
+        keep_in, got_in = ins[2 * i], ins[2 * i + 1]
+        mine = bits[bit]
+        keep_out, give_out = outs if joined else outs[2 * i : 2 * i + 2]
+        groups = slice(at, at + keep_in.shape[0])
+        at += keep_in.shape[0] if joined else 0
+        keep_out[groups, 0] = add_low(keep_in[:, mine], got_in[:, mine])
+        give_out[groups, 0] = add_low(keep_in[:, 1 - mine], got_in[:, 1 - mine])
+
+
+def merge(bits, which, *pairs, scale=None, joined=False):
+    rows, columns = pairs[0][0].shape[2:]
     tile = rows // 2 if rows % 32 == 0 else rows
-    both = pl.BlockSpec((groups, 2, tile, columns), lambda i, *_: (0, 0, i, 0))
-    out = pl.BlockSpec((groups, 1, tile, columns), lambda i, *_: (0, 0, i, 0))
-    return call(
-        functools.partial(merge_body, which=which),
+    both = [
+        pl.BlockSpec((item.shape[0], 2, tile, columns), lambda i, *_: (0, 0, i, 0)) for pair in pairs for item in pair
+    ]
+    groups = [keep.shape[0] for keep, _ in pairs]
+    total = sum(groups)
+    groups = [total] if joined else groups
+    return call(
+        functools.partial(merge_body, which=which, joined=joined),
+        (rows // tile,),
+        both,
+        [pl.BlockSpec((count, 1, tile, columns), lambda i, *_: (0, 0, i, 0)) for count in groups for _ in range(2)],
+        [shape((count, 1, rows, columns)) for count in groups for _ in range(2)],
+        "merge",
+        cost(0, 12 * total * rows * columns, scale=scale),
+        prefetch=1,
+    )(bits, *[item for pair in pairs for item in pair])
+
+
+def merge_heads_body(bits, keep_in, got_in, keep_a, give_a, keep_b, give_b):
+    low, high = bits[0], bits[1]
+    for j in range(keep_a.shape[0]):
+        keep_a[j] = add_low(keep_in[0, 2 * j + low], got_in[0, 2 * j + low])
+        give_a[j] = add_low(keep_in[0, 2 * j + 1 - low], got_in[0, 2 * j + 1 - low])
+        at = 4 * (j // 2) + j % 2
+        keep_b[j] = add_low(keep_in[1, at + 2 * high], got_in[1, at + 2 * high])
+        give_b[j] = add_low(keep_in[1, at + 2 * (1 - high)], got_in[1, at + 2 * (1 - high)])
+
+
+def merge_heads(bits, keep, got):
+    _, parts, rows, columns = keep.shape
+    tile = rows // 2 if rows % 32 == 0 else rows
+    both = pl.BlockSpec((2, parts, tile, columns), lambda i, *_: (0, 0, i, 0))
+    out = pl.BlockSpec((parts // 2, tile, columns), lambda i, *_: (0, i, 0))
+    return call(
+        merge_heads_body,
         (rows // tile,),
         [both, both],
-        [out, out],
-        [shape((groups, 1, rows, columns))] * 2,
-        "merge",
-        cost(0, 12 * groups * rows * columns),
+        [out] * 4,
+        [shape((parts // 2, rows, columns))] * 4,
+        "merge_heads",
+        cost(0, 12 * parts * rows * columns, scale=SHORT),
         prefetch=1,
     )(bits, keep, got)
 
@@ -889,7 +951,7 @@
     while parts > 1:
         parts //= 2
         view = (lead * parts, 2) + dims
-        keep, give = merge(then(bits), keep.reshape(view), got.reshape(view), which)
+        keep, give = merge(then(bits), (which,), (keep.reshape(view), got.reshape(view)), scale=SHORT)
         then.last = keep
         which += 1
         got = swap(give, "wide", 1 << (which - 1))
@@ -916,7 +978,7 @@
         item.wait()
 
 
-def place_blocks(order, blocks, dims, start=None, before=None):
+def place_blocks(order, blocks, dims, start=None, before=None, scale=None):
     anywhere = pl.BlockSpec(memory_space=pl.ANY)
     extra = () if before is None else (before,)
     return pl.pallas_call(
@@ -935,7 +997,7 @@
         out_shape=shape(dims),
         input_output_aliases={5: 0} if extra else {},
         compiler_params=pltpu.CompilerParams(vmem_limit_bytes=VMEM_LIMIT),
-        cost_estimate=cost(0, 16 * blocks[0].size),
+        cost_estimate=cost(0, 16 * blocks[0].size, scale=SHORT if scale is None else scale),
         name="place_blocks",
     )(order, *blocks, *extra)
 
@@ -955,17 +1017,17 @@
     order = (me ^ jnp.arange(4)).astype(jnp.int32)
     near_order = (me ^ jnp.array([1, 0])).astype(jnp.int32)
     far_order = (me ^ jnp.array([3, 2])).astype(jnp.int32)
-    gain_row = [gains[i : i + 1] for i in range(4)]
     then = Order()
 
     by_clip = memory.reshape(wide, narrow, share, width)
-    sizes = (-(-share // 32) * 16, share - -(-share // 32) * 16)
-    starts = (0, sizes[0])
+    first = -(-share // SPLIT) * 16
+    sizes = (first, share - first)
+    starts = (0, first)
     last = AUDIO - (wide - 1) * share
     valid = [(wide - 1) * size + min(max(last - start, 0), size) for start, size in zip(starts, sizes)]
 
     def encoder_rows(part, *named):
-        block = encode(then(order, *named), by_clip, gain_row[0], starts[part], sizes[part])
+        block = encode(then(order, *named), by_clip, gains, starts[part], sizes[part])
         then.last = block
         block = lax.all_to_all(block, "wide", 0, 0, tiled=True)
         return block.reshape(wide * sizes[part], width)
@@ -976,13 +1038,13 @@
     packs_one = gather_narrow(jnp.concatenate((self_out, then(cross_q).T)))
 
     normed_far, qkv_far, mixed_three, mixed_two, lse_far = self_fwd(
-        then(far_order), lengths, tokens, gain_row[1], self_qkv
+        then(far_order), lengths, tokens, gains, self_qkv
     )
     then.last = mixed_two
     mix_two = swap(mixed_two, "narrow", 2)
     crossing = swap(mixed_three, "narrow", 1)
     normed_near, qkv_near, mixed_one, mixed_zero, lse_near = self_fwd(
-        then(near_order), lengths, tokens, gain_row[1], self_qkv
+        then(near_order), lengths, tokens, gains, self_qkv
     )
     then.last = mixed_zero
     mix_three = swap(then(crossing), "narrow", 2)
@@ -991,7 +1053,7 @@
     packs_one = finish(packs_one, then)
     encoded_second = encoder_rows(1, mix_two, packs_one[2])
     encoded = (encoded_first, encoded_second)
-    after_self, normed_two, query = to_query(then(order), tokens, mixes, packs_one, gain_row[2])
+    after_self, normed_two, query = to_query(then(order), tokens, mixes, packs_one, gains)
     then.last = query
     packs_kv = finish(packs_kv, then)
     packs_out = gather_narrow(then(cross_out))
@@ -999,7 +1061,7 @@
     then.last = kv_first
     packs_out = finish(packs_out, then)
     kv_second, cross_mixed, cross_lse, after_cross, normed_three = cross_second(
-        query, encoded_second, packs_kv, packs_out, valid[1], before, after_self, gain_row[3]
+        query, encoded_second, packs_kv, packs_out, valid[1], before, after_self, gains
     )
     then.last = normed_three
 
@@ -1034,7 +1096,7 @@
     feed_got = swap(feed_give, "wide", 1)
 
     grad_cross, grad_two, grad_mixed, gain_three, dq, dkv_first, frames_first = cross_first_back(
-        then(order), lengths, out_grad, (part_zero, part_near, part_far), after_cross, gain_row[3],
+        then(order), lengths, out_grad, (part_zero, part_near, part_far), after_cross, gains,
         packs_kv, packs_out, query, kv_first, cross_mixed, cross_lse, valid[0],
     )
     then.last = dkv_first
@@ -1050,96 +1112,135 @@
     then.last = block_own
     block_all = gather_narrow(block_own)
     view = (2 * (wide // 4), 2, depth, width)
-    feed_keep, feed_give = merge(then(bits), feed_keep.reshape(view), feed_got.reshape(view), 1)
+    feed_keep, feed_give = merge(then(bits), (1,), (feed_keep.reshape(view), feed_got.reshape(view)))
     then.last = feed_keep
     feed_got = swap(feed_give, "wide", 2)
     dq, dkv_second, frames_second, grad_self, grad_one, head0, head1, head2, head3, gain_two = cross_second_back(
         query, kv_second, grad_mixed, cross_mixed, cross_lse, dq, packs_kv, packs_one, after_self,
-        then(gain_row[2]), grad_cross, valid[1],
+        then(gains), grad_cross, valid[1],
     )
     then.last = dq
+    head1, head2, head3, frames_second, feed_got, *block_all = then.join(
+        head1, head2, head3, frames_second, feed_got, *block_all
+    )
+    feed_view = (2 * (wide // 8), 2, depth, width)
+    feed_keep, feed_give = merge(
+        then(bits), (2,), (feed_keep.reshape(feed_view), feed_got.reshape(feed_view)), scale=SHORT
+    )
+    feed_give, head1, head2, head3 = then.join(feed_give, head1, head2, head3)
+    feed_got = swap(feed_give, "wide", 4)
     heads_one = swap(head1, "narrow", 1)
     heads_two = swap(head2, "narrow", 2)
     head3 = swap(head3, "narrow", 2)
+    block_all = block_all + [swap(block_all[2], "narrow", 1)]
+
+    self_keep, self_give = out_weights(then(grad_one), mixes, LONG)
+    then.last = self_give
+    self_got = swap(self_give, "narrow", 1)
+    back_first, gain_first = memory_back(then(order), by_clip, gains, frames_first, starts[0], SHORT)
+    back_first, frames_second, heads_one, heads_two, head3, feed_got = then.join(
+        back_first, frames_second, heads_one, heads_two, head3, feed_got
+    )
     frames_second = frames_sent(frames_second, 1)
-    block_all = finish(block_all, then)
-
-    back_first, gain_first = memory_back(then(order), by_clip, gain_row[0], frames_first, starts[0])
-    then.last = back_first
+    heads_three = swap(head3, "narrow", 1)
+    back_first = gather_narrow(back_first)
+    keep, give = head_weights(
+        encoded, (dkv_first, dkv_second), then(normed_two), dq, grad_two, cross_mixed, LONG
+    )
+    give, keep, heads_three, *block_all = then.join(give, keep, heads_three, *block_all)
+    got = swap(give, "narrow", 1)
     dqkv_near, part_one, part_zero = self_bwd(
-        then(near_order, heads_two, head3), lengths, qkv_near, mixed_one, mixed_zero, lse_near, heads_one, head0,
-        self_qkv,
+        then(near_order), lengths, qkv_near, mixed_one, mixed_zero, lse_near, heads_one, head0, self_qkv, SHORT
     )
     then.last = part_one
-    heads_three = swap(then(head3), "narrow", 1)
-    back_first = gather_narrow(back_first)
     part_near = swap(part_one, "narrow", 1)
-    feed_grads = scatter_wide(bits, then, feed_keep, feed_give, 2, feed_got)
     dqkv_far, part_three, part_two = self_bwd(
-        then(far_order), lengths, qkv_far, mixed_three, mixed_two, lse_far, heads_three, heads_two, self_qkv
-    )
-    then.last = part_three
+        then(far_order), lengths, qkv_far, mixed_three, mixed_two, lse_far, heads_three, heads_two, self_qkv, SHORT
+    )
+    part_three, part_two, self_got, frames_second, *back_first = then.join(
+        part_three, part_two, self_got, frames_second, *back_first
+    )
     part_cross = swap(part_three, "narrow", 1)
-    block_out = place_blocks(then(order), block_all, (clips, seq, width))
-    then.last = block_out
+    back_first = back_first + [swap(back_first[2], "narrow", 1)]
+    feed_grads = scatter_wide(bits, then, feed_keep, feed_give, 3, feed_got)
+    self_other = (then(self_keep)[1].astype(F32) + self_got[1].astype(F32)).astype(BF16)
+    then.last = self_other
+    self_other = swap(self_other, "narrow", 2)
+    back_second, gain_second = memory_back(then(order), by_clip, gains, frames_second, starts[1], LONG)
+    back_second, part_two, part_cross, part_near, got, *back_first = then.join(
+        back_second, part_two, part_cross, part_near, got, *back_first
+    )
+    view = (2, wide, depth, width)
+    keep_a, give_a, keep_b, give_b = merge_heads(then(bits), keep.reshape(view), got.reshape(view))
+    then.last = give_a
+    got_a, got_b = swap(give_a, "wide", 1), swap(give_b, "wide", 2)
     part_far = (then(part_two).astype(F32) + part_cross.astype(F32)).astype(BF16)
     then.last = part_far
     part_far = swap(part_far, "narrow", 2)
-    keep, give, self_keep, self_give = head_weights(
-        encoded, (dkv_first, dkv_second), then(normed_two), dq, grad_one, grad_two, cross_mixed, mixes
-    )
-    then.last = keep
-    got = swap(give, "narrow", 1)
-    self_got = swap(self_give, "narrow", 1)
-    back_second, gain_second = memory_back(then(order), by_clip, gain_row[0], frames_second, starts[1])
-    then.last = back_second
-    self_other = (self_keep[1].astype(F32) + self_got[1].astype(F32)).astype(BF16)
-    then.last = self_other
-    self_other = swap(self_other, "narrow", 2)
-    view = (wide, 2, depth, width)
-    keep, give = merge(then(bits), keep.reshape(view), got.reshape(view), 0)
-    then.last = keep
-    got = swap(give, "wide", 1)
+    self_keep, self_give = self_weights(
+        then(bits), normed_near, normed_far, dqkv_near, dqkv_far, self_keep, self_got, self_other, wide, LONG
+    )
+    then.last = self_give
+    self_got = swap(self_give, "wide", 1)
     tokens_own, gain_one = to_tokens_grad(
-        then(order), tokens, part_zero, part_near, part_far, grad_self, gain_row[1]
+        then(order), tokens, part_zero, part_near, part_far, grad_self, gains, SHORT
     )
     then.last = tokens_own
     tokens_all = gather_narrow(tokens_own)
-    self_keep, self_give = self_weights(
-        then(bits), normed_near, normed_far, dqkv_near, dqkv_far, self_keep, self_got, self_other, wide
-    )
-    then.last = self_keep
-    self_got = swap(self_give, "wide", 1)
+    gain_terms = jnp.concatenate((gain_first + gain_second, gain_one, gain_two, gain_three))
+    gain_other = swap(gain_terms, "narrow", 1)
+    view = (wide // 4, 2, depth, width)
+    pair = lambda keep, got: (keep.reshape(view), got.reshape(view))
+    keep_a, give_a, keep_b, give_b = merge(then(bits), (1, 0), pair(keep_a, got_a), pair(keep_b, got_b), scale=LONG)
+    give_a, give_b, keep_a, keep_b, gain_terms, gain_other = then.join(
+        give_a, give_b, keep_a, keep_b, gain_terms, gain_other
+    )
+    got_a, got_b = swap(give_a, "wide", 2), swap(give_b, "wide", 1)
+    gain_terms = gain_terms + gain_other
+    gain_other = swap(gain_terms, "narrow", 2)
+    block_out = place_blocks(then(order), block_all, (clips, seq, width), scale=LONG)
+    block_out, self_got, gain_other = then.join(block_out, self_got, gain_other)
+    gain_terms = gain_terms + gain_other
+    gain_other = swap(gain_terms, "wide", 1)
+    self_keep, self_give = merge(then(bits), (1,), pair(self_keep, self_got), scale=SHORT)
+    then.last = self_give
+    self_got = swap(self_give, "wide", 2)
+    view = (wide // 8, 2, depth, width)
+    keep, give = merge(
+        then(bits), (2, 2, 2), pair(keep_a, got_a), pair(keep_b, got_b), pair(self_keep, self_got), scale=SHORT, joined=True
+    )
+    give, keep, back_second, gain_other, gain_terms, *tokens_all = then.join(
+        give, keep, back_second, gain_other, gain_terms, *tokens_all
+    )
+    got = swap(give, "wide", 4)
     back_second = gather_narrow(back_second)
-    back_first = finish(back_first, then)
-    view = (2 * (wide // 4), 2, depth, width)
-    keep, give = merge(then(bits), keep.reshape(view), got.reshape(view), 1)
-    then.last = keep
-    got = swap(give, "wide", 2)
-    memory_grad = place_blocks(then(order), back_first, (wide, narrow, share, width), starts[0])
-    then.last = memory_grad
-    view = (wide // 4, 2, depth, width)
-    self_keep, self_give = merge(then(bits), self_keep.reshape(view), self_got.reshape(view), 1)
-    then.last = self_keep
-    self_got = swap(self_give, "wide", 2)
-    tokens_all = finish(tokens_all, then)
-    keep = scatter_wide(bits, then, keep, give, 2, got).astype(BF16)
-    then.last = keep
-    other = swap(keep[1], "narrow", 2)
+    tokens_all = tokens_all + [swap(tokens_all[2], "narrow", 1)]
+    gain_terms = gain_terms + gain_other
+    gain_other = swap(gain_terms, "wide", 2)
+    memory_grad = place_blocks(
+        then(order), back_first, (wide, narrow, share, width), starts[0], scale=LONG
+    )
+    memory_grad, gain_other, gain_terms, *tokens_all = then.join(memory_grad, gain_other, gain_terms, *tokens_all)
+    gain_terms = gain_terms + gain_other
+    gain_other = swap(gain_terms, "wide", 4)
     tokens_grad = place_blocks(then(order), tokens_all, (clips, seq, width))
-    then.last = tokens_grad
-    self_grads = scatter_wide(bits, then, self_keep, self_give, 2, self_got)[0]
-    back_second = finish(back_second, then)
-    head_grads = keep[0].astype(F32) + other.astype(F32)
+    tokens_grad, got, *back_second = then.join(tokens_grad, got, *back_second)
+    back_second = back_second + [swap(back_second[2], "narrow", 1)]
+    total = scatter_wide(bits, then, keep, give, 3, got)
+    other = swap(total[1].astype(BF16), "narrow", 2)
     memory_grad = place_blocks(
-        then(order), back_second, (wide, narrow, share, width), starts[1], memory_grad
-    ).reshape(memory.shape)
-
-    gain_terms = jnp.concatenate((gain_first + gain_second, gain_one, gain_two, gain_three))
-    gain_terms = gain_terms + swap(gain_terms, "narrow", 1)
-    gain_terms = gain_terms + swap(gain_terms, "narrow", 2)
-    gain_terms = gain_terms.reshape(4, wide, depth).transpose(1, 0, 2)
-    gains_grad = jnp.sum(lax.all_to_all(gain_terms, "wide", 0, 0, tiled=True), axis=0)
+        then(order), back_second, (wide, narrow, share, width), starts[1], memory_grad, scale=LONG
+    )
+    memory_grad, other, gain_other = then.join(memory_grad, other, gain_other)
+    memory_grad = memory_grad.reshape(memory.shape)
+    head_grads = total[0] + other.astype(F32)
+    self_grads = total[2]
+    gain_terms = gain_terms + gain_other
+    bit = 8
+    while bit < wide:
+        gain_terms = gain_terms + swap(gain_terms, "wide", bit)
+        bit *= 2
+    gains_grad = lax.dynamic_slice_in_dim(gain_terms, place * depth, depth, 1)
 
     heads = lambda i: head_grads[:, i * local : (i + 1) * local]
     own = lambda i: self_grads[:, i * local : (i + 1) * local]

time: 445 us -> 401 us (0.901)
  waiting for transfers between devices: 99.2 us -> 55.9 us
  local copies, waits for them, and re-layouts: 22.5 us -> 17 us
    ppermute x56 -> x60, waiting for transfers between devices: 99.2 us -> 55.9 us  [swap(): return lax.ppermute(values, axis, [(i, i ^ bit) for i in range(size)])]
    ppermute x56 -> x60, starting transfers between devices: 36.3 us -> 43.8 us  [swap(): return lax.ppermute(values, axis, [(i, i ^ bit) for i in range(size)])]
    all_to_all x1 -> x0, starting transfers between devices: 4.54 us -> none  [on_device(): lax.all_to_all(gain_terms, 'wide', 0, 0, tiled=True)]
    unnamed x110 -> x124, local copies, waits for them, and re-layouts: 18 us -> 14.5 us
  transfers between devices with their start and end apart: 61 -> 64, of which waited for: 19 -> 17; matrix products, arithmetic and copies ran while one was open for 3% -> 3% of each run, Pallas kernels for 44% -> 53%
where the time goes in v3:
time: 401 us; the launch traced here: 394 us
  Pallas kernels  238 us (59%)
  starting transfers between devices  69.2 us (17%)
  waiting for transfers between devices  55.9 us (14%)
  local copies, waits for them, and re-layouts  17 us (4%)
  other arithmetic  12.2 us (3%)
    ppermute x60, waiting for transfers between devices, swap(): return lax.ppermute(values, axis, [(i, i ^ bit) for i in range(size)])  55.9 us
    ppermute x60, starting transfers between devices, swap(): return lax.ppermute(values, axis, [(i, i ^ bit) for i in range(size)])  43.8 us
    pallas_call x1, Pallas kernels, cross_second_back(): call(functools.partial(cross_second_back_body, valid=valid), (2,), [head_...  25.2 us
    pallas_call x1, Pallas kernels, cross_first_back(): call(functools.partial(cross_first_back_body, valid=valid), (2,), [pl.Blo...  24.4 us
    pallas_call x3, Pallas kernels, feed_forward(): call(functools.partial(feed_body, count=count), (count, tiles), single +...  23.7 us
    pallas_call x1, Pallas kernels, cross_second(): call(functools.partial(cross_second_body, valid=valid), (2,), [rows, whol...  18.4 us
    pallas_call x2, Pallas kernels, self_bwd(): call(self_bwd_body, (2,), [pl.BlockSpec((1, 3, seq, local), lambda i, *_:...  18.4 us
    pallas_call x2, Pallas kernels, self_fwd(): call(self_fwd_body, (2,), [pl.BlockSpec((1, seq, width), lambda i, order,...  18.1 us
  transfers between devices with their start and end apart: 64, of which 17 were waited for; matrix products, arithmetic and copies ran while one was open for 3% of the time, Pallas kernels for 53%

profile of v3, /device:TPU:0, one launch (start us, length us, event | category | flops | bytes accessed | tf_op | source)
XLA Modules:
  0.0 394.2 jit_solution(2416179250911304388)
XLA Ops:
  4.5 7.4 %all-to-all-start.1 = ((bf16[8,96,768]{2,1,0:T(8,128)(2,1)}), bf16[8,96,768]{2,1,0:T(8,128)(2,1)S(1)}, u32[]{:S(2)}, u32[]{:S(2)}) async-start(bf16[8,96,768]{2,1,0:T(8,128)(2,1)} %encode.2), calls=%async_computation.1 | async-start | bytes 2359296 | tf_op jit(solution)/shard_map/all_to_all | solution.py:1032
  14.2 9.0 %self_forward.2 = (bf16[2,448,768]{2,1,0:T(8,128)(2,1)}, bf16[2,3,448,192]{3,2,1,0:T(8,128)(2,1)}, bf16[448,192]{1,0:T(8,128)(2,1)}, bf16[448,192]{1,0:T(8,128)(2,1)}, f32[2,3,448]{2,1,0:T(4,128)}) custom-call(s32[2]{0:T(128)} %get-tuple-element.318.order, s32[4]{0:T(128)} %lengths.15, bf16[4,448,768]{2,1,0:T(8,128)(2,1)} %token_ref.7, f32[4,768]{1,0:T(4,128)} %gain_ref.20, ...), custom_call_target="tpu_custom_call" | custom-call | flops 1409286144 | bytes 5505024 | tf_op jit(solution)/shard_map/self_forward/pallas_call | solution.py:207
  23.1 9.2 %self_forward.3 = (bf16[2,448,768]{2,1,0:T(8,128)(2,1)}, bf16[2,3,448,192]{3,2,1,0:T(8,128)(2,1)}, bf16[448,192]{1,0:T(8,128)(2,1)}, bf16[448,192]{1,0:T(8,128)(2,1)}, f32[2,3,448]{2,1,0:T(4,128)}) custom-call(s32[2]{0:T(128)} %get-tuple-element.312.order, s32[4]{0:T(128)} %lengths.15, bf16[4,448,768]{2,1,0:T(8,128)(2,1)} %token_ref.7, f32[4,768]{1,0:T(4,128)} %gain_ref.20, ...), custom_call_target="tpu_custom_call" | custom-call | flops 1409286144 | bytes 5505024 | tf_op jit(solution)/shard_map/self_forward/pallas_call | solution.py:207
  34.9 6.4 %collective-permute-done.m2 = bf16[448,192]{1,0:T(8,128)(2,1)S(1)} collective-permute-done((bf16[448,192]{1,0:T(8,128)(2,1)S(1)}, bf16[448,192]{1,0:T(8,128)(2,1)S(1)}, u32[]{:S(2)}, u32[]{:S(2)}) %collective-permute-start) | collective-permute-done | bytes 172064 | tf_op jit(solution)/shard_map/ppermute | solution.py:78
  44.7 6.6 %all-to-all-start = ((bf16[8,96,768]{2,1,0:T(8,128)(2,1)}), bf16[8,96,768]{2,1,0:T(8,128)(2,1)S(1)}, u32[]{:S(2)}, u32[]{:S(2)}) async-start(bf16[8,96,768]{2,1,0:T(8,128)(2,1)} %encode.3), calls=%async_computation | async-start | bytes 2359296 | tf_op jit(solution)/shard_map/all_to_all | solution.py:1032
  53.6 7.1 %collective-permute-done.4.m3 = bf16[448,192]{1,0:T(8,128)(2,1)S(1)} collective-permute-done((bf16[448,192]{1,0:T(8,128)(2,1)S(1)}, bf16[448,192]{1,0:T(8,128)(2,1)S(1)}, u32[]{:S(2)}, u32[]{:S(2)}) %collective-permute-start.4) | collective-permute-done | bytes 172064 | tf_op jit(solution)/shard_map/ppermute | solution.py:78
  61.4 6.8 %self_out_to_query.1 = (f32[448,768]{1,0:T(8,128)}, bf16[448,768]{1,0:T(8,128)(2,1)}, bf16[2,448,384]{2,1,0:T(8,128)(2,1)}) custom-call(s32[4]{0:T(128)} %iota_xor_fusion.order, bf16[4,448,768]{2,1,0:T(8,128)(2,1)} %token_ref.7, bf16[448,192]{1,0:T(8,128)(2,1)} %get-tuple-element.220.m0.mixed1_ref, bf16[448,192]{1,0:T(8,128)(2,1)} %copy-done.36, ...), custom_call_target="tpu_custom_call" | custom-call | flops 1056964608 | bytes 6488064 | tf_op jit(solution)/shard_map/self_out_to_query/pallas_call | solution.py:334
  71.3 14.2 %cross_first.1 = (bf16[768,1536]{1,0:T(8,128)(2,1)}, f32[2,384,448]{2,1,0:T(8,128)}, f32[2,6,448]{2,1,0:T(8,128)}, f32[2,6,448]{2,1,0:T(8,128)}) custom-call(bf16[2,448,384]{2,1,0:T(8,128)(2,1)} %get-tuple-element.230.query_ref, bf16[768,768]{1,0:T(8,128)(2,1)} %bitcast.75, bf16[384,768]{1,0:T(8,128)(2,1)} %bitcast.5.w0, bf16[384,768]{1,0:T(8,128)(2,1)} %copy-done.51, ...), custom_call_target="tpu_custom_call" | custom-call | flops 7096762368 | bytes 4718592 | tf_op jit(solution)/shard_map/cross_first/pallas_call | solution.py:438
  88.3 18.4 %cross_second.1 = (bf16[768,1536]{1,0:T(8,128)(2,1)}, bf16[2,448,384]{2,1,0:T(8,128)(2,1)}, f32[2,6,448]{2,1,0:T(8,128)}, f32[448,768]{1,0:T(8,128)}, bf16[448,768]{1,0:T(8,128)(2,1)}) custom-call(bf16[2,448,384]{2,1,0:T(8,128)(2,1)} %get-tuple-element.230.query_ref, bf16[768,768]{1,0:T(8,128)(2,1)} %bitcast.77, bf16[384,768]{1,0:T(8,128)(2,1)} %bitcast.5.w0, ...), custom_call_target="tpu_custom_call" | custom-call | flops 7096762368 | bytes 5898240 | tf_op jit(solution)/shard_map/cross_second/pallas_call | solution.py:466
  110.0 10.2 %feed_forward.3 = (bf16[2,448,768]{2,1,0:T(8,128)(2,1)}, bf16[2,448,768]{2,1,0:T(8,128)(2,1)}, bf16[2,448,768]{2,1,0:T(8,128)(2,1)}, bf16[448,768]{1,0:T(8,128)(...) custom-call(s32[2]{0:T(128)} %bitcast.95, s32[4]{0:T(128)} %lengths.15, ...), custom_call_target="tpu_custom_call" | custom-call | flops 4227858432 | bytes 9633792 | tf_op jit(solution)/shard_map/feed_forward/pallas_call | solution.py:528
  127.8 6.8 %feed_forward.4 = (bf16[1,448,768]{2,1,0:T(8,128)(2,1)}, bf16[1,448,768]{2,1,0:T(8,128)(2,1)}, bf16[1,448,768]{2,1,0:T(8,128)(2,1)}, bf16[448,768]{1,0:T(8,128)(2,1)}, bf16[448,768]{1,0:T(8,128)(2,1)}) custom-call(s32[1]{0:T(128)} %get-tuple-element.443.order, s32[4]{0:T(128)} %lengths.15, bf16[448,768]{1,0:T(8,128)(2,1)} %copy-done.48, ...), custom_call_target="tpu_custom_call" | custom-call | flops 2113929216 | bytes 4816896 | tf_op jit(solution)/shard_map/feed_forward/pallas_call | solution.py:528
  135.7 6.7 %feed_forward.5 = (bf16[1,448,768]{2,1,0:T(8,128)(2,1)}, bf16[1,448,768]{2,1,0:T(8,128)(2,1)}, bf16[1,448,768]{2,1,0:T(8,128)(2,1)}, bf16[448,768]{1,0:T(8,128)(2,1)}, bf16[448,768]{1,0:T(8,128)(2,1)}) custom-call(s32[1]{0:T(128)} %get-tuple-element.243.order, s32[4]{0:T(128)} %lengths.15, bf16[448,768]{1,0:T(8,128)(2,1)} %copy-done.47, ...), custom_call_target="tpu_custom_call" | custom-call | flops 2113929216 | bytes 4816896 | tf_op jit(solution)/shard_map/feed_forward/pallas_call | solution.py:528
  144.9 11.4 %feed_weight_grads.1 = (bf16[2,4,96,768]{3,2,1,0:T(8,128)(2,1)}, bf16[2,4,96,768]{3,2,1,0:T(8,128)(2,1)}) custom-call(s32[8]{0:T(128)} %shift-right-arithmetic_and_fusion.bits, bf16[448,768]{1,0:T(8,128)(2,1)} %get-tuple-element.239.refs_0_, bf16[448,768]{1,0:T(8,128)(2,1)} %copy-done.45, bf16[448,768]{1,0:T(8,128)(2,1)} %copy-done.47, ...), custom_call_target="tpu_custom_call" | custom-call | flops 4227858432 | bytes 8257536 | tf_op jit(solution)/shard_map/feed_weight_grads/pallas_call | solution.py:784
  162.1 24.4 %cross_first_back.1 = (f32[448,768]{1,0:T(8,128)}, bf16[448,768]{1,0:T(8,128)(2,1)}, bf16[2,448,384]{2,1,0:T(8,128)(2,1)}, f32[1,768]{1,0:T(1,128)}, f32[2,384,4...) custom-call(s32[4]{0:T(128)} %iota_xor_fusion.order, s32[4]{0:T(128)} %lengths.15, ...), custom_call_target="tpu_custom_call" | custom-call | flops 17666408448 | bytes 11796480 | tf_op jit(solution)/shard_map/cross_first_back/pallas_call | solution.py:624
  186.5 6.6 %all-to-all-start.2 = ((bf16[8,96,768]{2,1,0:T(8,128)(2,1)}), bf16[8,96,768]{2,1,0:T(8,128)(2,1)S(1)}, u32[]{:S(2)}, u32[]{:S(2)}) async-start(bf16[8,96,768]{2,1,0:T(8,128)(2,1)} %bitcast.79), calls=%async_computation.2 | async-start | bytes 2359296 | tf_op jit(solution)/shard_map/all_to_all | solution.py:1106
  201.4 25.2 %cross_second_back.1 = (bf16[2,448,384]{2,1,0:T(8,128)(2,1)}, bf16[768,1536]{1,0:T(8,128)(2,1)}, bf16[768,768]{1,0:T(8,128)(2,1)}, f32[448,768]{1,0:T(8,128)}, b...) custom-call(bf16[2,448,384]{2,1,0:T(8,128)(2,1)} %get-tuple-element., ...), custom_call_target="tpu_custom_call" | custom-call | flops 17666408448 | bytes 11796480 | tf_op jit(solution)/shard_map/cross_second_back/pallas_call | solution.py:696
  247.6 4.8 %all-to-all-start.3 = ((bf16[8,96,768]{2,1,0:T(8,128)(2,1)}), bf16[8,96,768]{2,1,0:T(8,128)(2,1)}, u32[]{:S(2)}, u32[]{:S(2)}) async-start(bf16[8,96,768]{2,1,0:T(8,128)(2,1)} %bitcast.12), calls=%async_computation.3 | async-start | bytes 2359296 | tf_op jit(solution)/shard_map/all_to_all | solution.py:1106
  252.6 12.1 %head_weight_grads.1 = (bf16[2,768,768]{2,1,0:T(8,128)(2,1)}, bf16[2,768,768]{2,1,0:T(8,128)(2,1)}) custom-call(bf16[768,768]{1,0:T(8,128)(2,1)} %bitcast.76, bf16[768,768]{1,0:T(8,128)(2,1)} %bitcast.78, bf16[768,1536]{1,0:T(8,128)(2,1)} %get-tuple-element.267.dkv0, bf16[768,1536]{1,0:T(8,128)(2,1)} %get-tuple-element.291.dkv1, ...), custom_call_target="tpu_custom_call" | custom-call | flops 234042163200 | bytes 353894400 | tf_op jit(solution)/shard_map/head_weight_grads/pallas_call | solution.py:817
  265.4 9.2 %self_backward.2 = (bf16[2,3,448,192]{3,2,1,0:T(8,128)(2,1)}, bf16[448,768]{1,0:T(8,128)(2,1)}, bf16[448,768]{1,0:T(8,128)(2,1)}) custom-call(s32[2]{0:T(128)} %get-tuple-element.312.order, s32[4]{0:T(128)} %lengths.15, bf16[2,3,448,192]{3,2,1,0:T(8,128)(2,1)} %get-tuple-element.313.qkv_ref, bf16[448,192]{1,0:T(8,128)(2,1)} %get-tuple-element.223.mixed0_ref, ...), custom_call_target="tpu_custom_call" | custom-call | flops 2334 | bytes 5 | tf_op jit(solution)/shard_map/self_backward/pallas_call | solution.py:292
  274.6 9.2 %self_backward.3 = (bf16[2,3,448,192]{3,2,1,0:T(8,128)(2,1)}, bf16[448,768]{1,0:T(8,128)(2,1)}, bf16[448,768]{1,0:T(8,128)(2,1)}) custom-call(s32[2]{0:T(128)} %get-tuple-element.318.order, s32[4]{0:T(128)} %lengths.15, bf16[2,3,448,192]{3,2,1,0:T(8,128)(2,1)} %get-tuple-element.319.qkv_ref, bf16[448,192]{1,0:T(8,128)(2,1)} %get-tuple-element.224.mixed0_ref, ...), custom_call_target="tpu_custom_call" | custom-call | flops 2334 | bytes 5 | tf_op jit(solution)/shard_map/self_backward/pallas_call | solution.py:292
  302.8 7.3 %self_weight_grads.1 = (bf16[4,96,768]{2,1,0:T(8,128)(2,1)}, bf16[4,96,768]{2,1,0:T(8,128)(2,1)}) custom-call(s32[8]{0:T(128)} %shift-right-arithmetic_and_fusion.bits, bf16[2,448,768]{2,1,0:T(8,128)(2,1)} %get-tuple-element.345.near, bf16[2,448,768]{2,1,0:T(8,128)(2,1)} %get-tuple-element.346.far, bf16[2,3,448,192]{3,2,1,0:T(8,128)(2,1)} %get-tuple-element.347.dnear, ...), custom_call_target="tpu_custom_call" | custom-call | flops 79272345600 | bytes 275251200 | tf_op jit(solution)/shard_map/self_weight_grads/pallas_call | solution.py:868
  310.8 5.8 %collective-permute-done.40.far_ref = bf16[448,768]{1,0:T(8,128)(2,1)S(1)} collective-permute-done((bf16[448,768]{1,0:T(8,128)(2,1)S(1)}, bf16[448,768]{1,0:T(8,128)(2,1)S(1)}, u32[]{:S(2)}, u32[]{:S(2)}) %collective-permute-start.40) | collective-permute-done | bytes 688160 | tf_op jit(solution)/shard_map/ppermute | solution.py:78
  343.2 4.8 %collective-permute-done.48 = bf16[2,1,96,768]{3,2,0,1:T(8,128)(2,1)S(1)} collective-permute-done((bf16[2,1,96,768]{3,2,0,1:T(8,128)(2,1)}, bf16[2,1,96,768]{3,2,0,1:T(8,128)(2,1)S(1)}, u32[]{:S(2)}, u32[]{:S(2)}) %collective-permute-start.48) | collective-permute-done | bytes 294944 | tf_op jit(solution)/shard_map/ppermute | solution.py:78
  370.1 6.7 %collective-permute-done.54 = bf16[3,1,96,768]{3,2,1,0:T(8,128)(2,1)S(1)} collective-permute-done((bf16[3,1,96,768]{3,2,1,0:T(8,128)(2,1)}, bf16[3,1,96,768]{3,2,1,0:T(8,128)(2,1)S(1)}, u32[]{:S(2)}, u32[]{:S(2)}) %collective-permute-start.54) | collective-permute-done | bytes 442400 | tf_op jit(solution)/shard_map/ppermute | solution.py:78
  (286 shorter events, 156.3 us)
Async XLA Ops:
  4.5 40.2 %all-to-all-start.1 = ((bf16[8,96,768]{2,1,0:T(8,128)(2,1)}), bf16[8,96,768]{2,1,0:T(8,128)(2,1)S(1)}, u32[]{:S(2)}, u32[]{:S(2)}) async-start(bf16[8,96,768]{2,1,0:T(8,128)(2,1)} %encode.2), calls=%async_computation.1 | async-start | bytes 2359296 | tf_op jit(solution)/shard_map/all_to_all | solution.py:1032
  13.6 47.1 %collective-permute-start.5 = (bf16[384,768]{1,0:T(8,128)(2,1)S(1)}, bf16[384,768]{1,0:T(8,128)(2,1)}, u32[]{:S(2)}, u32[]{:S(2)}) collective-permute-start(bf16[384,768]{1,0:T(8,128)(2,1)S(1)} %pad_maximum_fusion.p0), channel_id=1, source_target_pairs={{0,1},{1,0},{2,3},{3,2},{4,5},{5,4},{6,7},{7,6},{8,9},{9,8},{10,11... | collective-permute-start | bytes 1769480 | tf_op jit(solution)/shard_map/ppermute | solution.py:78
  32.3 28.4 %collective-permute-start.6 = (bf16[384,768]{1,0:T(8,128)(2,1)S(1)}, bf16[384,768]{1,0:T(8,128)(2,1)}, u32[]{:S(2)}, u32[]{:S(2)}) collective-permute-start(bf16[384,768]{1,0:T(8,128)(2,1)S(1)} %collective-permute-done.1.p2), channel_id=1, source_target_pairs={{0,1},{1,0},{2,3},{3,2},{4,5},{5,4},{6,7},{7,6},{8,9},{9,8},{10,11... | collective-permute-start | bytes 1769480 | tf_op jit(solution)/shard_map/ppermute | solution.py:78
  33.4 34.8 %collective-permute-start.8 = (bf16[384,768]{1,0:T(8,128)(2,1)}, bf16[384,768]{1,0:T(8,128)(2,1)}, u32[]{:S(2)}, u32[]{:S(2)}) collective-permute-start(bf16[384,768]{1,0:T(8,128)(2,1)} %bitcast.5.w0), channel_id=1, source_target_pairs={{0,2},{1,3},{2,0},{3,1},{4,6},{5,7},{6,4},{7,5},{8,10},{9,11},{10,... | collective-permute-start | bytes 1769480 | tf_op jit(solution)/shard_map/ppermute | solution.py:78
  44.7 42.4 %all-to-all-start = ((bf16[8,96,768]{2,1,0:T(8,128)(2,1)}), bf16[8,96,768]{2,1,0:T(8,128)(2,1)S(1)}, u32[]{:S(2)}, u32[]{:S(2)}) async-start(bf16[8,96,768]{2,1,0:T(8,128)(2,1)} %encode.3), calls=%async_computation | async-start | bytes 2359296 | tf_op jit(solution)/shard_map/all_to_all | solution.py:1032
  156.3 39.9 %collective-permute-start.22 = (bf16[2,4,96,768]{3,2,1,0:T(8,128)(2,1)}, bf16[2,4,96,768]{3,2,1,0:T(8,128)(2,1)}, u32[]{:S(2)}, u32[]{:S(2)}) collective-permute-start(bf16[2,4,96,768]{3,2,1,0:T(8,128)(2,1)} %get-tuple-element.258), channel_id=1, source_target_pairs={{0,4},{4,0},{8,12},{12,8},{16,20},{20,16},{24,28},{28,24},{1,5},{5... | collective-permute-start | bytes 3538952 | tf_op jit(solution)/shard_map/ppermute | solution.py:78
  161.3 31.9 %collective-permute-start.21 = (bf16[448,768]{1,0:T(8,128)(2,1)S(1)}, bf16[448,768]{1,0:T(8,128)(2,1)}, u32[]{:S(2)}, u32[]{:S(2)}) collective-permute-start(bf16[448,768]{1,0:T(8,128)(2,1)S(1)} %add_convert_fusion.2), channel_id=1, source_target_pairs={{0,2},{1,3},{2,0},{3,1},{4,6},{5,7},{6,4},{7,5},{8,10},{9,11},{10,... | collective-permute-start | bytes 2064392 | tf_op jit(solution)/shard_map/ppermute | solution.py:78
  186.5 51.4 %all-to-all-start.2 = ((bf16[8,96,768]{2,1,0:T(8,128)(2,1)}), bf16[8,96,768]{2,1,0:T(8,128)(2,1)S(1)}, u32[]{:S(2)}, u32[]{:S(2)}) async-start(bf16[8,96,768]{2,1,0:T(8,128)(2,1)} %bitcast.79), calls=%async_computation.2 | async-start | bytes 2359296 | tf_op jit(solution)/shard_map/all_to_all | solution.py:1106
  195.0 31.7 %collective-permute-start.25 = (bf16[448,768]{1,0:T(8,128)(2,1)S(1)}, bf16[448,768]{1,0:T(8,128)(2,1)}, u32[]{:S(2)}, u32[]{:S(2)}) collective-permute-start(bf16[448,768]{1,0:T(8,128)(2,1)S(1)} %add_convert_fusion.1.a), channel_id=1, source_target_pairs={{0,2},{1,3},{2,0},{3,1},{4,6},{5,7},{6,4},{7,5},{8,10},{9,11},{10,... | collective-permute-start | bytes 2064392 | tf_op jit(solution)/shard_map/ppermute | solution.py:78
  196.2 30.5 %collective-permute-start.24 = (bf16[448,768]{1,0:T(8,128)(2,1)S(1)}, bf16[448,768]{1,0:T(8,128)(2,1)S(1)}, u32[]{:S(2)}, u32[]{:S(2)}) collective-permute-start(bf16[448,768]{1,0:T(8,128)(2,1)S(1)} %add_convert_fusion.1.a), channel_id=1, source_target_pairs={{0,1},{1,0},{2,3},{3,2},{4,5},{5,4},{6,7},{7,6},{8,9},{9,8},{10,11... | collective-permute-start | bytes 2064392 | tf_op jit(solution)/shard_map/ppermute | solution.py:78
  199.4 27.2 %collective-permute-start.23 = (bf16[4,1,96,768]{3,2,1,0:T(8,128)(2,1)}, bf16[4,1,96,768]{3,2,1,0:T(8,128)(2,1)S(1)}, u32[]{:S(2)}, u32[]{:S(2)}) collective-permute-start(bf16[4,1,96,768]{3,2,1,0:T(8,128)(2,1)} %get-tuple-element.281), channel_id=1, source_target_pairs={{0,8},{4,12},{8,0},{12,4},{16,24},{20,28},{24,16},{28,20},{1,9},{5... | collective-permute-start | bytes 1769480 | tf_op jit(solution)/shard_map/ppermute | solution.py:78
  238.0 26.8 %collective-permute-start.31 = (bf16[448,768]{1,0:T(8,128)(2,1)}, bf16[448,768]{1,0:T(8,128)(2,1)}, u32[]{:S(2)}, u32[]{:S(2)}) collective-permute-start(bf16[448,768]{1,0:T(8,128)(2,1)} %collective-permute-done.25.c), channel_id=1, source_target_pairs={{0,1},{1,0},{2,3},{3,2},{4,5},{5,4},{6,7},{7,6},{8,9},{9,8},{10,11... | collective-permute-start | bytes 2064392 | tf_op jit(solution)/shard_map/ppermute | solution.py:78
  246.7 37.1 %collective-permute-start.34 = (bf16[8,96,768]{2,1,0:T(8,128)(2,1)}, bf16[8,96,768]{2,1,0:T(8,128)(2,1)}, u32[]{:S(2)}, u32[]{:S(2)}) collective-permute-start(bf16[8,96,768]{2,1,0:T(8,128)(2,1)} %get-tuple-element.391.a), channel_id=1, source_target_pairs={{0,2},{1,3},{2,0},{3,1},{4,6},{5,7},{6,4},{7,5},{8,10},{9,11},{10,... | collective-permute-start | bytes 3538952 | tf_op jit(solution)/shard_map/ppermute | solution.py:78
  247.6 36.2 %collective-permute-start.33 = (bf16[8,96,768]{2,1,0:T(8,128)(2,1)}, bf16[8,96,768]{2,1,0:T(8,128)(2,1)}, u32[]{:S(2)}, u32[]{:S(2)}) collective-permute-start(bf16[8,96,768]{2,1,0:T(8,128)(2,1)} %get-tuple-element.391.a), channel_id=1, source_target_pairs={{0,1},{1,0},{2,3},{3,2},{4,5},{5,4},{6,7},{7,6},{8,9},{9,8},{10,11... | collective-permute-start | bytes 3538952 | tf_op jit(solution)/shard_map/ppermute | solution.py:78
  247.6 36.3 %all-to-all-start.3 = ((bf16[8,96,768]{2,1,0:T(8,128)(2,1)}), bf16[8,96,768]{2,1,0:T(8,128)(2,1)}, u32[]{:S(2)}, u32[]{:S(2)}) async-start(bf16[8,96,768]{2,1,0:T(8,128)(2,1)} %bitcast.12), calls=%async_computation.3 | async-start | bytes 2359296 | tf_op jit(solution)/shard_map/all_to_all | solution.py:1106
  264.8 26.6 %collective-permute-start.37 = (bf16[2,768,768]{2,1,0:T(8,128)(2,1)}, bf16[2,768,768]{2,1,0:T(8,128)(2,1)S(1)}, u32[]{:S(2)}, u32[]{:S(2)}) collective-permute-start(bf16[2,768,768]{2,1,0:T(8,128)(2,1)} %get-tuple-element.311), channel_id=1, source_target_pairs={{0,1},{1,0},{2,3},{3,2},{4,5},{5,4},{6,7},{7,6},{8,9},{9,8},{10,11... | collective-permute-start | bytes 7077896 | tf_op jit(solution)/shard_map/ppermute | solution.py:78
  297.4 26.6 %collective-permute-start.41 = (bf16[4,96,768]{2,1,0:T(8,128)(2,1)}, bf16[4,96,768]{2,1,0:T(8,128)(2,1)S(1)}, u32[]{:S(2)}, u32[]{:S(2)}) collective-permute-start(bf16[4,96,768]{2,1,0:T(8,128)(2,1)} %get-tuple-element.341), channel_id=1, source_target_pairs={{0,4},{4,0},{8,12},{12,8},{16,20},{20,16},{24,28},{28,24},{1,5},{5... | collective-permute-start | bytes 1769480 | tf_op jit(solution)/shard_map/ppermute | solution.py:78
  300.6 22.8 %collective-permute-start.42 = (bf16[4,96,768]{2,1,0:T(8,128)(2,1)S(1)}, bf16[4,96,768]{2,1,0:T(8,128)(2,1)S(1)}, u32[]{:S(2)}, u32[]{:S(2)}) collective-permute-start(bf16[4,96,768]{2,1,0:T(8,128)(2,1)S(1)} %copy-done.54), channel_id=1, source_target_pairs={{0,8},{4,12},{8,0},{12,4},{16,24},{20,28},{24,16},{28,20},{1,9},{5... | collective-permute-start | bytes 1769480 | tf_op jit(solution)/shard_map/ppermute | solution.py:78
  310.1 22.8 %collective-permute-start.44 = (bf16[4,96,768]{2,1,0:T(8,128)(2,1)}, bf16[4,96,768]{2,1,0:T(8,128)(2,1)S(1)}, u32[]{:S(2)}, u32[]{:S(2)}) collective-permute-start(bf16[4,96,768]{2,1,0:T(8,128)(2,1)} %get-tuple-element.349), channel_id=1, source_target_pairs={{0,4},{4,0},{8,12},{12,8},{16,20},{20,16},{24,28},{28,24},{1,5},{5... | collective-permute-start | bytes 1769480 | tf_op jit(solution)/shard_map/ppermute | solution.py:78
  321.8 30.0 %collective-permute-start.51 = (bf16[448,768]{1,0:T(8,128)(2,1)}, bf16[448,768]{1,0:T(8,128)(2,1)S(1)}, u32[]{:S(2)}, u32[]{:S(2)}) collective-permute-start(bf16[448,768]{1,0:T(8,128)(2,1)} %get-tuple-element.402.a), channel_id=1, source_target_pairs={{0,2},{1,3},{2,0},{3,1},{4,6},{5,7},{6,4},{7,5},{8,10},{9,11},{10,... | collective-permute-start | bytes 2064392 | tf_op jit(solution)/shard_map/ppermute | solution.py:78
  322.7 29.2 %collective-permute-start.50 = (bf16[448,768]{1,0:T(8,128)(2,1)}, bf16[448,768]{1,0:T(8,128)(2,1)S(1)}, u32[]{:S(2)}, u32[]{:S(2)}) collective-permute-start(bf16[448,768]{1,0:T(8,128)(2,1)} %get-tuple-element.402.a), channel_id=1, source_target_pairs={{0,1},{1,0},{2,3},{3,2},{4,5},{5,4},{6,7},{7,6},{8,9},{9,8},{10,11... | collective-permute-start | bytes 2064392 | tf_op jit(solution)/shard_map/ppermute | solution.py:78
  352.8 24.5 %collective-permute-start.56 = (bf16[8,96,768]{2,1,0:T(8,128)(2,1)S(1)}, bf16[8,96,768]{2,1,0:T(8,128)(2,1)S(1)}, u32[]{:S(2)}, u32[]{:S(2)}) collective-permute-start(bf16[8,96,768]{2,1,0:T(8,128)(2,1)S(1)} %copy-done.5), channel_id=1, source_target_pairs={{0,2},{1,3},{2,0},{3,1},{4,6},{5,7},{6,4},{7,5},{8,10},{9,11},{10,... | collective-permute-start | bytes 3538952 | tf_op jit(solution)/shard_map/ppermute | solution.py:78
  353.7 23.6 %collective-permute-start.55 = (bf16[8,96,768]{2,1,0:T(8,128)(2,1)S(1)}, bf16[8,96,768]{2,1,0:T(8,128)(2,1)}, u32[]{:S(2)}, u32[]{:S(2)}) collective-permute-start(bf16[8,96,768]{2,1,0:T(8,128)(2,1)S(1)} %copy-done.5), channel_id=1, source_target_pairs={{0,1},{1,0},{2,3},{3,2},{4,5},{5,4},{6,7},{7,6},{8,9},{9,8},{10,11... | collective-permute-start | bytes 3538952 | tf_op jit(solution)/shard_map/ppermute | solution.py:78
  354.2 22.7 %collective-permute-start.54 = (bf16[3,1,96,768]{3,2,1,0:T(8,128)(2,1)}, bf16[3,1,96,768]{3,2,1,0:T(8,128)(2,1)S(1)}, u32[]{:S(2)}, u32[]{:S(2)}) collective-permute-start(bf16[3,1,96,768]{3,2,1,0:T(8,128)(2,1)} %get-tuple-element.389), channel_id=1, source_target_pairs={{0,16},{4,20},{8,24},{12,28},{16,0},{20,4},{24,8},{28,12},{1,17},{... | collective-permute-start | bytes 1327112 | tf_op jit(solution)/shard_map/ppermute | solution.py:78
  (101 other events, 858.4 us)

commit v4 on v3

--- a/solution.py
+++ b/solution.py
@@ -108,7 +108,7 @@
     out_ref[...] = (unit * gain_ref[0 : 1]).astype(BF16)
 
 
-def encode(order, memory, gains_all, start, size):
+def encode(order, memory, gains_all, start, size, scale=None):
     wide, _, _, width = memory.shape
     group = min(4, wide)
     return call(
@@ -121,7 +121,7 @@
         pl.BlockSpec((group, size, width), lambda i, *_: (i, 0, 0)),
         shape((wide, size, width)),
         "encode",
-        cost(0, 4 * wide * size * width),
+        cost(0, 4 * wide * size * width, scale=scale),
         prefetch=1,
     )(order, memory, gains_all)
 
@@ -200,7 +200,7 @@
         second_ref[...] = mixed
 
 
-def self_fwd(order, lengths, tokens, gains_all, weights):
+def self_fwd(order, lengths, tokens, gains_all, weights, scale=None):
     _, seq, width = tokens.shape
     local = weights.shape[1]
     heads = local // HEAD_DIM
@@ -227,54 +227,58 @@
             shape((2, heads, seq), F32),
         ],
         "self_forward",
-        cost(2 * (6 * seq * width * local + 8 * seq * seq * local), 2 * seq * width * 8, 2 * heads * seq * seq),
+        cost(2 * (6 * seq * width * local + 8 * seq * seq * local), 2 * seq * width * 8, 2 * heads * seq * seq, scale=scale),
         prefetch=2,
     )(order, lengths, tokens, gains_all, weights)
 
 
-def self_bwd_body(order, lengths, qkv_ref, mixed0_ref, mixed1_ref, lse_ref, grad0_ref, grad1_ref, weight_ref, dqkv_ref, first_ref, second_ref):
+def self_bwd_body(
+    order, lengths, qkv_ref, mixed0_ref, mixed1_ref, lse_ref, grad0_ref, grad1_ref, weight_ref,
+    dq_ref, dkv_ref, first_ref, second_ref,
+):
     seq = qkv_ref.shape[2]
-    heads = weight_ref.shape[1] // HEAD_DIM
+    local = weight_ref.shape[1]
+    heads = local // HEAD_DIM
     step = pl.program_id(0)
     length = lengths[order[step]]
     grad = jnp.where(step == 0, grad0_ref[...], grad1_ref[...])
     mixed = jnp.where(step == 0, mixed0_ref[...], mixed1_ref[...])
-    inner = (grad.astype(F32) * mixed.astype(F32)).T
+    inner = grad.astype(F32) * mixed.astype(F32)
+    totals = jnp.concatenate((lse_ref[0], jnp.zeros((8 - heads % 8, seq), F32)), axis=0).T
     cut = 256 if seq > 256 else seq
     for h in range(heads):
         columns = slice(h * HEAD_DIM, (h + 1) * HEAD_DIM)
         keys = qkv_ref[0, 1, :, columns]
         values = qkv_ref[0, 2, :, columns]
         dq_parts = []
-        dk = jnp.zeros((seq, HEAD_DIM), F32)
-        dv = jnp.zeros((seq, HEAD_DIM), F32)
+        dk, dv = 0.0, 0.0
         for start, stop in ((0, cut), (cut, seq)):
             if start == stop:
                 continue
             queries = qkv_ref[0, 0, start:stop, columns] * jnp.asarray(INV_ROOT, BF16)
             grads = grad[start:stop, columns]
-            scores = dot(keys[:stop], queries, 1, 1)
-            key = lax.broadcasted_iota(jnp.int32, scores.shape, 0)
-            query = lax.broadcasted_iota(jnp.int32, scores.shape, 1) + start
+            scores = dot(queries, keys[:stop], 1, 1)
+            key = lax.broadcasted_iota(jnp.int32, scores.shape, 1)
+            query = lax.broadcasted_iota(jnp.int32, scores.shape, 0) + start
             allowed = (key <= query) & (key < length)
-            probs = jnp.exp(jnp.where(allowed, scores, NEG_FILL) - lse_ref[0, h : h + 1, start:stop])
-            dp = dot(values[:stop], grads, 1, 1)
-            centre = jnp.sum(inner[columns, start:stop], axis=0, keepdims=True)
+            probs = jnp.exp(jnp.where(allowed, scores, NEG_FILL) - totals[start:stop, h : h + 1])
+            dp = dot(grads, values[:stop], 1, 1)
+            centre = jnp.sum(inner[start:stop, columns], axis=1, keepdims=True)
             ds = (probs * (dp - centre)).astype(BF16)
-            dk_now = dot(ds, queries)
-            dv_now = dot(probs.astype(BF16), grads)
+            dk_now = dot(queries, ds, 0, 0)
+            dv_now = dot(grads, probs.astype(BF16), 0, 0)
             if stop < seq:
-                pad = jnp.zeros((seq - stop, HEAD_DIM), F32)
-                dk_now = jnp.concatenate((dk_now, pad), axis=0)
-                dv_now = jnp.concatenate((dv_now, pad), axis=0)
+                pad = jnp.zeros((HEAD_DIM, seq - stop), F32)
+                dk_now = jnp.concatenate((dk_now, pad), axis=1)
+                dv_now = jnp.concatenate((dv_now, pad), axis=1)
             dk, dv = dk + dk_now, dv + dv_now
-            dq_parts.append((dot(keys[:stop], ds, 0, 0) * INV_ROOT).T)
-        dqkv_ref[0, 0, :, columns] = jnp.concatenate(dq_parts, axis=0).astype(BF16)
-        dqkv_ref[0, 1, :, columns] = dk.astype(BF16)
-        dqkv_ref[0, 2, :, columns] = dv.astype(BF16)
-    total = dot(dqkv_ref[0, 0], weight_ref[0])
-    total = total + dot(dqkv_ref[0, 1], weight_ref[1])
-    total = (total + dot(dqkv_ref[0, 2], weight_ref[2])).astype(BF16)
+            dq_parts.append(dot(ds, keys[:stop]) * INV_ROOT)
+        dq_ref[0, :, columns] = jnp.concatenate(dq_parts, axis=0).astype(BF16)
+        dkv_ref[0, columns, :] = dk.astype(BF16)
+        dkv_ref[0, local + h * HEAD_DIM : local + (h + 1) * HEAD_DIM, :] = dv.astype(BF16)
+    total = dot(dq_ref[0], weight_ref[0])
+    total = total + dot(dkv_ref[0, :local, :], weight_ref[1], 0, 0)
+    total = (total + dot(dkv_ref[0, local:, :], weight_ref[2], 0, 0)).astype(BF16)
 
     @pl.when(step == 0)
     def _():
@@ -302,11 +306,12 @@
             whole((3, local, width)),
         ],
         [
-            pl.BlockSpec((1, 3, seq, local), lambda i, *_: (i, 0, 0, 0)),
+            pl.BlockSpec((1, seq, local), lambda i, *_: (i, 0, 0)),
+            pl.BlockSpec((1, 2 * local, seq), lambda i, *_: (i, 0, 0)),
             whole((seq, width)),
             whole((seq, width)),
         ],
-        [shape((2, 3, seq, local)), shape((seq, width)), shape((seq, width))],
+        [shape((2, seq, local)), shape((2, 2 * local, seq)), shape((seq, width)), shape((seq, width))],
         "self_backward",
         cost(2 * (6 * seq * width * local + 20 * seq * seq * local), 2 * seq * width * 8, 2 * heads * seq * seq, scale=scale),
         prefetch=2,
@@ -553,21 +558,23 @@
 
 def cross_back(queries_ref, kv_ref, grads_ref, mixed_ref, lse_ref, dkv_ref, local, valid, store):
     frames = kv_ref.shape[0]
-    inner = (grads_ref.astype(F32) * mixed_ref[0].astype(F32)).T
+    inner = grads_ref.astype(F32) * mixed_ref[0].astype(F32)
+    heads, seq = lse_ref.shape[1:]
+    totals = jnp.concatenate((lse_ref[0], jnp.zeros((8 - heads % 8, seq), F32)), axis=0).T
     for head, columns, key, value in head_places(local):
         queries = queries_ref[0, :, columns] * jnp.asarray(INV_ROOT, BF16)
         grads = grads_ref[:, columns]
-        centre = jnp.sum(inner[columns, :], axis=0, keepdims=True)
+        centre = jnp.sum(inner[:, columns], axis=1, keepdims=True)
         keys = kv_ref[:, key]
-        probs = jnp.exp(dot(keys, queries, 1, 1) - lse_ref[0, head : head + 1, :])
+        probs = jnp.exp(dot(queries, keys, 1, 1) - totals[:, head : head + 1])
         if valid < frames:
-            frame = lax.broadcasted_iota(jnp.int32, probs.shape, 0)
+            frame = lax.broadcasted_iota(jnp.int32, probs.shape, 1)
             probs = jnp.where(frame < valid, probs, 0.0)
-        dp = dot(kv_ref[:, value], grads, 1, 1)
+        dp = dot(grads, kv_ref[:, value], 1, 1)
         ds = (probs * (dp - centre)).astype(BF16)
-        dkv_ref[:, value] = dot(probs.astype(BF16), grads).astype(BF16)
-        dkv_ref[:, key] = dot(ds, queries).astype(BF16)
-        store(columns, dot(keys, ds, 0, 0))
+        dkv_ref[value, :] = dot(grads, probs.astype(BF16), 0, 0).astype(BF16)
+        dkv_ref[key, :] = dot(queries, ds, 0, 0).astype(BF16)
+        store(columns, dot(ds, keys))
 
 
 def encoded_back(dkv_ref, weights, out_ref, acc):
@@ -576,7 +583,8 @@
 
         @pl.when(pl.program_id(0) == step)
         def _():
-            total = dot(dkv_ref[:, :pair], weights[2 * step][...]) + dot(dkv_ref[:, pair:], weights[2 * step + 1][...])
+            total = dot(dkv_ref[:pair, :], weights[2 * step][...], 0, 0)
+            total = total + dot(dkv_ref[pair:, :], weights[2 * step + 1][...], 0, 0)
             if step == 0:
                 acc[...] = total
             else:
@@ -607,7 +615,7 @@
         gain_out[...] = jnp.sum(normed_grad * unit, axis=0, keepdims=True)
 
     def store(columns, dq):
-        dq_ref[0, columns, :] = dq
+        dq_ref[0, :, columns] = dq
 
     cross_back(query_ref, kv_ref, grads_ref[step], mixed_ref, lse_ref, dkv_ref, local, valid, store)
     encoded_back(dkv_ref, (w0, w1, w2, w3), encoded_ref, acc)
@@ -634,8 +642,8 @@
             rows,
             whole((2, seq, pair)),
             whole((1, width)),
-            pl.BlockSpec((1, pair, seq), lambda i, *_: (i, 0, 0)),
-            both,
+            head_rows,
+            pl.BlockSpec((2 * pair, frames), lambda i, *_: (i, 0)),
             whole((frames, width)),
         ],
         [
@@ -643,8 +651,8 @@
             shape((seq, width)),
             shape((2, seq, pair)),
             shape((1, width), F32),
-            shape((2, pair, seq), F32),
-            shape((frames, 2 * width)),
+            shape((2, seq, pair), F32),
+            shape((2 * width, frames)),
             shape((frames, width)),
         ],
         "cross_first_back",
@@ -663,7 +671,7 @@
     step = pl.program_id(0)
 
     def store(columns, dq):
-        dq_ref[step, :, columns] = ((dq + dq_in[0, columns, :]) * INV_ROOT).T.astype(BF16)
+        dq_ref[step, :, columns] = ((dq + dq_in[0, :, columns]) * INV_ROOT).astype(BF16)
 
     cross_back(query_ref, kv_ref, grads_ref[0], mixed_ref, lse_ref, dkv_ref, local, valid, store)
     encoded_back(dkv_ref, (w0, w1, w2, w3), encoded_ref, acc)
@@ -697,16 +705,16 @@
         functools.partial(cross_second_back_body, valid=valid),
         (2,),
         [head_rows, both, head_rows, head_rows, pl.BlockSpec((1, heads, seq), lambda i: (i, 0, 0))]
-        + [pl.BlockSpec((1, pair, seq), lambda i: (i, 0, 0))]
+        + [head_rows]
         + pack_specs(packs_two, pair, 0)
         + pack_specs(packs_one, pair, 0)
         + [rows, whole(gains_all.shape), rows],
-        [whole((2, seq, pair)), both, whole((frames, width)), rows, rows]
+        [whole((2, seq, pair)), pl.BlockSpec((2 * pair, frames), lambda i: (i, 0)), whole((frames, width)), rows, rows]
         + [whole((seq, local))] * 4
         + [whole((1, width))],
         [
             shape((2, seq, pair)),
-            shape((frames, 2 * width)),
+            shape((2 * width, frames)),
             shape((frames, width)),
             shape((seq, width), F32),
             shape((seq, width)),
@@ -795,36 +803,35 @@
     )(bits, *rows, *pres, *lives, *hiddens)
 
 
-def head_weights_body(enc0, enc1, dkv0, dkv1, two, dq_ref, grad_two, cross_mixed, keep_ref, give_ref):
+def head_weights_body(enc0, enc1, dkv0, dkv1, two, grad_two, dq_ref, cross_mixed, keep_ref, give_ref):
     local = dq_ref.shape[2] // 2
-    for r in range(4):
-        out = (keep_ref, give_ref)[r % 2]
-        columns = slice((r % 2) * local, (r % 2 + 1) * local)
+    for r, out in enumerate((keep_ref, give_ref)):
+        columns = slice(r * local, (r + 1) * local)
         pair = slice(2 * r * local, 2 * (r + 1) * local)
-        kv = dot(enc0[...], dkv0[:, pair], 0, 0) + dot(enc1[...], dkv1[:, pair], 0, 0)
-        out[r // 2, :, : 2 * local] = kv.astype(BF16)
-        query = dot(two[...], dq_ref[r // 2, :, columns], 0, 0)
-        cross = dot(grad_two[...], cross_mixed[r // 2, :, columns], 0, 0)
-        out[r // 2, :, 2 * local :] = jnp.concatenate((query, cross), axis=1).astype(BF16)
+        kv = dot(dkv0[pair, :], enc0[...]) + dot(dkv1[pair, :], enc1[...])
+        out[0, :, : 2 * local] = kv.T.astype(BF16)
+        query = dot(two[...], dq_ref[0, :, columns], 0, 0)
+        cross = dot(grad_two[...], cross_mixed[0, :, columns], 0, 0)
+        out[0, :, 2 * local :] = jnp.concatenate((query, cross), axis=1).astype(BF16)
 
 
 def head_weights(encs, dkvs, normed_two, dq, grad_two, cross_mixed, scale):
     seq, width = normed_two.shape
-    tile = width // 2
-    rows = pl.BlockSpec((seq, tile), lambda i: (0, i))
-    out = pl.BlockSpec((2, tile, width), lambda i: (0, i, 0))
+    heads = pl.BlockSpec((1, seq, width // 2), lambda i: (i, 0, 0))
+    out = pl.BlockSpec((1, width, width), lambda i: (i, 0, 0))
     frames = encs[0].shape[0] + encs[1].shape[0]
     return call(
         head_weights_body,
         (2,),
-        [pl.BlockSpec((item.shape[0], tile), lambda i: (0, i)) for item in encs]
-        + [whole(item.shape) for item in dkvs]
-        + [rows, whole(dq.shape), rows, whole(cross_mixed.shape)],
+        [whole(item.shape) for item in encs]
+        + [pl.BlockSpec((width, item.shape[1]), lambda i: (i, 0)) for item in dkvs]
+        + [whole((seq, width))] * 2
+        + [heads] * 2,
         [out, out],
         [shape((2, width, width))] * 2,
         "head_weight_grads",
         cost(4 * frames * width * width + 4 * seq * width * width, 6 * frames * width, scale=scale),
-    )(*encs, *dkvs, normed_two, dq, grad_two, cross_mixed)
+    )(*encs, *dkvs, normed_two, grad_two, dq, cross_mixed)
 
 
 def out_weights_body(one, m0, m1, m2, m3, keep_ref, give_ref):
@@ -846,20 +853,21 @@
     )(grad_one, *mixes)
 
 
-def self_weights_body(bits, near, far, dnear, dfar, own, core, other, keep_ref, give_ref, scratch):
-    totals = []
-    for i in range(3):
-        total = 0.0
+def self_weights_body(bits, near, far, dq_near, dkv_near, dq_far, dkv_far, own, core, other, keep_ref, give_ref, scratch):
+    local = dq_near.shape[2]
+    totals = [0.0, 0.0, 0.0]
+    for rows, dq, dkv in ((near, dq_near, dkv_near), (far, dq_far, dkv_far)):
         for c in range(2):
-            total = total + dot(near[c], dnear[c, i], 0, 0) + dot(far[c], dfar[c, i], 0, 0)
-        totals.append(total)
+            totals[0] = totals[0] + dot(rows[c], dq[c], 0, 0)
+            totals[1] = totals[1] + dot(rows[c], dkv[c, :local, :], 0, 1)
+            totals[2] = totals[2] + dot(rows[c], dkv[c, local:, :], 0, 1)
     totals.append((own[0].astype(F32) + core[0].astype(F32) + other[...].astype(F32)).T)
     split_store(jnp.concatenate(totals, axis=1), bits[0], keep_ref, give_ref, scratch)
 
 
-def self_weights(bits, near, far, dnear, dfar, own, core, other, wide, scale):
+def self_weights(bits, near, far, dq_near, dkv_near, dq_far, dkv_far, own, core, other, wide, scale):
     _, seq, width = near.shape
-    local = dnear.shape[3]
+    local = dq_near.shape[2]
     tile = width // 2
     depth = width // wide
     rows = pl.BlockSpec((2, seq, tile), lambda i, *_: (0, 0, i))
@@ -868,7 +876,7 @@
     return call(
         self_weights_body,
         (2,),
-        [rows, rows, whole(dnear.shape), whole(dfar.shape), turned, turned]
+        [rows, rows] + [whole(item.shape) for item in (dq_near, dkv_near, dq_far, dkv_far)] + [turned, turned]
         + [pl.BlockSpec((local, tile), lambda i, *_: (0, i))],
         [out, out],
         [shape((wide // 2, depth, 4 * local))] * 2,
@@ -876,7 +884,7 @@
         cost(24 * seq * width * local, 16 * seq * width, scale=scale),
         prefetch=1,
         scratch=[pltpu.VMEM((tile, 4 * local), F32)],
-    )(bits, near, far, dnear, dfar, own, core, other)
+    )(bits, near, far, dq_near, dkv_near, dq_far, dkv_far, own, core, other)
 
 
 def add_low(keep, got):
@@ -955,8 +963,56 @@
         then.last = keep
         which += 1
         got = swap(give, "wide", 1 << (which - 1))
-    view = (lead,) + dims
-    return keep.reshape(view).astype(F32) + got.reshape(view).astype(F32)
+    return keep.reshape((lead,) + dims), got.reshape((lead,) + dims)
+
+
+def finish_self_body(keep_ref, got_ref, give_ref, heads_ref, qkv_ref, out_ref):
+    local = out_ref.shape[0]
+    heads_ref[...] = keep_ref[0].astype(F32) + got_ref[0].astype(F32)
+    give_ref[...] = (keep_ref[1].astype(F32) + got_ref[1].astype(F32)).astype(BF16)
+    own = keep_ref[2].astype(F32) + got_ref[2].astype(F32)
+    for i in range(3):
+        qkv_ref[i] = own[:, i * local : (i + 1) * local]
+    out_ref[...] = own[:, 3 * local :].T
+
+
+def finish_self(keep, got):
+    _, depth, width = keep.shape
+    local = width // 4
+    dims = [(depth, width), (depth, width), (3, depth, local), (local, depth)]
+    return call(
+        finish_self_body,
+        (1,),
+        [whole(keep.shape)] * 2,
+        [whole(item) for item in dims],
+        [shape(dims[0])] + [shape(item, F32) for item in dims[1:]],
+        "finish_self",
+        cost(0, 12 * keep.size, scale=SHORT),
+    )(keep, got)
+
+
+def finish_heads_body(own_ref, other_ref, kv_ref, query_ref, out_ref):
+    local = out_ref.shape[0]
+    total = own_ref[...] + other_ref[...].astype(F32)
+    for i in range(2):
+        kv_ref[i] = total[:, i * local : (i + 1) * local]
+    query_ref[...] = total[:, 2 * local : 3 * local]
+    out_ref[...] = total[:, 3 * local :].T
+
+
+def finish_heads(own, other):
+    depth, width = own.shape
+    local = width // 4
+    dims = [(2, depth, local), (depth, local), (local, depth)]
+    return call(
+        finish_heads_body,
+        (1,),
+        [whole(own.shape)] * 2,
+        [whole(item) for item in dims],
+        [shape(item, F32) for item in dims],
+        "finish_heads",
+        cost(0, 12 * own.size, scale=SHORT),
+    )(own, other)
 
 
 def place_body(order, a, b, c, d, *refs, start):
@@ -1026,13 +1082,13 @@
     last = AUDIO - (wide - 1) * share
     valid = [(wide - 1) * size + min(max(last - start, 0), size) for start, size in zip(starts, sizes)]
 
-    def encoder_rows(part, *named):
-        block = encode(then(order, *named), by_clip, gains, starts[part], sizes[part])
-        then.last = block
+    def encoder_rows(part, *arrived):
+        block = encode(then(order), by_clip, gains, starts[part], sizes[part], LONG if part else None)
+        block, *arrived = then.join(block, *arrived)
         block = lax.all_to_all(block, "wide", 0, 0, tiled=True)
-        return block.reshape(wide * sizes[part], width)
-
-    encoded_first = encoder_rows(0)
+        return block.reshape(wide * sizes[part], width), *arrived
+
+    (encoded_first,) = encoder_rows(0)
     self_qkv = self_qkv.transpose(0, 2, 1)
     pack_kv = cross_kv.transpose(0, 2, 1).reshape(2 * local, width)
     packs_one = gather_narrow(jnp.concatenate((self_out, then(cross_q).T)))
@@ -1044,18 +1100,20 @@
     mix_two = swap(mixed_two, "narrow", 2)
     crossing = swap(mixed_three, "narrow", 1)
     normed_near, qkv_near, mixed_one, mixed_zero, lse_near = self_fwd(
-        then(near_order), lengths, tokens, gains, self_qkv
-    )
-    then.last = mixed_zero
-    mix_three = swap(then(crossing), "narrow", 2)
+        then(near_order), lengths, tokens, gains, self_qkv, LONG
+    )
+    mixed_one, mixed_zero, mix_two, crossing, *packs_one = then.join(
+        mixed_one, mixed_zero, mix_two, crossing, *packs_one
+    )
+    mix_one, mix_three = swap(mixed_one, "narrow", 1), swap(crossing, "narrow", 2)
+    packs_one = packs_one + [swap(packs_one[2], "narrow", 1)]
+    encoded_second, mix_one, mix_three, *packs_one = encoder_rows(1, mix_one, mix_three, *packs_one)
+    encoded = (encoded_first, encoded_second)
     packs_kv = gather_narrow(then(pack_kv))
-    mixes = [mixed_zero, swap(mixed_one, "narrow", 1), mix_two, mix_three]
-    packs_one = finish(packs_one, then)
-    encoded_second = encoder_rows(1, mix_two, packs_one[2])
-    encoded = (encoded_first, encoded_second)
+    mixes = [mixed_zero, mix_one, mix_two, mix_three]
     after_self, normed_two, query = to_query(then(order), tokens, mixes, packs_one, gains)
-    then.last = query
-    packs_kv = finish(packs_kv, then)
+    query, *packs_kv = then.join(query, *packs_kv)
+    packs_kv = packs_kv + [swap(packs_kv[2], "narrow", 1)]
     packs_out = gather_narrow(then(cross_out))
     kv_first, *before = cross_first(then(query), encoded_first, packs_kv, valid[0])
     then.last = kv_first
@@ -1149,12 +1207,12 @@
     )
     give, keep, heads_three, *block_all = then.join(give, keep, heads_three, *block_all)
     got = swap(give, "narrow", 1)
-    dqkv_near, part_one, part_zero = self_bwd(
+    *dqkv_near, part_one, part_zero = self_bwd(
         then(near_order), lengths, qkv_near, mixed_one, mixed_zero, lse_near, heads_one, head0, self_qkv, SHORT
     )
     then.last = part_one
     part_near = swap(part_one, "narrow", 1)
-    dqkv_far, part_three, part_two = self_bwd(
+    *dqkv_far, part_three, part_two = self_bwd(
         then(far_order), lengths, qkv_far, mixed_three, mixed_two, lse_far, heads_three, heads_two, self_qkv, SHORT
     )
     part_three, part_two, self_got, frames_second, *back_first = then.join(
@@ -1162,7 +1220,8 @@
     )
     part_cross = swap(part_three, "narrow", 1)
     back_first = back_first + [swap(back_first[2], "narrow", 1)]
-    feed_grads = scatter_wide(bits, then, feed_keep, feed_give, 3, feed_got)
+    feed_keep, feed_got = scatter_wide(bits, then, feed_keep, feed_give, 3, feed_got)
+    feed_grads = feed_keep.astype(F32) + feed_got.astype(F32)
     self_other = (then(self_keep)[1].astype(F32) + self_got[1].astype(F32)).astype(BF16)
     then.last = self_other
     self_other = swap(self_other, "narrow", 2)
@@ -1178,30 +1237,26 @@
     then.last = part_far
     part_far = swap(part_far, "narrow", 2)
     self_keep, self_give = self_weights(
-        then(bits), normed_near, normed_far, dqkv_near, dqkv_far, self_keep, self_got, self_other, wide, LONG
+        then(bits), normed_near, normed_far, *dqkv_near, *dqkv_far, self_keep, self_got, self_other, wide, LONG
     )
     then.last = self_give
     self_got = swap(self_give, "wide", 1)
+    view = (wide // 4, 2, depth, width)
+    pair = lambda keep, got: (keep.reshape(view), got.reshape(view))
+    keep_a, give_a, keep_b, give_b = merge(then(bits), (1, 0), pair(keep_a, got_a), pair(keep_b, got_b), scale=SHORT)
+    then.last = give_a
+    got_a, got_b = swap(give_a, "wide", 2), swap(give_b, "wide", 1)
     tokens_own, gain_one = to_tokens_grad(
-        then(order), tokens, part_zero, part_near, part_far, grad_self, gains, SHORT
+        then(order), tokens, part_zero, part_near, part_far, grad_self, gains, LONG
     )
     then.last = tokens_own
     tokens_all = gather_narrow(tokens_own)
     gain_terms = jnp.concatenate((gain_first + gain_second, gain_one, gain_two, gain_three))
-    gain_other = swap(gain_terms, "narrow", 1)
-    view = (wide // 4, 2, depth, width)
-    pair = lambda keep, got: (keep.reshape(view), got.reshape(view))
-    keep_a, give_a, keep_b, give_b = merge(then(bits), (1, 0), pair(keep_a, got_a), pair(keep_b, got_b), scale=LONG)
-    give_a, give_b, keep_a, keep_b, gain_terms, gain_other = then.join(
-        give_a, give_b, keep_a, keep_b, gain_terms, gain_other
-    )
-    got_a, got_b = swap(give_a, "wide", 2), swap(give_b, "wide", 1)
+    gain_other = swap(gain_terms, "wide", 1)
+    block_out = place_blocks(then(order), block_all, (clips, seq, width), scale=LONG)
+    block_out, self_got, gain_other, gain_terms = then.join(block_out, self_got, gain_other, gain_terms)
     gain_terms = gain_terms + gain_other
-    gain_other = swap(gain_terms, "narrow", 2)
-    block_out = place_blocks(then(order), block_all, (clips, seq, width), scale=LONG)
-    block_out, self_got, gain_other = then.join(block_out, self_got, gain_other)
-    gain_terms = gain_terms + gain_other
-    gain_other = swap(gain_terms, "wide", 1)
+    gain_other = swap(gain_terms, "wide", 2)
     self_keep, self_give = merge(then(bits), (1,), pair(self_keep, self_got), scale=SHORT)
     then.last = self_give
     self_got = swap(self_give, "wide", 2)
@@ -1216,44 +1271,44 @@
     back_second = gather_narrow(back_second)
     tokens_all = tokens_all + [swap(tokens_all[2], "narrow", 1)]
     gain_terms = gain_terms + gain_other
-    gain_other = swap(gain_terms, "wide", 2)
+    gain_other = swap(gain_terms, "wide", 4)
     memory_grad = place_blocks(
         then(order), back_first, (wide, narrow, share, width), starts[0], scale=LONG
     )
     memory_grad, gain_other, gain_terms, *tokens_all = then.join(memory_grad, gain_other, gain_terms, *tokens_all)
-    gain_terms = gain_terms + gain_other
-    gain_other = swap(gain_terms, "wide", 4)
-    tokens_grad = place_blocks(then(order), tokens_all, (clips, seq, width))
-    tokens_grad, got, *back_second = then.join(tokens_grad, got, *back_second)
-    back_second = back_second + [swap(back_second[2], "narrow", 1)]
-    total = scatter_wide(bits, then, keep, give, 3, got)
-    other = swap(total[1].astype(BF16), "narrow", 2)
-    memory_grad = place_blocks(
-        then(order), back_second, (wide, narrow, share, width), starts[1], memory_grad, scale=LONG
-    )
-    memory_grad, other, gain_other = then.join(memory_grad, other, gain_other)
-    memory_grad = memory_grad.reshape(memory.shape)
-    head_grads = total[0] + other.astype(F32)
-    self_grads = total[2]
     gain_terms = gain_terms + gain_other
     bit = 8
     while bit < wide:
         gain_terms = gain_terms + swap(gain_terms, "wide", bit)
         bit *= 2
-    gains_grad = lax.dynamic_slice_in_dim(gain_terms, place * depth, depth, 1)
-
-    heads = lambda i: head_grads[:, i * local : (i + 1) * local]
-    own = lambda i: self_grads[:, i * local : (i + 1) * local]
+    gain_terms = lax.dynamic_slice_in_dim(gain_terms, place * depth, depth, 1)
+    gain_other = swap(gain_terms, "narrow", 1)
+    tokens_grad = place_blocks(then(order), tokens_all, (clips, seq, width))
+    tokens_grad, got, gain_other, gain_terms, *back_second = then.join(
+        tokens_grad, got, gain_other, gain_terms, *back_second
+    )
+    back_second = back_second + [swap(back_second[2], "narrow", 1)]
+    gain_terms = gain_terms + gain_other
+    gain_other = swap(gain_terms, "narrow", 2)
+    keep, got = scatter_wide(bits, then, keep, give, 3, got)
+    give, head_grads, qkv_grad, self_out_grad = finish_self(keep, then(got))
+    then.last = give
+    other = swap(give, "narrow", 2)
+    memory_grad = place_blocks(
+        then(order), back_second, (wide, narrow, share, width), starts[1], memory_grad, scale=LONG
+    )
+    memory_grad, other, gain_other, gain_terms = then.join(memory_grad, other, gain_other, gain_terms)
+    kv_grad, query_grad, cross_out_grad = finish_heads(head_grads, other)
     return (
         block_out,
         tokens_grad,
-        memory_grad,
-        gains_grad,
-        jnp.stack([own(i) for i in range(3)]),
-        own(3).T,
-        heads(2),
-        jnp.stack((heads(0), heads(1))),
-        heads(3).T,
+        memory_grad.reshape(memory.shape),
+        gain_terms + gain_other,
+        qkv_grad,
+        self_out_grad,
+        query_grad,
+        kv_grad,
+        cross_out_grad,
         feed_grads[0],
         feed_grads[1].T,
     )

time: 401 us -> 386 us (0.963)
  other arithmetic: 12.2 us -> 7.3 us
  starting transfers between devices: 69.2 us -> 64.5 us
    ppermute x60, waiting for transfers between devices: 55.9 us -> 50.3 us  [swap(): return lax.ppermute(values, axis, [(i, i ^ bit) for i in range(size)])]
    unnamed x124 -> x134, local copies, waits for them, and re-layouts: 14.5 us -> 12.4 us
    pallas_call x2 -> x4, Pallas kernels: 19.5 us -> 21.4 us  [the longest x1 10.2 us: head_weights(): call(head_weights_body, (2,), [whole(item.shape) for item in encs] + [pl....]
  transfers between devices with their start and end apart: 64 -> 64, of which waited for: 17 -> 16; matrix products, arithmetic and copies ran while one was open for 3% -> 2% of each run, Pallas kernels for 53% -> 55%
where the time goes in v4:
time: 386 us; the launch traced here: 379 us
  Pallas kernels  238 us (62%)
  starting transfers between devices  64.5 us (17%)
  waiting for transfers between devices  53.4 us (14%)
  local copies, waits for them, and re-layouts  14 us (4%)
  other arithmetic  7.3 us (2%)
    ppermute x60, waiting for transfers between devices, swap(): return lax.ppermute(values, axis, [(i, i ^ bit) for i in range(size)])  50.3 us
    ppermute x60, starting transfers between devices, swap(): return lax.ppermute(values, axis, [(i, i ^ bit) for i in range(size)])  42.4 us
    pallas_call x3, Pallas kernels, feed_forward(): call(functools.partial(feed_body, count=count), (count, tiles), single +...  23.7 us
    pallas_call x1, Pallas kernels, cross_second_back(): call(functools.partial(cross_second_back_body, valid=valid), (2,), [head_...  23.3 us
    pallas_call x1, Pallas kernels, cross_first_back(): call(functools.partial(cross_first_back_body, valid=valid), (2,), [pl.Blo...  23.1 us
    pallas_call x2, Pallas kernels, self_bwd(): call(self_bwd_body, (2,), [pl.BlockSpec((1, 3, seq, local), lambda i, *_:...  19 us
    pallas_call x1, Pallas kernels, cross_second(): call(functools.partial(cross_second_body, valid=valid), (2,), [rows, whol...  18.5 us
    pallas_call x2, Pallas kernels, self_fwd(): call(self_fwd_body, (2,), [pl.BlockSpec((1, seq, width), lambda i, order,...  17.9 us
  transfers between devices with their start and end apart: 64, of which 16 were waited for; matrix products, arithmetic and copies ran while one was open for 2% of the time, Pallas kernels for 55%

profile of v4, /device:TPU:0, one launch (start us, length us, event | category | flops | bytes accessed | tf_op | source)
XLA Modules:
  0.0 379.0 jit_solution(9974612847715944535)
XLA Ops:
  4.5 7.4 %all-to-all-start.1 = ((bf16[8,96,768]{2,1,0:T(8,128)(2,1)}), bf16[8,96,768]{2,1,0:T(8,128)(2,1)S(1)}, u32[]{:S(2)}, u32[]{:S(2)}) async-start(bf16[8,96,768]{2,1,0:T(8,128)(2,1)} %encode.2), calls=%async_computation.1 | async-start | bytes 2359296 | tf_op jit(solution)/shard_map/all_to_all | solution.py:1088
  14.2 9.0 %self_forward.2 = (bf16[2,448,768]{2,1,0:T(8,128)(2,1)}, bf16[2,3,448,192]{3,2,1,0:T(8,128)(2,1)}, bf16[448,192]{1,0:T(8,128)(2,1)}, bf16[448,192]{1,0:T(8,128)(2,1)}, f32[2,3,448]{2,1,0:T(4,128)}) custom-call(s32[2]{0:T(128)} %get-tuple-element.356.order, s32[4]{0:T(128)} %lengths.15, bf16[4,448,768]{2,1,0:T(8,128)(2,1)} %token_ref.7, f32[4,768]{1,0:T(4,128)} %gain_ref.20, ...), custom_call_target="tpu_custom_call" | custom-call | flops 1409286144 | bytes 5505024 | tf_op jit(solution)/shard_map/self_forward/pallas_call | solution.py:207
  24.2 9.0 %self_forward.3 = (bf16[2,448,768]{2,1,0:T(8,128)(2,1)}, bf16[2,3,448,192]{3,2,1,0:T(8,128)(2,1)}, bf16[448,192]{1,0:T(8,128)(2,1)}, bf16[448,192]{1,0:T(8,128)(2,1)}, f32[2,3,448]{2,1,0:T(4,128)}) custom-call(s32[2]{0:T(128)} %get-tuple-element.350.order, s32[4]{0:T(128)} %lengths.15, bf16[4,448,768]{2,1,0:T(8,128)(2,1)} %token_ref.7, f32[4,768]{1,0:T(4,128)} %gain_ref.20, ...), custom_call_target="tpu_custom_call" | custom-call | flops 70464307200 | bytes 275251200 | tf_op jit(solution)/shard_map/self_forward/pallas_call | solution.py:207
  43.6 6.2 %all-to-all-start = ((bf16[8,96,768]{2,1,0:T(8,128)(2,1)}), bf16[8,96,768]{2,1,0:T(8,128)(2,1)S(1)}, u32[]{:S(2)}, u32[]{:S(2)}) async-start(bf16[8,96,768]{2,1,0:T(8,128)(2,1)} %encode.3), calls=%async_computation | async-start | bytes 2359296 | tf_op jit(solution)/shard_map/all_to_all | solution.py:1088
  49.8 6.9 %self_out_to_query.1 = (f32[448,768]{1,0:T(8,128)}, bf16[448,768]{1,0:T(8,128)(2,1)}, bf16[2,448,384]{2,1,0:T(8,128)(2,1)}) custom-call(s32[4]{0:T(128)} %iota_xor_fusion.order, bf16[4,448,768]{2,1,0:T(8,128)(2,1)} %token_ref.7, bf16[448,192]{1,0:T(8,128)(2,1)} %get-tuple-element.254.m0.mixed1_ref, bf16[448,192]{1,0:T(8,128)(2,1)} %copy-done.38, ...), custom_call_target="tpu_custom_call" | custom-call | flops 1056964608 | bytes 6488064 | tf_op jit(solution)/shard_map/self_out_to_query/pallas_call | solution.py:339
  60.1 14.2 %cross_first.1 = (bf16[768,1536]{1,0:T(8,128)(2,1)}, f32[2,384,448]{2,1,0:T(8,128)}, f32[2,6,448]{2,1,0:T(8,128)}, f32[2,6,448]{2,1,0:T(8,128)}) custom-call(bf16[2,448,384]{2,1,0:T(8,128)(2,1)} %get-tuple-element.268.query_ref, bf16[768,768]{1,0:T(8,128)(2,1)} %bitcast.56, bf16[384,768]{1,0:T(8,128)(2,1)} %bitcast.4.w0, bf16[384,768]{1,0:T(8,128)(2,1)} %copy-done.56, ...), custom_call_target="tpu_custom_call" | custom-call | flops 7096762368 | bytes 4718592 | tf_op jit(solution)/shard_map/cross_first/pallas_call | solution.py:443
  80.0 18.5 %cross_second.1 = (bf16[768,1536]{1,0:T(8,128)(2,1)}, bf16[2,448,384]{2,1,0:T(8,128)(2,1)}, f32[2,6,448]{2,1,0:T(8,128)}, f32[448,768]{1,0:T(8,128)}, bf16[448,768]{1,0:T(8,128)(2,1)}) custom-call(bf16[2,448,384]{2,1,0:T(8,128)(2,1)} %get-tuple-element.268.query_ref, bf16[768,768]{1,0:T(8,128)(2,1)} %bitcast.58, bf16[384,768]{1,0:T(8,128)(2,1)} %bitcast.4.w0, ...), custom_call_target="tpu_custom_call" | custom-call | flops 7096762368 | bytes 5898240 | tf_op jit(solution)/shard_map/cross_second/pallas_call | solution.py:471
  101.8 10.2 %feed_forward.3 = (bf16[2,448,768]{2,1,0:T(8,128)(2,1)}, bf16[2,448,768]{2,1,0:T(8,128)(2,1)}, bf16[2,448,768]{2,1,0:T(8,128)(2,1)}, bf16[448,768]{1,0:T(8,128)(...) custom-call(s32[2]{0:T(128)} %bitcast.77, s32[4]{0:T(128)} %lengths.15, ...), custom_call_target="tpu_custom_call" | custom-call | flops 4227858432 | bytes 9633792 | tf_op jit(solution)/shard_map/feed_forward/pallas_call | solution.py:533
  111.9 4.7 %collective-permute-done.13.refs_0_.refs_2_ = bf16[448,768]{1,0:T(8,128)(2,1)S(1)} collective-permute-done((bf16[448,768]{1,0:T(8,128)(2,1)}, bf16[448,768]{1,0:T(8,128)(2,1)S(1)}, u32[]{:S(2)}, u32[]{:S(2)}) %collective-permute-start.13) | collective-permute-done | bytes 688160 | tf_op jit(solution)/shard_map/ppermute | solution.py:78
  119.7 6.8 %feed_forward.4 = (bf16[1,448,768]{2,1,0:T(8,128)(2,1)}, bf16[1,448,768]{2,1,0:T(8,128)(2,1)}, bf16[1,448,768]{2,1,0:T(8,128)(2,1)}, bf16[448,768]{1,0:T(8,128)(2,1)}, bf16[448,768]{1,0:T(8,128)(2,1)}) custom-call(s32[1]{0:T(128)} %get-tuple-element.470.order, s32[4]{0:T(128)} %lengths.15, bf16[448,768]{1,0:T(8,128)(2,1)} %copy-done.52, ...), custom_call_target="tpu_custom_call" | custom-call | flops 2113929216 | bytes 4816896 | tf_op jit(solution)/shard_map/feed_forward/pallas_call | solution.py:533
  127.6 6.7 %feed_forward.5 = (bf16[1,448,768]{2,1,0:T(8,128)(2,1)}, bf16[1,448,768]{2,1,0:T(8,128)(2,1)}, bf16[1,448,768]{2,1,0:T(8,128)(2,1)}, bf16[448,768]{1,0:T(8,128)(2,1)}, bf16[448,768]{1,0:T(8,128)(2,1)}) custom-call(s32[1]{0:T(128)} %get-tuple-element.281.order, s32[4]{0:T(128)} %lengths.15, bf16[448,768]{1,0:T(8,128)(2,1)} %copy-done.51, ...), custom_call_target="tpu_custom_call" | custom-call | flops 2113929216 | bytes 4816896 | tf_op jit(solution)/shard_map/feed_forward/pallas_call | solution.py:533
  136.8 11.7 %feed_weight_grads.1 = (bf16[2,4,96,768]{3,2,1,0:T(8,128)(2,1)}, bf16[2,4,96,768]{3,2,1,0:T(8,128)(2,1)}) custom-call(s32[8]{0:T(128)} %shift-right-arithmetic_and_fusion.bits, bf16[448,768]{1,0:T(8,128)(2,1)} %get-tuple-element.277.refs_0_, bf16[448,768]{1,0:T(8,128)(2,1)} %copy-done.49, bf16[448,768]{1,0:T(8,128)(2,1)} %copy-done.51, ...), custom_call_target="tpu_custom_call" | custom-call | flops 4227858432 | bytes 8257536 | tf_op jit(solution)/shard_map/feed_weight_grads/pallas_call | solution.py:792
  154.1 23.1 %cross_first_back.1 = (f32[448,768]{1,0:T(8,128)}, bf16[448,768]{1,0:T(8,128)(2,1)}, bf16[2,448,384]{2,1,0:T(8,128)(2,1)}, f32[1,768]{1,0:T(1,128)}, f32[2,448,3...) custom-call(s32[4]{0:T(128)} %iota_xor_fusion.order, s32[4]{0:T(128)} %lengths.15, ...), custom_call_target="tpu_custom_call" | custom-call | flops 17666408448 | bytes 11796480 | tf_op jit(solution)/shard_map/cross_first_back/pallas_call | solution.py:632
  189.5 23.3 %cross_second_back.1 = (bf16[2,448,384]{2,1,0:T(8,128)(2,1)}, bf16[1536,768]{1,0:T(8,128)(2,1)}, bf16[768,768]{1,0:T(8,128)(2,1)}, f32[448,768]{1,0:T(8,128)}, b...) custom-call(bf16[2,448,384]{2,1,0:T(8,128)(2,1)} %get-tuple-element., ...), custom_call_target="tpu_custom_call" | custom-call | flops 17666408448 | bytes 11796480 | tf_op jit(solution)/shard_map/cross_second_back/pallas_call | solution.py:704
  227.0 4.4 %memory_back.2 = (bf16[8,96,768]{2,1,0:T(8,128)(2,1)}, f32[1,768]{1,0:T(1,128)}) custom-call(s32[4]{0:T(128)} %iota_xor_fusion.order, bf16[8,4,192,768]{3,2,1,0:T(8,128)(2,1)} %bitcast.46, f32[4,768]{1,0:T(4,128)} %gain_ref.20, bf16[8,96,768]{2,1,0:T(8,128)(2,1)} %copy-done), custom_call_target="tpu_custom_call" | custom-call | bytes 3 | tf_op jit(solution)/shard_map/memory_back/pallas_call | solution.py:146
  234.9 4.5 %all-to-all-start.3 = ((bf16[8,96,768]{2,1,0:T(8,128)(2,1)}), bf16[8,96,768]{2,1,0:T(8,128)(2,1)}, u32[]{:S(2)}, u32[]{:S(2)}) async-start(bf16[8,96,768]{2,1,0:T(8,128)(2,1)} %bitcast.12), calls=%async_computation.3 | async-start | bytes 2359296 | tf_op jit(solution)/shard_map/all_to_all | solution.py:1164
  240.0 10.2 %head_weight_grads.1 = (bf16[2,768,768]{2,1,0:T(8,128)(2,1)}, bf16[2,768,768]{2,1,0:T(8,128)(2,1)}) custom-call(bf16[768,768]{1,0:T(8,128)(2,1)} %bitcast.57, bf16[768,768]{1,0:T(8,128)(2,1)} %bitcast.59, bf16[1536,768]{1,0:T(8,128)(2,1)} %get-tuple-element.305.dkv0, bf16[1536,768]{1,0:T(8,128)(2,1)} %get-tuple-element.329.dkv1, ...), custom_call_target="tpu_custom_call" | custom-call | flops 234042163200 | bytes 353894400 | tf_op jit(solution)/shard_map/head_weight_grads/pallas_call | solution.py:823
  250.9 9.4 %self_backward.2 = (bf16[2,448,192]{2,1,0:T(8,128)(2,1)}, bf16[2,384,448]{2,1,0:T(8,128)(2,1)}, bf16[448,768]{1,0:T(8,128)(2,1)}, bf16[448,768]{1,0:T(8,128)(2,1)}) custom-call(s32[2]{0:T(128)} %get-tuple-element.350.order, s32[4]{0:T(128)} %lengths.15, bf16[2,3,448,192]{3,2,1,0:T(8,128)(2,1)} %get-tuple-element.351.qkv_ref, ...), custom_call_target="tpu_custom_call" | custom-call | flops 2334 | bytes 5 | tf_op jit(solution)/shard_map/self_backward/pallas_call | solution.py:296
  260.3 9.6 %self_backward.3 = (bf16[2,448,192]{2,1,0:T(8,128)(2,1)}, bf16[2,384,448]{2,1,0:T(8,128)(2,1)}, bf16[448,768]{1,0:T(8,128)(2,1)}, bf16[448,768]{1,0:T(8,128)(2,1)}) custom-call(s32[2]{0:T(128)} %get-tuple-element.356.order, s32[4]{0:T(128)} %lengths.15, bf16[2,3,448,192]{3,2,1,0:T(8,128)(2,1)} %get-tuple-element.357.qkv_ref, ...), custom_call_target="tpu_custom_call" | custom-call | flops 2334 | bytes 5 | tf_op jit(solution)/shard_map/self_backward/pallas_call | solution.py:296
  277.9 4.5 %merge_heads.1 = (bf16[4,96,768]{2,1,0:T(8,128)(2,1)}, bf16[4,96,768]{2,1,0:T(8,128)(2,1)}, bf16[4,96,768]{2,1,0:T(8,128)(2,1)}, bf16[4,96,768]{2,1,0:T(8,128)(2,1)}) custom-call(s32[8]{0:T(128)} %shift-right-arithmetic_and_fusion.bits, bf16[2,8,96,768]{3,2,1,0:T(8,128)(2,1)} %bitcast.53, bf16[2,8,96,768]{3,2,1,0:T(8,128)(2,1)} %bitcast.54), custom_call_target="tpu_custom_call" | custom-call | bytes 7 | tf_op jit(solution)/shard_map/merge_heads/pallas_call | solution.py:943
  287.5 7.2 %self_weight_grads.1 = (bf16[4,96,768]{2,1,0:T(8,128)(2,1)}, bf16[4,96,768]{2,1,0:T(8,128)(2,1)}) custom-call(s32[8]{0:T(128)} %shift-right-arithmetic_and_fusion.bits, bf16[2,448,768]{2,1,0:T(8,128)(2,1)} %get-tuple-element.383.near, bf16[2,448,768]{2,1,0:T(8,128)(2,1)} %get-tuple-element.384.far, bf16[2,448,192]{2,1,0:T(8,128)(2,1)} %get-tuple-element.385.dq_near, ...), custom_call_target="tpu_custom_call" | custom-call | flops 79272345600 | bytes 275251200 | tf_op jit(solution)/shard_map/self_weight_grads/pallas_call | solution.py:876
  295.3 4.6 %collective-permute-done.41 = bf16[4,96,768]{2,1,0:T(8,128)(2,1)S(1)} collective-permute-done((bf16[4,96,768]{2,1,0:T(8,128)(2,1)S(1)}, bf16[4,96,768]{2,1,0:T(8,128)(2,1)S(1)}, u32[]{:S(2)}, u32[]{:S(2)}) %collective-permute-start.41) | collective-permute-done | bytes 589856 | tf_op jit(solution)/shard_map/ppermute | solution.py:78
  326.9 5.4 %collective-permute-done.47 = bf16[2,1,96,768]{3,2,0,1:T(8,128)(2,1)S(1)} collective-permute-done((bf16[2,1,96,768]{3,2,0,1:T(8,128)(2,1)}, bf16[2,1,96,768]{3,2,0,1:T(8,128)(2,1)S(1)}, u32[]{:S(2)}, u32[]{:S(2)}) %collective-permute-start.47) | collective-permute-done | bytes 294944 | tf_op jit(solution)/shard_map/ppermute | solution.py:78
  344.8 16.0 %collective-permute-done.51 = f32[4,768]{1,0:T(4,128)} collective-permute-done((f32[4,768]{1,0:T(4,128)S(1)}, f32[4,768]{1,0:T(4,128)}, u32[]{:S(2)}, u32[]{:S(2)}) %collective-permute-start.51) | collective-permute-done | bytes 12320 | tf_op jit(solution)/shard_map/ppermute | solution.py:78
  (290 shorter events, 143.8 us)
Async XLA Ops:
  4.5 39.0 %all-to-all-start.1 = ((bf16[8,96,768]{2,1,0:T(8,128)(2,1)}), bf16[8,96,768]{2,1,0:T(8,128)(2,1)S(1)}, u32[]{:S(2)}, u32[]{:S(2)}) async-start(bf16[8,96,768]{2,1,0:T(8,128)(2,1)} %encode.2), calls=%async_computation.1 | async-start | bytes 2359296 | tf_op jit(solution)/shard_map/all_to_all | solution.py:1088
  12.0 21.3 %collective-permute-start.3 = (bf16[384,768]{1,0:T(8,128)(2,1)S(1)}, bf16[384,768]{1,0:T(8,128)(2,1)S(1)}, u32[]{:S(2)}, u32[]{:S(2)}) collective-permute-start(bf16[384,768]{1,0:T(8,128)(2,1)S(1)} %pad_maximum_fusion.p0), channel_id=1, source_target_pairs={{0,2},{1,3},{2,0},{3,1},{4,6},{5,7},{6,4},{7,5},{8,10},{9,11},{10,... | collective-permute-start | bytes 1769480 | tf_op jit(solution)/shard_map/ppermute | solution.py:78
  13.6 19.7 %collective-permute-start.2 = (bf16[384,768]{1,0:T(8,128)(2,1)S(1)}, bf16[384,768]{1,0:T(8,128)(2,1)S(1)}, u32[]{:S(2)}, u32[]{:S(2)}) collective-permute-start(bf16[384,768]{1,0:T(8,128)(2,1)S(1)} %pad_maximum_fusion.p0), channel_id=1, source_target_pairs={{0,1},{1,0},{2,3},{3,2},{4,5},{5,4},{6,7},{7,6},{8,9},{9,8},{10,11... | collective-permute-start | bytes 1769480 | tf_op jit(solution)/shard_map/ppermute | solution.py:78
  43.6 35.4 %all-to-all-start = ((bf16[8,96,768]{2,1,0:T(8,128)(2,1)}), bf16[8,96,768]{2,1,0:T(8,128)(2,1)S(1)}, u32[]{:S(2)}, u32[]{:S(2)}) async-start(bf16[8,96,768]{2,1,0:T(8,128)(2,1)} %encode.3), calls=%async_computation | async-start | bytes 2359296 | tf_op jit(solution)/shard_map/all_to_all | solution.py:1088
  148.5 35.8 %collective-permute-start.22 = (bf16[2,4,96,768]{3,2,1,0:T(8,128)(2,1)}, bf16[2,4,96,768]{3,2,1,0:T(8,128)(2,1)}, u32[]{:S(2)}, u32[]{:S(2)}) collective-permute-start(bf16[2,4,96,768]{3,2,1,0:T(8,128)(2,1)} %get-tuple-element.296), channel_id=1, source_target_pairs={{0,4},{4,0},{8,12},{12,8},{16,20},{20,16},{24,28},{28,24},{1,5},{5... | collective-permute-start | bytes 3538952 | tf_op jit(solution)/shard_map/ppermute | solution.py:78
  153.2 28.0 %collective-permute-start.21 = (bf16[448,768]{1,0:T(8,128)(2,1)S(1)}, bf16[448,768]{1,0:T(8,128)(2,1)}, u32[]{:S(2)}, u32[]{:S(2)}) collective-permute-start(bf16[448,768]{1,0:T(8,128)(2,1)S(1)} %add_convert_fusion.2), channel_id=1, source_target_pairs={{0,2},{1,3},{2,0},{3,1},{4,6},{5,7},{6,4},{7,5},{8,10},{9,11},{10,... | collective-permute-start | bytes 2064392 | tf_op jit(solution)/shard_map/ppermute | solution.py:78
  177.2 48.8 %all-to-all-start.2 = ((bf16[8,96,768]{2,1,0:T(8,128)(2,1)}), bf16[8,96,768]{2,1,0:T(8,128)(2,1)S(1)}, u32[]{:S(2)}, u32[]{:S(2)}) async-start(bf16[8,96,768]{2,1,0:T(8,128)(2,1)} %bitcast.60), calls=%async_computation.2 | async-start | bytes 2359296 | tf_op jit(solution)/shard_map/all_to_all | solution.py:1164
  183.0 31.8 %collective-permute-start.25 = (bf16[448,768]{1,0:T(8,128)(2,1)S(1)}, bf16[448,768]{1,0:T(8,128)(2,1)}, u32[]{:S(2)}, u32[]{:S(2)}) collective-permute-start(bf16[448,768]{1,0:T(8,128)(2,1)S(1)} %add_convert_fusion.1.a), channel_id=1, source_target_pairs={{0,2},{1,3},{2,0},{3,1},{4,6},{5,7},{6,4},{7,5},{8,10},{9,11},{10,... | collective-permute-start | bytes 2064392 | tf_op jit(solution)/shard_map/ppermute | solution.py:78
  184.2 30.6 %collective-permute-start.24 = (bf16[448,768]{1,0:T(8,128)(2,1)S(1)}, bf16[448,768]{1,0:T(8,128)(2,1)S(1)}, u32[]{:S(2)}, u32[]{:S(2)}) collective-permute-start(bf16[448,768]{1,0:T(8,128)(2,1)S(1)} %add_convert_fusion.1.a), channel_id=1, source_target_pairs={{0,1},{1,0},{2,3},{3,2},{4,5},{5,4},{6,7},{7,6},{8,9},{9,8},{10,11... | collective-permute-start | bytes 2064392 | tf_op jit(solution)/shard_map/ppermute | solution.py:78
  187.5 27.3 %collective-permute-start.23 = (bf16[4,1,96,768]{3,2,1,0:T(8,128)(2,1)}, bf16[4,1,96,768]{3,2,1,0:T(8,128)(2,1)S(1)}, u32[]{:S(2)}, u32[]{:S(2)}) collective-permute-start(bf16[4,1,96,768]{3,2,1,0:T(8,128)(2,1)} %get-tuple-element.319), channel_id=1, source_target_pairs={{0,8},{4,12},{8,0},{12,4},{16,24},{20,28},{24,16},{28,20},{1,9},{5... | collective-permute-start | bytes 1769480 | tf_op jit(solution)/shard_map/ppermute | solution.py:78
  226.0 24.3 %collective-permute-start.31 = (bf16[448,768]{1,0:T(8,128)(2,1)}, bf16[448,768]{1,0:T(8,128)(2,1)}, u32[]{:S(2)}, u32[]{:S(2)}) collective-permute-start(bf16[448,768]{1,0:T(8,128)(2,1)} %collective-permute-done.25.c), channel_id=1, source_target_pairs={{0,1},{1,0},{2,3},{3,2},{4,5},{5,4},{6,7},{7,6},{8,9},{9,8},{10,11... | collective-permute-start | bytes 2064392 | tf_op jit(solution)/shard_map/ppermute | solution.py:78
  234.1 35.7 %collective-permute-start.34 = (bf16[8,96,768]{2,1,0:T(8,128)(2,1)}, bf16[8,96,768]{2,1,0:T(8,128)(2,1)}, u32[]{:S(2)}, u32[]{:S(2)}) collective-permute-start(bf16[8,96,768]{2,1,0:T(8,128)(2,1)} %get-tuple-element.426.a), channel_id=1, source_target_pairs={{0,2},{1,3},{2,0},{3,1},{4,6},{5,7},{6,4},{7,5},{8,10},{9,11},{10,... | collective-permute-start | bytes 3538952 | tf_op jit(solution)/shard_map/ppermute | solution.py:78
  234.9 34.9 %collective-permute-start.33 = (bf16[8,96,768]{2,1,0:T(8,128)(2,1)}, bf16[8,96,768]{2,1,0:T(8,128)(2,1)}, u32[]{:S(2)}, u32[]{:S(2)}) collective-permute-start(bf16[8,96,768]{2,1,0:T(8,128)(2,1)} %get-tuple-element.426.a), channel_id=1, source_target_pairs={{0,1},{1,0},{2,3},{3,2},{4,5},{5,4},{6,7},{7,6},{8,9},{9,8},{10,11... | collective-permute-start | bytes 3538952 | tf_op jit(solution)/shard_map/ppermute | solution.py:78
  234.9 35.0 %all-to-all-start.3 = ((bf16[8,96,768]{2,1,0:T(8,128)(2,1)}), bf16[8,96,768]{2,1,0:T(8,128)(2,1)}, u32[]{:S(2)}, u32[]{:S(2)}) async-start(bf16[8,96,768]{2,1,0:T(8,128)(2,1)} %bitcast.12), calls=%async_computation.3 | async-start | bytes 2359296 | tf_op jit(solution)/shard_map/all_to_all | solution.py:1164
  250.3 26.1 %collective-permute-start.37 = (bf16[2,768,768]{2,1,0:T(8,128)(2,1)}, bf16[2,768,768]{2,1,0:T(8,128)(2,1)S(1)}, u32[]{:S(2)}, u32[]{:S(2)}) collective-permute-start(bf16[2,768,768]{2,1,0:T(8,128)(2,1)} %get-tuple-element.349), channel_id=1, source_target_pairs={{0,1},{1,0},{2,3},{3,2},{4,5},{5,4},{6,7},{7,6},{8,9},{9,8},{10,11... | collective-permute-start | bytes 7077896 | tf_op jit(solution)/shard_map/ppermute | solution.py:78
  284.5 19.7 %collective-permute-start.42 = (bf16[448,768]{1,0:T(8,128)(2,1)S(1)}, bf16[448,768]{1,0:T(8,128)(2,1)S(1)}, u32[]{:S(2)}, u32[]{:S(2)}) collective-permute-start(bf16[448,768]{1,0:T(8,128)(2,1)S(1)} %add_convert_fusion), channel_id=1, source_target_pairs={{0,2},{1,3},{2,0},{3,1},{4,6},{5,7},{6,4},{7,5},{8,10},{9,11},{10,... | collective-permute-start | bytes 2064392 | tf_op jit(solution)/shard_map/ppermute | solution.py:78
  294.7 22.1 %collective-permute-start.43 = (bf16[4,96,768]{2,1,0:T(8,128)(2,1)}, bf16[4,96,768]{2,1,0:T(8,128)(2,1)S(1)}, u32[]{:S(2)}, u32[]{:S(2)}) collective-permute-start(bf16[4,96,768]{2,1,0:T(8,128)(2,1)} %get-tuple-element.389), channel_id=1, source_target_pairs={{0,4},{4,0},{8,12},{12,8},{16,20},{20,16},{24,28},{28,24},{1,5},{5... | collective-permute-start | bytes 1769480 | tf_op jit(solution)/shard_map/ppermute | solution.py:78
  309.4 26.7 %collective-permute-start.50 = (bf16[448,768]{1,0:T(8,128)(2,1)}, bf16[448,768]{1,0:T(8,128)(2,1)}, u32[]{:S(2)}, u32[]{:S(2)}) collective-permute-start(bf16[448,768]{1,0:T(8,128)(2,1)} %get-tuple-element.437.a), channel_id=1, source_target_pairs={{0,2},{1,3},{2,0},{3,1},{4,6},{5,7},{6,4},{7,5},{8,10},{9,11},{10,... | collective-permute-start | bytes 2064392 | tf_op jit(solution)/shard_map/ppermute | solution.py:78
  310.7 25.4 %collective-permute-start.49 = (bf16[448,768]{1,0:T(8,128)(2,1)}, bf16[448,768]{1,0:T(8,128)(2,1)S(1)}, u32[]{:S(2)}, u32[]{:S(2)}) collective-permute-start(bf16[448,768]{1,0:T(8,128)(2,1)} %get-tuple-element.437.a), channel_id=1, source_target_pairs={{0,1},{1,0},{2,3},{3,2},{4,5},{5,4},{6,7},{7,6},{8,9},{9,8},{10,11... | collective-permute-start | bytes 2064392 | tf_op jit(solution)/shard_map/ppermute | solution.py:78
  336.1 29.0 %collective-permute-start.56 = (bf16[8,96,768]{2,1,0:T(8,128)(2,1)S(1)}, bf16[8,96,768]{2,1,0:T(8,128)(2,1)S(1)}, u32[]{:S(2)}, u32[]{:S(2)}) collective-permute-start(bf16[8,96,768]{2,1,0:T(8,128)(2,1)S(1)} %copy-done.5), channel_id=1, source_target_pairs={{0,2},{1,3},{2,0},{3,1},{4,6},{5,7},{6,4},{7,5},{8,10},{9,11},{10,... | collective-permute-start | bytes 3538952 | tf_op jit(solution)/shard_map/ppermute | solution.py:78
  336.9 28.2 %collective-permute-start.55 = (bf16[8,96,768]{2,1,0:T(8,128)(2,1)S(1)}, bf16[8,96,768]{2,1,0:T(8,128)(2,1)S(1)}, u32[]{:S(2)}, u32[]{:S(2)}) collective-permute-start(bf16[8,96,768]{2,1,0:T(8,128)(2,1)S(1)} %copy-done.5), channel_id=1, source_target_pairs={{0,1},{1,0},{2,3},{3,2},{4,5},{5,4},{6,7},{7,6},{8,9},{9,8},{10,11... | collective-permute-start | bytes 3538952 | tf_op jit(solution)/shard_map/ppermute | solution.py:78
  337.0 23.8 %collective-permute-start.52 = (bf16[448,768]{1,0:T(8,128)(2,1)}, bf16[448,768]{1,0:T(8,128)(2,1)}, u32[]{:S(2)}, u32[]{:S(2)}) collective-permute-start(bf16[448,768]{1,0:T(8,128)(2,1)} %collective-permute-done.50.c), channel_id=1, source_target_pairs={{0,1},{1,0},{2,3},{3,2},{4,5},{5,4},{6,7},{7,6},{8,9},{9,8},{10,11... | collective-permute-start | bytes 2064392 | tf_op jit(solution)/shard_map/ppermute | solution.py:78
  337.5 27.6 %collective-permute-start.53 = (bf16[3,1,96,768]{3,2,0,1:T(8,128)(2,1)}, bf16[3,1,96,768]{3,2,0,1:T(8,128)(2,1)}, u32[]{:S(2)}, u32[]{:S(2)}) collective-permute-start(bf16[3,1,96,768]{3,2,0,1:T(8,128)(2,1)} %bitcast.78), channel_id=1, source_target_pairs={{0,16},{4,20},{8,24},{12,28},{16,0},{20,4},{24,8},{28,12},{1,17},{... | collective-permute-start | bytes 1327112 | tf_op jit(solution)/shard_map/ppermute | solution.py:78
  339.9 20.9 %collective-permute-start.51 = (f32[4,768]{1,0:T(4,128)S(1)}, f32[4,768]{1,0:T(4,128)}, u32[]{:S(2)}, u32[]{:S(2)}) collective-permute-start(f32[4,768]{1,0:T(4,128)S(1)} %add.56), channel_id=1, source_target_pairs={{0,16},{4,20},{8,24},{12,28},{16,0},{20,4},{24,8},{28,12},{1,17},{... | collective-permute-start | bytes 36872 | tf_op jit(solution)/shard_map/ppermute | solution.py:78
  (107 other events, 839.9 us)

commit v5 on v4

--- a/solution.py
+++ b/solution.py
@@ -18,6 +18,7 @@
 COST_SCALE = 1.0
 LONG = 50.0
 SHORT = 1e-6
+MID = 1e-6
 SPLIT = 32
 
 
@@ -1191,48 +1192,49 @@
     heads_two = swap(head2, "narrow", 2)
     head3 = swap(head3, "narrow", 2)
     block_all = block_all + [swap(block_all[2], "narrow", 1)]
-
-    self_keep, self_give = out_weights(then(grad_one), mixes, LONG)
-    then.last = self_give
-    self_got = swap(self_give, "narrow", 1)
-    back_first, gain_first = memory_back(then(order), by_clip, gains, frames_first, starts[0], SHORT)
-    back_first, frames_second, heads_one, heads_two, head3, feed_got = then.join(
-        back_first, frames_second, heads_one, heads_two, head3, feed_got
-    )
     frames_second = frames_sent(frames_second, 1)
-    heads_three = swap(head3, "narrow", 1)
-    back_first = gather_narrow(back_first)
+
     keep, give = head_weights(
         encoded, (dkv_first, dkv_second), then(normed_two), dq, grad_two, cross_mixed, LONG
     )
-    give, keep, heads_three, *block_all = then.join(give, keep, heads_three, *block_all)
+    give, keep, heads_one, heads_two, head3, feed_got, *block_all = then.join(
+        give, keep, heads_one, heads_two, head3, feed_got, *block_all
+    )
     got = swap(give, "narrow", 1)
+    heads_three = swap(head3, "narrow", 1)
+    back_first, gain_first = memory_back(then(order), by_clip, gains, frames_first, starts[0], SHORT)
+    then.last = back_first
+    back_first = gather_narrow(back_first)
+
     *dqkv_near, part_one, part_zero = self_bwd(
         then(near_order), lengths, qkv_near, mixed_one, mixed_zero, lse_near, heads_one, head0, self_qkv, SHORT
     )
-    then.last = part_one
+    part_one, got, heads_three = then.join(part_one, got, heads_three)
     part_near = swap(part_one, "narrow", 1)
-    *dqkv_far, part_three, part_two = self_bwd(
-        then(far_order), lengths, qkv_far, mixed_three, mixed_two, lse_far, heads_three, heads_two, self_qkv, SHORT
-    )
-    part_three, part_two, self_got, frames_second, *back_first = then.join(
-        part_three, part_two, self_got, frames_second, *back_first
-    )
-    part_cross = swap(part_three, "narrow", 1)
-    back_first = back_first + [swap(back_first[2], "narrow", 1)]
-    feed_keep, feed_got = scatter_wide(bits, then, feed_keep, feed_give, 3, feed_got)
-    feed_grads = feed_keep.astype(F32) + feed_got.astype(F32)
-    self_other = (then(self_keep)[1].astype(F32) + self_got[1].astype(F32)).astype(BF16)
-    then.last = self_other
-    self_other = swap(self_other, "narrow", 2)
-    back_second, gain_second = memory_back(then(order), by_clip, gains, frames_second, starts[1], LONG)
-    back_second, part_two, part_cross, part_near, got, *back_first = then.join(
-        back_second, part_two, part_cross, part_near, got, *back_first
-    )
     view = (2, wide, depth, width)
     keep_a, give_a, keep_b, give_b = merge_heads(then(bits), keep.reshape(view), got.reshape(view))
     then.last = give_a
     got_a, got_b = swap(give_a, "wide", 1), swap(give_b, "wide", 2)
+    self_keep, self_give = out_weights(then(grad_one), mixes, MID)
+    then.last = self_give
+    self_got = swap(self_give, "narrow", 1)
+    *dqkv_far, part_three, part_two = self_bwd(
+        then(far_order), lengths, qkv_far, mixed_three, mixed_two, lse_far, heads_three, heads_two, self_qkv, MID
+    )
+    part_three, part_two, self_got, frames_second, *back_first = then.join(
+        part_three, part_two, self_got, frames_second, *back_first
+    )
+    part_cross = swap(part_three, "narrow", 1)
+    back_first = back_first + [swap(back_first[2], "narrow", 1)]
+    self_other = (then(self_keep)[1].astype(F32) + self_got[1].astype(F32)).astype(BF16)
+    then.last = self_other
+    self_other = swap(self_other, "narrow", 2)
+    feed_keep, feed_got = scatter_wide(bits, then, feed_keep, feed_give, 3, feed_got)
+    feed_grads = feed_keep.astype(F32) + feed_got.astype(F32)
+    back_second, gain_second = memory_back(then(order), by_clip, gains, frames_second, starts[1], LONG)
+    back_second, part_two, part_cross, part_near, *back_first = then.join(
+        back_second, part_two, part_cross, part_near, *back_first
+    )
     part_far = (then(part_two).astype(F32) + part_cross.astype(F32)).astype(BF16)
     then.last = part_far
     part_far = swap(part_far, "narrow", 2)
@@ -1275,21 +1277,19 @@
     memory_grad = place_blocks(
         then(order), back_first, (wide, narrow, share, width), starts[0], scale=LONG
     )
-    memory_grad, gain_other, gain_terms, *tokens_all = then.join(memory_grad, gain_other, gain_terms, *tokens_all)
+    memory_grad, *tokens_all = then.join(memory_grad, *tokens_all)
+    tokens_grad = place_blocks(then(order), tokens_all, (clips, seq, width))
+    tokens_grad, got, gain_other, gain_terms, *back_second = then.join(
+        tokens_grad, got, gain_other, gain_terms, *back_second
+    )
+    back_second = back_second + [swap(back_second[2], "narrow", 1)]
     gain_terms = gain_terms + gain_other
     bit = 8
     while bit < wide:
         gain_terms = gain_terms + swap(gain_terms, "wide", bit)
         bit *= 2
     gain_terms = lax.dynamic_slice_in_dim(gain_terms, place * depth, depth, 1)
-    gain_other = swap(gain_terms, "narrow", 1)
-    tokens_grad = place_blocks(then(order), tokens_all, (clips, seq, width))
-    tokens_grad, got, gain_other, gain_terms, *back_second = then.join(
-        tokens_grad, got, gain_other, gain_terms, *back_second
-    )
-    back_second = back_second + [swap(back_second[2], "narrow", 1)]
-    gain_terms = gain_terms + gain_other
-    gain_other = swap(gain_terms, "narrow", 2)
+    gain_others = [swap(gain_terms, "narrow", distance) for distance in (1, 2, 3)]
     keep, got = scatter_wide(bits, then, keep, give, 3, got)
     give, head_grads, qkv_grad, self_out_grad = finish_self(keep, then(got))
     then.last = give
@@ -1297,13 +1297,14 @@
     memory_grad = place_blocks(
         then(order), back_second, (wide, narrow, share, width), starts[1], memory_grad, scale=LONG
     )
-    memory_grad, other, gain_other, gain_terms = then.join(memory_grad, other, gain_other, gain_terms)
+    memory_grad, other, gain_terms, *gain_others = then.join(memory_grad, other, gain_terms, *gain_others)
+    gain_terms = gain_terms + gain_others[0] + gain_others[1] + gain_others[2]
     kv_grad, query_grad, cross_out_grad = finish_heads(head_grads, other)
     return (
         block_out,
         tokens_grad,
         memory_grad.reshape(memory.shape),
-        gain_terms + gain_other,
+        gain_terms,
         qkv_grad,
         self_out_grad,
         query_grad,

time: 386 us -> 384 us (level)
  waiting for transfers between devices: 53.4 us -> 47.5 us
    ppermute x60 -> x61, waiting for transfers between devices: 50.3 us -> 44.7 us  [swap(): return lax.ppermute(values, axis, [(i, i ^ bit) for i in range(size)])]
    ppermute x60 -> x61, starting transfers between devices: 42.4 us -> 44.2 us  [swap(): return lax.ppermute(values, axis, [(i, i ^ bit) for i in range(size)])]
    unnamed x134 -> x130, local copies, waits for them, and re-layouts: 12.4 us -> 13.3 us
  transfers between devices with their start and end apart: 64 -> 65, of which waited for: 16 -> 17; matrix products, arithmetic and copies ran while one was open for 2% -> 2% of each run, Pallas kernels for 55% -> 55%
where the time goes in v5:
time: 384 us; the launch traced here: 378 us
  Pallas kernels  238 us (62%)
  starting transfers between devices  66.9 us (17%)
  waiting for transfers between devices  47.5 us (12%)
  local copies, waits for them, and re-layouts  14.9 us (4%)
  other arithmetic  8.75 us (2%)
    ppermute x61, waiting for transfers between devices, swap(): return lax.ppermute(values, axis, [(i, i ^ bit) for i in range(size)])  44.7 us
    ppermute x61, starting transfers between devices, swap(): return lax.ppermute(values, axis, [(i, i ^ bit) for i in range(size)])  44.2 us
    pallas_call x3, Pallas kernels, feed_forward(): call(functools.partial(feed_body, count=count), (count, tiles), single +...  23.7 us
    pallas_call x1, Pallas kernels, cross_second_back(): call(functools.partial(cross_second_back_body, valid=valid), (2,), [head_...  23.4 us
    pallas_call x1, Pallas kernels, cross_first_back(): call(functools.partial(cross_first_back_body, valid=valid), (2,), [pl.Blo...  23.1 us
    pallas_call x2, Pallas kernels, self_bwd(): call(self_bwd_body, (2,), [pl.BlockSpec((1, 3, seq, local), lambda i, *_:...  18.9 us
    pallas_call x1, Pallas kernels, cross_second(): call(functools.partial(cross_second_body, valid=valid), (2,), [rows, whol...  18.4 us
    pallas_call x2, Pallas kernels, self_fwd(): call(self_fwd_body, (2,), [pl.BlockSpec((1, seq, width), lambda i, order,...  18 us
  transfers between devices with their start and end apart: 65, of which 17 were waited for; matrix products, arithmetic and copies ran while one was open for 2% of the time, Pallas kernels for 55%

profile of v5, /device:TPU:0, one launch (start us, length us, event | category | flops | bytes accessed | tf_op | source)
XLA Modules:
  0.0 377.7 jit_solution(10343068934324520578)
XLA Ops:
  4.5 7.4 %all-to-all-start.1 = ((bf16[8,96,768]{2,1,0:T(8,128)(2,1)}), bf16[8,96,768]{2,1,0:T(8,128)(2,1)S(1)}, u32[]{:S(2)}, u32[]{:S(2)}) async-start(bf16[8,96,768]{2,1,0:T(8,128)(2,1)} %encode.2), calls=%async_computation.1 | async-start | bytes 2359296 | tf_op jit(solution)/shard_map/all_to_all | solution.py:1089
  14.2 9.0 %self_forward.2 = (bf16[2,448,768]{2,1,0:T(8,128)(2,1)}, bf16[2,3,448,192]{3,2,1,0:T(8,128)(2,1)}, bf16[448,192]{1,0:T(8,128)(2,1)}, bf16[448,192]{1,0:T(8,128)(2,1)}, f32[2,3,448]{2,1,0:T(4,128)}) custom-call(s32[2]{0:T(128)} %get-tuple-element.358.order, s32[4]{0:T(128)} %lengths.15, bf16[4,448,768]{2,1,0:T(8,128)(2,1)} %token_ref.7, f32[4,768]{1,0:T(4,128)} %gain_ref.20, ...), custom_call_target="tpu_custom_call" | custom-call | flops 1409286144 | bytes 5505024 | tf_op jit(solution)/shard_map/self_forward/pallas_call | solution.py:208
  24.2 9.0 %self_forward.3 = (bf16[2,448,768]{2,1,0:T(8,128)(2,1)}, bf16[2,3,448,192]{3,2,1,0:T(8,128)(2,1)}, bf16[448,192]{1,0:T(8,128)(2,1)}, bf16[448,192]{1,0:T(8,128)(2,1)}, f32[2,3,448]{2,1,0:T(4,128)}) custom-call(s32[2]{0:T(128)} %get-tuple-element.343.order, s32[4]{0:T(128)} %lengths.15, bf16[4,448,768]{2,1,0:T(8,128)(2,1)} %token_ref.7, f32[4,768]{1,0:T(4,128)} %gain_ref.20, ...), custom_call_target="tpu_custom_call" | custom-call | flops 70464307200 | bytes 275251200 | tf_op jit(solution)/shard_map/self_forward/pallas_call | solution.py:208
  43.0 6.2 %all-to-all-start = ((bf16[8,96,768]{2,1,0:T(8,128)(2,1)}), bf16[8,96,768]{2,1,0:T(8,128)(2,1)S(1)}, u32[]{:S(2)}, u32[]{:S(2)}) async-start(bf16[8,96,768]{2,1,0:T(8,128)(2,1)} %encode.3), calls=%async_computation | async-start | bytes 2359296 | tf_op jit(solution)/shard_map/all_to_all | solution.py:1089
  49.3 6.9 %self_out_to_query.1 = (f32[448,768]{1,0:T(8,128)}, bf16[448,768]{1,0:T(8,128)(2,1)}, bf16[2,448,384]{2,1,0:T(8,128)(2,1)}) custom-call(s32[4]{0:T(128)} %iota_xor_fusion.order, bf16[4,448,768]{2,1,0:T(8,128)(2,1)} %token_ref.7, bf16[448,192]{1,0:T(8,128)(2,1)} %get-tuple-element.253.m0.mixed1_ref, bf16[448,192]{1,0:T(8,128)(2,1)} %copy-done.16, ...), custom_call_target="tpu_custom_call" | custom-call | flops 1056964608 | bytes 6488064 | tf_op jit(solution)/shard_map/self_out_to_query/pallas_call | solution.py:340
  59.8 14.1 %cross_first.1 = (bf16[768,1536]{1,0:T(8,128)(2,1)}, f32[2,384,448]{2,1,0:T(8,128)}, f32[2,6,448]{2,1,0:T(8,128)}, f32[2,6,448]{2,1,0:T(8,128)}) custom-call(bf16[2,448,384]{2,1,0:T(8,128)(2,1)} %get-tuple-element.267.query_ref, bf16[768,768]{1,0:T(8,128)(2,1)} %bitcast.57, bf16[384,768]{1,0:T(8,128)(2,1)} %bitcast.4.w0, ...), custom_call_target="tpu_custom_call" | custom-call | flops 7096762368 | bytes 4718592 | tf_op jit(solution)/shard_map/cross_first/pallas_call | solution.py:444
  79.4 18.4 %cross_second.1 = (bf16[768,1536]{1,0:T(8,128)(2,1)}, bf16[2,448,384]{2,1,0:T(8,128)(2,1)}, f32[2,6,448]{2,1,0:T(8,128)}, f32[448,768]{1,0:T(8,128)}, bf16[448,768]{1,0:T(8,128)(2,1)}) custom-call(bf16[2,448,384]{2,1,0:T(8,128)(2,1)} %get-tuple-element.267.query_ref, bf16[768,768]{1,0:T(8,128)(2,1)} %bitcast.59, bf16[384,768]{1,0:T(8,128)(2,1)} %bitcast.4.w0, ...), custom_call_target="tpu_custom_call" | custom-call | flops 7096762368 | bytes 5898240 | tf_op jit(solution)/shard_map/cross_second/pallas_call | solution.py:472
  101.2 10.2 %feed_forward.3 = (bf16[2,448,768]{2,1,0:T(8,128)(2,1)}, bf16[2,448,768]{2,1,0:T(8,128)(2,1)}, bf16[2,448,768]{2,1,0:T(8,128)(2,1)}, bf16[448,768]{1,0:T(8,128)(...) custom-call(s32[2]{0:T(128)} %bitcast.80, s32[4]{0:T(128)} %lengths.15, ...), custom_call_target="tpu_custom_call" | custom-call | flops 4227858432 | bytes 9633792 | tf_op jit(solution)/shard_map/feed_forward/pallas_call | solution.py:534
  111.3 4.7 %collective-permute-done.13.refs_0_.refs_2_ = bf16[448,768]{1,0:T(8,128)(2,1)S(1)} collective-permute-done((bf16[448,768]{1,0:T(8,128)(2,1)}, bf16[448,768]{1,0:T(8,128)(2,1)S(1)}, u32[]{:S(2)}, u32[]{:S(2)}) %collective-permute-start.13) | collective-permute-done | bytes 688160 | tf_op jit(solution)/shard_map/ppermute | solution.py:79
  119.0 6.8 %feed_forward.4 = (bf16[1,448,768]{2,1,0:T(8,128)(2,1)}, bf16[1,448,768]{2,1,0:T(8,128)(2,1)}, bf16[1,448,768]{2,1,0:T(8,128)(2,1)}, bf16[448,768]{1,0:T(8,128)(2,1)}, bf16[448,768]{1,0:T(8,128)(2,1)}) custom-call(s32[1]{0:T(128)} %get-tuple-element.468.order, s32[4]{0:T(128)} %lengths.15, bf16[448,768]{1,0:T(8,128)(2,1)} %copy-done.54, ...), custom_call_target="tpu_custom_call" | custom-call | flops 2113929216 | bytes 4816896 | tf_op jit(solution)/shard_map/feed_forward/pallas_call | solution.py:534
  126.9 6.7 %feed_forward.5 = (bf16[1,448,768]{2,1,0:T(8,128)(2,1)}, bf16[1,448,768]{2,1,0:T(8,128)(2,1)}, bf16[1,448,768]{2,1,0:T(8,128)(2,1)}, bf16[448,768]{1,0:T(8,128)(2,1)}, bf16[448,768]{1,0:T(8,128)(2,1)}) custom-call(s32[1]{0:T(128)} %get-tuple-element.280.order, s32[4]{0:T(128)} %lengths.15, bf16[448,768]{1,0:T(8,128)(2,1)} %copy-done.53, ...), custom_call_target="tpu_custom_call" | custom-call | flops 2113929216 | bytes 4816896 | tf_op jit(solution)/shard_map/feed_forward/pallas_call | solution.py:534
  136.4 11.6 %feed_weight_grads.1 = (bf16[2,4,96,768]{3,2,1,0:T(8,128)(2,1)}, bf16[2,4,96,768]{3,2,1,0:T(8,128)(2,1)}) custom-call(s32[8]{0:T(128)} %shift-right-arithmetic_and_fusion.bits, bf16[448,768]{1,0:T(8,128)(2,1)} %get-tuple-element.276.refs_0_, bf16[448,768]{1,0:T(8,128)(2,1)} %copy-done.51, bf16[448,768]{1,0:T(8,128)(2,1)} %copy-done.53, ...), custom_call_target="tpu_custom_call" | custom-call | flops 4227858432 | bytes 8257536 | tf_op jit(solution)/shard_map/feed_weight_grads/pallas_call | solution.py:793
  153.4 23.1 %cross_first_back.1 = (f32[448,768]{1,0:T(8,128)}, bf16[448,768]{1,0:T(8,128)(2,1)}, bf16[2,448,384]{2,1,0:T(8,128)(2,1)}, f32[1,768]{1,0:T(1,128)}, f32[2,448,3...) custom-call(s32[4]{0:T(128)} %iota_xor_fusion.order, s32[4]{0:T(128)} %lengths.15, ...), custom_call_target="tpu_custom_call" | custom-call | flops 17666408448 | bytes 11796480 | tf_op jit(solution)/shard_map/cross_first_back/pallas_call | solution.py:633
  176.5 4.6 %all-to-all-start.2 = ((bf16[8,96,768]{2,1,0:T(8,128)(2,1)}), bf16[8,96,768]{2,1,0:T(8,128)(2,1)}, u32[]{:S(2)}, u32[]{:S(2)}) async-start(bf16[8,96,768]{2,1,0:T(8,128)(2,1)} %bitcast.62), calls=%async_computation.2 | async-start | bytes 2359296 | tf_op jit(solution)/shard_map/all_to_all | solution.py:1165
  190.3 23.4 %cross_second_back.1 = (bf16[2,448,384]{2,1,0:T(8,128)(2,1)}, bf16[1536,768]{1,0:T(8,128)(2,1)}, bf16[768,768]{1,0:T(8,128)(2,1)}, f32[448,768]{1,0:T(8,128)}, b...) custom-call(bf16[2,448,384]{2,1,0:T(8,128)(2,1)} %get-tuple-element., ...), custom_call_target="tpu_custom_call" | custom-call | flops 17666408448 | bytes 11796480 | tf_op jit(solution)/shard_map/cross_second_back/pallas_call | solution.py:705
  222.7 10.3 %head_weight_grads.1 = (bf16[2,768,768]{2,1,0:T(8,128)(2,1)}, bf16[2,768,768]{2,1,0:T(8,128)(2,1)}) custom-call(bf16[768,768]{1,0:T(8,128)(2,1)} %bitcast.58, bf16[768,768]{1,0:T(8,128)(2,1)} %bitcast.60, bf16[1536,768]{1,0:T(8,128)(2,1)} %get-tuple-element.304.dkv0, bf16[1536,768]{1,0:T(8,128)(2,1)} %get-tuple-element.314.dkv1, ...), custom_call_target="tpu_custom_call" | custom-call | flops 234042163200 | bytes 353894400 | tf_op jit(solution)/shard_map/head_weight_grads/pallas_call | solution.py:824
  234.2 4.5 %all-to-all-start.3 = ((bf16[8,96,768]{2,1,0:T(8,128)(2,1)}), bf16[8,96,768]{2,1,0:T(8,128)(2,1)S(1)}, u32[]{:S(2)}, u32[]{:S(2)}) async-start(bf16[8,96,768]{2,1,0:T(8,128)(2,1)} %bitcast.61), calls=%async_computation.3 | async-start | bytes 2359296 | tf_op jit(solution)/shard_map/all_to_all | solution.py:1165
  244.6 9.4 %self_backward.2 = (bf16[2,448,192]{2,1,0:T(8,128)(2,1)}, bf16[2,384,448]{2,1,0:T(8,128)(2,1)}, bf16[448,768]{1,0:T(8,128)(2,1)}, bf16[448,768]{1,0:T(8,128)(2,1)}) custom-call(s32[2]{0:T(128)} %get-tuple-element.343.order, s32[4]{0:T(128)} %lengths.15, bf16[2,3,448,192]{3,2,1,0:T(8,128)(2,1)} %get-tuple-element.344.qkv_ref, ...), custom_call_target="tpu_custom_call" | custom-call | flops 2334 | bytes 5 | tf_op jit(solution)/shard_map/self_backward/pallas_call | solution.py:297
  255.5 4.4 %merge_heads.1 = (bf16[4,96,768]{2,1,0:T(8,128)(2,1)}, bf16[4,96,768]{2,1,0:T(8,128)(2,1)}, bf16[4,96,768]{2,1,0:T(8,128)(2,1)}, bf16[4,96,768]{2,1,0:T(8,128)(2,1)}) custom-call(s32[8]{0:T(128)} %shift-right-arithmetic_and_fusion.bits, bf16[2,8,96,768]{3,2,1,0:T(8,128)(2,1)} %bitcast.53, bf16[2,8,96,768]{3,2,1,0:T(8,128)(2,1)} %bitcast.54), custom_call_target="tpu_custom_call" | custom-call | bytes 7 | tf_op jit(solution)/shard_map/merge_heads/pallas_call | solution.py:944
  263.1 9.5 %self_backward.3 = (bf16[2,448,192]{2,1,0:T(8,128)(2,1)}, bf16[2,384,448]{2,1,0:T(8,128)(2,1)}, bf16[448,768]{1,0:T(8,128)(2,1)}, bf16[448,768]{1,0:T(8,128)(2,1)}) custom-call(s32[2]{0:T(128)} %get-tuple-element.358.order, s32[4]{0:T(128)} %lengths.15, bf16[2,3,448,192]{3,2,1,0:T(8,128)(2,1)} %get-tuple-element.359.qkv_ref, ...), custom_call_target="tpu_custom_call" | custom-call | flops 2334 | bytes 5 | tf_op jit(solution)/shard_map/self_backward/pallas_call | solution.py:297
  285.3 7.0 %self_weight_grads.1 = (bf16[4,96,768]{2,1,0:T(8,128)(2,1)}, bf16[4,96,768]{2,1,0:T(8,128)(2,1)}) custom-call(s32[8]{0:T(128)} %shift-right-arithmetic_and_fusion.bits, bf16[2,448,768]{2,1,0:T(8,128)(2,1)} %get-tuple-element.381.near, bf16[2,448,768]{2,1,0:T(8,128)(2,1)} %get-tuple-element.382.far, bf16[2,448,192]{2,1,0:T(8,128)(2,1)} %get-tuple-element.383.dq_near, ...), custom_call_target="tpu_custom_call" | custom-call | flops 79272345600 | bytes 275251200 | tf_op jit(solution)/shard_map/self_weight_grads/pallas_call | solution.py:877
  302.5 4.6 %norm_one_back.1 = (bf16[448,768]{1,0:T(8,128)(2,1)}, f32[1,768]{1,0:T(1,128)}) custom-call(s32[4]{0:T(128)} %iota_xor_fusion.order, bf16[4,448,768]{2,1,0:T(8,128)(2,1)} %token_ref.7, bf16[448,768]{1,0:T(8,128)(2,1)} %get-tuple-element.394.own_ref, bf16[448,768]{1,0:T(8,128)(2,1)} %copy-done.23, bf16[448,768]{1,0:T(8,128)(2,1)} %copy-done.24, ...), custom_call_target="tpu_custom_call" | custom-call | bytes 240844800 | tf_op jit(solution)/shard_map/norm_one_back/pallas_call | solution.py:749
  324.2 5.4 %collective-permute-done.47 = bf16[2,1,96,768]{3,2,0,1:T(8,128)(2,1)S(1)} collective-permute-done((bf16[2,1,96,768]{3,2,0,1:T(8,128)(2,1)}, bf16[2,1,96,768]{3,2,0,1:T(8,128)(2,1)S(1)}, u32[]{:S(2)}, u32[]{:S(2)}) %collective-permute-start.47) | collective-permute-done | bytes 294944 | tf_op jit(solution)/shard_map/ppermute | solution.py:79
  346.9 11.5 %collective-permute-done.53 = f32[4,768]{1,0:T(4,128)S(1)} collective-permute-done((f32[4,768]{1,0:T(4,128)S(1)}, f32[4,768]{1,0:T(4,128)S(1)}, u32[]{:S(2)}, u32[]{:S(2)}) %collective-permute-start.53) | collective-permute-done | bytes 12320 | tf_op jit(solution)/shard_map/ppermute | solution.py:79
  (287 shorter events, 147.1 us)
Async XLA Ops:
  4.5 38.5 %all-to-all-start.1 = ((bf16[8,96,768]{2,1,0:T(8,128)(2,1)}), bf16[8,96,768]{2,1,0:T(8,128)(2,1)S(1)}, u32[]{:S(2)}, u32[]{:S(2)}) async-start(bf16[8,96,768]{2,1,0:T(8,128)(2,1)} %encode.2), calls=%async_computation.1 | async-start | bytes 2359296 | tf_op jit(solution)/shard_map/all_to_all | solution.py:1089
  12.0 21.3 %collective-permute-start.3 = (bf16[384,768]{1,0:T(8,128)(2,1)S(1)}, bf16[384,768]{1,0:T(8,128)(2,1)S(1)}, u32[]{:S(2)}, u32[]{:S(2)}) collective-permute-start(bf16[384,768]{1,0:T(8,128)(2,1)S(1)} %pad_maximum_fusion.p0), channel_id=1, source_target_pairs={{0,2},{1,3},{2,0},{3,1},{4,6},{5,7},{6,4},{7,5},{8,10},{9,11},{10,... | collective-permute-start | bytes 1769480 | tf_op jit(solution)/shard_map/ppermute | solution.py:79
  13.6 19.7 %collective-permute-start.2 = (bf16[384,768]{1,0:T(8,128)(2,1)S(1)}, bf16[384,768]{1,0:T(8,128)(2,1)S(1)}, u32[]{:S(2)}, u32[]{:S(2)}) collective-permute-start(bf16[384,768]{1,0:T(8,128)(2,1)S(1)} %pad_maximum_fusion.p0), channel_id=1, source_target_pairs={{0,1},{1,0},{2,3},{3,2},{4,5},{5,4},{6,7},{7,6},{8,9},{9,8},{10,11... | collective-permute-start | bytes 1769480 | tf_op jit(solution)/shard_map/ppermute | solution.py:79
  43.0 35.4 %all-to-all-start = ((bf16[8,96,768]{2,1,0:T(8,128)(2,1)}), bf16[8,96,768]{2,1,0:T(8,128)(2,1)S(1)}, u32[]{:S(2)}, u32[]{:S(2)}) async-start(bf16[8,96,768]{2,1,0:T(8,128)(2,1)} %encode.3), calls=%async_computation | async-start | bytes 2359296 | tf_op jit(solution)/shard_map/all_to_all | solution.py:1089
  98.0 18.1 %collective-permute-start.13 = (bf16[448,768]{1,0:T(8,128)(2,1)}, bf16[448,768]{1,0:T(8,128)(2,1)S(1)}, u32[]{:S(2)}, u32[]{:S(2)}) collective-permute-start(bf16[448,768]{1,0:T(8,128)(2,1)} %get-tuple-element.276.refs_0_), channel_id=1, source_target_pairs={{0,2},{1,3},{2,0},{3,1},{4,6},{5,7},{6,4},{7,5},{8,10},{9,11},{10,... | collective-permute-start | bytes 2064392 | tf_op jit(solution)/shard_map/ppermute | solution.py:79
  134.9 17.5 %collective-permute-start.20 = (bf16[448,768]{1,0:T(8,128)(2,1)S(1)}, bf16[448,768]{1,0:T(8,128)(2,1)S(1)}, u32[]{:S(2)}, u32[]{:S(2)}) collective-permute-start(bf16[448,768]{1,0:T(8,128)(2,1)S(1)} %add_convert_fusion.3), channel_id=1, source_target_pairs={{0,2},{1,3},{2,0},{3,1},{4,6},{5,7},{6,4},{7,5},{8,10},{9,11},{10,... | collective-permute-start | bytes 2064392 | tf_op jit(solution)/shard_map/ppermute | solution.py:79
  148.0 36.1 %collective-permute-start.22 = (bf16[2,4,96,768]{3,2,1,0:T(8,128)(2,1)}, bf16[2,4,96,768]{3,2,1,0:T(8,128)(2,1)S(1)}, u32[]{:S(2)}, u32[]{:S(2)}) collective-permute-start(bf16[2,4,96,768]{3,2,1,0:T(8,128)(2,1)} %get-tuple-element.295), channel_id=1, source_target_pairs={{0,4},{4,0},{8,12},{12,8},{16,20},{20,16},{24,28},{28,24},{1,5},{5... | collective-permute-start | bytes 3538952 | tf_op jit(solution)/shard_map/ppermute | solution.py:79
  152.5 28.6 %collective-permute-start.21 = (bf16[448,768]{1,0:T(8,128)(2,1)S(1)}, bf16[448,768]{1,0:T(8,128)(2,1)}, u32[]{:S(2)}, u32[]{:S(2)}) collective-permute-start(bf16[448,768]{1,0:T(8,128)(2,1)S(1)} %add_convert_fusion.2), channel_id=1, source_target_pairs={{0,2},{1,3},{2,0},{3,1},{4,6},{5,7},{6,4},{7,5},{8,10},{9,11},{10,... | collective-permute-start | bytes 2064392 | tf_op jit(solution)/shard_map/ppermute | solution.py:79
  176.5 57.7 %all-to-all-start.2 = ((bf16[8,96,768]{2,1,0:T(8,128)(2,1)}), bf16[8,96,768]{2,1,0:T(8,128)(2,1)}, u32[]{:S(2)}, u32[]{:S(2)}) async-start(bf16[8,96,768]{2,1,0:T(8,128)(2,1)} %bitcast.62), calls=%async_computation.2 | async-start | bytes 2359296 | tf_op jit(solution)/shard_map/all_to_all | solution.py:1165
  182.9 31.8 %collective-permute-start.25 = (bf16[448,768]{1,0:T(8,128)(2,1)S(1)}, bf16[448,768]{1,0:T(8,128)(2,1)}, u32[]{:S(2)}, u32[]{:S(2)}) collective-permute-start(bf16[448,768]{1,0:T(8,128)(2,1)S(1)} %add_convert_fusion.1.a), channel_id=1, source_target_pairs={{0,2},{1,3},{2,0},{3,1},{4,6},{5,7},{6,4},{7,5},{8,10},{9,11},{10,... | collective-permute-start | bytes 2064392 | tf_op jit(solution)/shard_map/ppermute | solution.py:79
  184.1 30.6 %collective-permute-start.24 = (bf16[448,768]{1,0:T(8,128)(2,1)S(1)}, bf16[448,768]{1,0:T(8,128)(2,1)S(1)}, u32[]{:S(2)}, u32[]{:S(2)}) collective-permute-start(bf16[448,768]{1,0:T(8,128)(2,1)S(1)} %add_convert_fusion.1.a), channel_id=1, source_target_pairs={{0,1},{1,0},{2,3},{3,2},{4,5},{5,4},{6,7},{7,6},{8,9},{9,8},{10,11... | collective-permute-start | bytes 2064392 | tf_op jit(solution)/shard_map/ppermute | solution.py:79
  188.4 26.3 %collective-permute-start.23 = (bf16[4,1,96,768]{3,2,1,0:T(8,128)(2,1)}, bf16[4,1,96,768]{3,2,1,0:T(8,128)(2,1)S(1)}, u32[]{:S(2)}, u32[]{:S(2)}) collective-permute-start(bf16[4,1,96,768]{3,2,1,0:T(8,128)(2,1)} %get-tuple-element.320), channel_id=1, source_target_pairs={{0,8},{4,12},{8,0},{12,4},{16,24},{20,28},{24,16},{28,20},{1,9},{5... | collective-permute-start | bytes 1769480 | tf_op jit(solution)/shard_map/ppermute | solution.py:79
  234.2 19.8 %collective-permute-start.31 = (bf16[2,768,768]{2,1,0:T(8,128)(2,1)}, bf16[2,768,768]{2,1,0:T(8,128)(2,1)S(1)}, u32[]{:S(2)}, u32[]{:S(2)}) collective-permute-start(bf16[2,768,768]{2,1,0:T(8,128)(2,1)} %get-tuple-element.339), channel_id=1, source_target_pairs={{0,1},{1,0},{2,3},{3,2},{4,5},{5,4},{6,7},{7,6},{8,9},{9,8},{10,11... | collective-permute-start | bytes 7077896 | tf_op jit(solution)/shard_map/ppermute | solution.py:79
  234.2 39.5 %all-to-all-start.3 = ((bf16[8,96,768]{2,1,0:T(8,128)(2,1)}), bf16[8,96,768]{2,1,0:T(8,128)(2,1)S(1)}, u32[]{:S(2)}, u32[]{:S(2)}) async-start(bf16[8,96,768]{2,1,0:T(8,128)(2,1)} %bitcast.61), calls=%async_computation.3 | async-start | bytes 2359296 | tf_op jit(solution)/shard_map/all_to_all | solution.py:1165
  243.2 29.5 %collective-permute-start.35 = (bf16[8,96,768]{2,1,0:T(8,128)(2,1)}, bf16[8,96,768]{2,1,0:T(8,128)(2,1)S(1)}, u32[]{:S(2)}, u32[]{:S(2)}) collective-permute-start(bf16[8,96,768]{2,1,0:T(8,128)(2,1)} %get-tuple-element.424.a), channel_id=1, source_target_pairs={{0,2},{1,3},{2,0},{3,1},{4,6},{5,7},{6,4},{7,5},{8,10},{9,11},{10,... | collective-permute-start | bytes 3538952 | tf_op jit(solution)/shard_map/ppermute | solution.py:79
  244.1 29.6 %collective-permute-start.34 = (bf16[8,96,768]{2,1,0:T(8,128)(2,1)}, bf16[8,96,768]{2,1,0:T(8,128)(2,1)}, u32[]{:S(2)}, u32[]{:S(2)}) collective-permute-start(bf16[8,96,768]{2,1,0:T(8,128)(2,1)} %get-tuple-element.424.a), channel_id=1, source_target_pairs={{0,1},{1,0},{2,3},{3,2},{4,5},{5,4},{6,7},{7,6},{8,9},{9,8},{10,11... | collective-permute-start | bytes 3538952 | tf_op jit(solution)/shard_map/ppermute | solution.py:79
  276.1 21.3 %collective-permute-start.40 = (bf16[4,96,768]{2,1,0:T(8,128)(2,1)S(1)}, bf16[4,96,768]{2,1,0:T(8,128)(2,1)S(1)}, u32[]{:S(2)}, u32[]{:S(2)}) collective-permute-start(bf16[4,96,768]{2,1,0:T(8,128)(2,1)S(1)} %copy-done.57), channel_id=1, source_target_pairs={{0,4},{4,0},{8,12},{12,8},{16,20},{20,16},{24,28},{28,24},{1,5},{5... | collective-permute-start | bytes 1769480 | tf_op jit(solution)/shard_map/ppermute | solution.py:79
  292.3 21.9 %collective-permute-start.43 = (bf16[4,96,768]{2,1,0:T(8,128)(2,1)}, bf16[4,96,768]{2,1,0:T(8,128)(2,1)S(1)}, u32[]{:S(2)}, u32[]{:S(2)}) collective-permute-start(bf16[4,96,768]{2,1,0:T(8,128)(2,1)} %get-tuple-element.387), channel_id=1, source_target_pairs={{0,4},{4,0},{8,12},{12,8},{16,20},{20,16},{24,28},{28,24},{1,5},{5... | collective-permute-start | bytes 1769480 | tf_op jit(solution)/shard_map/ppermute | solution.py:79
  307.2 26.3 %collective-permute-start.50 = (bf16[448,768]{1,0:T(8,128)(2,1)}, bf16[448,768]{1,0:T(8,128)(2,1)S(1)}, u32[]{:S(2)}, u32[]{:S(2)}) collective-permute-start(bf16[448,768]{1,0:T(8,128)(2,1)} %get-tuple-element.433.a), channel_id=1, source_target_pairs={{0,2},{1,3},{2,0},{3,1},{4,6},{5,7},{6,4},{7,5},{8,10},{9,11},{10,... | collective-permute-start | bytes 2064392 | tf_op jit(solution)/shard_map/ppermute | solution.py:79
  308.0 25.5 %collective-permute-start.49 = (bf16[448,768]{1,0:T(8,128)(2,1)}, bf16[448,768]{1,0:T(8,128)(2,1)S(1)}, u32[]{:S(2)}, u32[]{:S(2)}) collective-permute-start(bf16[448,768]{1,0:T(8,128)(2,1)} %get-tuple-element.433.a), channel_id=1, source_target_pairs={{0,1},{1,0},{2,3},{3,2},{4,5},{5,4},{6,7},{7,6},{8,9},{9,8},{10,11... | collective-permute-start | bytes 2064392 | tf_op jit(solution)/shard_map/ppermute | solution.py:79
  333.5 26.9 %collective-permute-start.55 = (bf16[8,96,768]{2,1,0:T(8,128)(2,1)S(1)}, bf16[8,96,768]{2,1,0:T(8,128)(2,1)S(1)}, u32[]{:S(2)}, u32[]{:S(2)}) collective-permute-start(bf16[8,96,768]{2,1,0:T(8,128)(2,1)S(1)} %copy-done.5), channel_id=1, source_target_pairs={{0,2},{1,3},{2,0},{3,1},{4,6},{5,7},{6,4},{7,5},{8,10},{9,11},{10,... | collective-permute-start | bytes 3538952 | tf_op jit(solution)/shard_map/ppermute | solution.py:79
  334.7 25.7 %collective-permute-start.54 = (bf16[8,96,768]{2,1,0:T(8,128)(2,1)S(1)}, bf16[8,96,768]{2,1,0:T(8,128)(2,1)S(1)}, u32[]{:S(2)}, u32[]{:S(2)}) collective-permute-start(bf16[8,96,768]{2,1,0:T(8,128)(2,1)S(1)} %copy-done.5), channel_id=1, source_target_pairs={{0,1},{1,0},{2,3},{3,2},{4,5},{5,4},{6,7},{7,6},{8,9},{9,8},{10,11... | collective-permute-start | bytes 3538952 | tf_op jit(solution)/shard_map/ppermute | solution.py:79
  335.2 23.2 %collective-permute-start.52 = (bf16[3,1,96,768]{3,2,0,1:T(8,128)(2,1)}, bf16[3,1,96,768]{3,2,0,1:T(8,128)(2,1)S(1)}, u32[]{:S(2)}, u32[]{:S(2)}) collective-permute-start(bf16[3,1,96,768]{3,2,0,1:T(8,128)(2,1)} %bitcast.81), channel_id=1, source_target_pairs={{0,16},{4,20},{8,24},{12,28},{16,0},{20,4},{24,8},{28,12},{1,17},{... | collective-permute-start | bytes 1327112 | tf_op jit(solution)/shard_map/ppermute | solution.py:79
  337.6 20.8 %collective-permute-start.53 = (f32[4,768]{1,0:T(4,128)S(1)}, f32[4,768]{1,0:T(4,128)S(1)}, u32[]{:S(2)}, u32[]{:S(2)}) collective-permute-start(f32[4,768]{1,0:T(4,128)S(1)} %add.59), channel_id=1, source_target_pairs={{0,16},{4,20},{8,24},{12,28},{16,0},{20,4},{24,8},{28,12},{1,17},{... | collective-permute-start | bytes 36872 | tf_op jit(solution)/shard_map/ppermute | solution.py:79
  (106 other events, 843.1 us)

commit v6 on v5

--- a/solution.py
+++ b/solution.py
@@ -14,7 +14,7 @@
 INV_ROOT = HEAD_DIM**-0.5
 F32 = jnp.float32
 BF16 = jnp.bfloat16
-VMEM_LIMIT = 56 << 20
+VMEM_LIMIT = 52 << 20
 COST_SCALE = 1.0
 LONG = 50.0
 SHORT = 1e-6

time: 384 us -> 373 us (0.971)
  Pallas kernels: 238 us -> 219 us
  local copies, waits for them, and re-layouts: 14.9 us -> 19.2 us
    pallas_call x5, Pallas kernels: 15.1 us -> 8.66 us  [merge(): call(functools.partial(merge_body, which=which, joined=joined), (rows //...]
    unnamed x130 -> x152, local copies, waits for them, and re-layouts: 13.3 us -> 17.6 us
  transfers between devices with their start and end apart: 65 -> 65, of which waited for: 17 -> 18; matrix products, arithmetic and copies ran while one was open for 2% -> 3% of each run, Pallas kernels for 55% -> 52%
where the time goes in v6:
time: 373 us; the launch traced here: 366 us
  Pallas kernels  219 us (59%)
  starting transfers between devices  66.4 us (18%)
  waiting for transfers between devices  51.3 us (14%)
  local copies, waits for them, and re-layouts  19.2 us (5%)
  other arithmetic  8.75 us (2%)
    ppermute x61, waiting for transfers between devices, swap(): return lax.ppermute(values, axis, [(i, i ^ bit) for i in range(size)])  47 us
    ppermute x61, starting transfers between devices, swap(): return lax.ppermute(values, axis, [(i, i ^ bit) for i in range(size)])  43.9 us
    pallas_call x1, Pallas kernels, cross_second_back(): call(functools.partial(cross_second_back_body, valid=valid), (2,), [head_...  23.2 us
    pallas_call x3, Pallas kernels, feed_forward(): call(functools.partial(feed_body, count=count), (count, tiles), single +...  22.7 us
    pallas_call x1, Pallas kernels, cross_first_back(): call(functools.partial(cross_first_back_body, valid=valid), (2,), [pl.Blo...  22.3 us
    pallas_call x2, Pallas kernels, self_bwd(): call(self_bwd_body, (2,), [pl.BlockSpec((1, 3, seq, local), lambda i, *_:...  18 us
    pallas_call x1, Pallas kernels, cross_second(): call(functools.partial(cross_second_body, valid=valid), (2,), [rows, whol...  17.7 us
    unnamed x152, local copies, waits for them, and re-layouts  17.6 us
  transfers between devices with their start and end apart: 65, of which 18 were waited for; matrix products, arithmetic and copies ran while one was open for 3% of the time, Pallas kernels for 52%

profile of v6, /device:TPU:0, one launch (start us, length us, event | category | flops | bytes accessed | tf_op | source)
XLA Modules:
  0.0 366.4 jit_solution(8562244946971395363)
XLA Ops:
  4.6 7.4 %all-to-all-start.1 = ((bf16[8,96,768]{2,1,0:T(8,128)(2,1)}), bf16[8,96,768]{2,1,0:T(8,128)(2,1)}, u32[]{:S(2)}, u32[]{:S(2)}) async-start(bf16[8,96,768]{2,1,0:T(8,128)(2,1)} %encode.2), calls=%async_computation.1 | async-start | bytes 2359296 | tf_op jit(solution)/shard_map/all_to_all | solution.py:1089
  13.8 8.3 %self_forward.2 = (bf16[2,448,768]{2,1,0:T(8,128)(2,1)}, bf16[2,3,448,192]{3,2,1,0:T(8,128)(2,1)}, bf16[448,192]{1,0:T(8,128)(2,1)S(1)}, bf16[448,192]{1,0:T(8,128)(2,1)S(1)}, f32[2,3,448]{2,1,0:T(4,128)S(1)}) custom-call(s32[2]{0:T(128)S(1)} %get-tuple-element.358.order, s32[4]{0:T(128)S(1)} %copy-done.27, bf16[4,448,768]{2,1,0:T(8,128)(2,1)} %token_ref.7, ...), custom_call_target="tpu_custom_call" | custom-call | flops 1409286144 | bytes 5505024 | tf_op jit(solution)/shard_map/self_forward/pallas_call | solution.py:208
  23.2 8.3 %self_forward.3 = (bf16[2,448,768]{2,1,0:T(8,128)(2,1)}, bf16[2,3,448,192]{3,2,1,0:T(8,128)(2,1)}, bf16[448,192]{1,0:T(8,128)(2,1)S(1)}, bf16[448,192]{1,0:T(8,128)(2,1)S(1)}, f32[2,3,448]{2,1,0:T(4,128)S(1)}) custom-call(s32[2]{0:T(128)S(1)} %get-tuple-element.343.order, s32[4]{0:T(128)S(1)} %copy-done.27, bf16[4,448,768]{2,1,0:T(8,128)(2,1)} %token_ref.7, ...), custom_call_target="tpu_custom_call" | custom-call | flops 70464307200 | bytes 275251200 | tf_op jit(solution)/shard_map/self_forward/pallas_call | solution.py:208
  42.4 6.2 %all-to-all-start = ((bf16[8,96,768]{2,1,0:T(8,128)(2,1)}), bf16[8,96,768]{2,1,0:T(8,128)(2,1)}, u32[]{:S(2)}, u32[]{:S(2)}) async-start(bf16[8,96,768]{2,1,0:T(8,128)(2,1)} %encode.3), calls=%async_computation | async-start | bytes 2359296 | tf_op jit(solution)/shard_map/all_to_all | solution.py:1089
  48.7 6.1 %self_out_to_query.1 = (f32[448,768]{1,0:T(8,128)}, bf16[448,768]{1,0:T(8,128)(2,1)}, bf16[2,448,384]{2,1,0:T(8,128)(2,1)}) custom-call(s32[4]{0:T(128)S(1)} %iota_xor_fusion.order, bf16[4,448,768]{2,1,0:T(8,128)(2,1)} %token_ref.7, bf16[448,192]{1,0:T(8,128)(2,1)S(1)} %get-tuple-element.253.m0.mixed1_ref, bf16[448,192]{1,0:T(8,128)(2,1)S(1)} %collective-permute-done.4.m1, ...), custom_call_target="tpu_custom_call" | custom-call | flops 1056964608 | bytes 6488064 | tf_op jit(solution)/shard_map/self_out_to_query/pallas_call | solution.py:340
  57.9 14.2 %cross_first.1 = (bf16[768,1536]{1,0:T(8,128)(2,1)}, f32[2,384,448]{2,1,0:T(8,128)}, f32[2,6,448]{2,1,0:T(8,128)S(1)}, f32[2,6,448]{2,1,0:T(8,128)S(1)}) custom-call(bf16[2,448,384]{2,1,0:T(8,128)(2,1)} %get-tuple-element.267.query_ref, bf16[768,768]{1,0:T(8,128)(2,1)} %bitcast.6.encoded_ref.enc0, bf16[384,768]{1,0:T(8,128)(2,1)S(1)} %bitcast.65, ...), custom_call_target="tpu_custom_call" | custom-call | flops 7096762368 | bytes 4718592 | tf_op jit(solution)/shard_map/cross_first/pallas_call | solution.py:444
  77.9 17.7 %cross_second.1 = (bf16[768,1536]{1,0:T(8,128)(2,1)}, bf16[2,448,384]{2,1,0:T(8,128)(2,1)}, f32[2,6,448]{2,1,0:T(8,128)S(1)}, f32[448,768]{1,0:T(8,128)}, bf16[448,768]{1,0:T(8,128)(2,1)}) custom-call(bf16[2,448,384]{2,1,0:T(8,128)(2,1)} %get-tuple-element.267.query_ref, bf16[768,768]{1,0:T(8,128)(2,1)} %bitcast.5.encoded_ref.enc1, ...), custom_call_target="tpu_custom_call" | custom-call | flops 7096762368 | bytes 5898240 | tf_op jit(solution)/shard_map/cross_second/pallas_call | solution.py:472
  98.9 9.6 %feed_forward.3 = (bf16[2,448,768]{2,1,0:T(8,128)(2,1)}, bf16[2,448,768]{2,1,0:T(8,128)(2,1)}, bf16[2,448,768]{2,1,0:T(8,128)(2,1)}, bf16[448,768]{1,0:T(8,128)(...) custom-call(s32[2]{0:T(128)S(1)} %bitcast.62, s32[4]{0:T(128)S(1)} %copy-done.27, ...), custom_call_target="tpu_custom_call" | custom-call | flops 4227858432 | bytes 9633792 | tf_op jit(solution)/shard_map/feed_forward/pallas_call | solution.py:534
  109.4 4.4 %collective-permute-done.13.refs_0_.refs_2_ = bf16[448,768]{1,0:T(8,128)(2,1)S(1)} collective-permute-done((bf16[448,768]{1,0:T(8,128)(2,1)}, bf16[448,768]{1,0:T(8,128)(2,1)S(1)}, u32[]{:S(2)}, u32[]{:S(2)}) %collective-permute-start.13) | collective-permute-done | bytes 688160 | tf_op jit(solution)/shard_map/ppermute | solution.py:79
  116.8 6.5 %feed_forward.4 = (bf16[1,448,768]{2,1,0:T(8,128)(2,1)S(1)}, bf16[1,448,768]{2,1,0:T(8,128)(2,1)S(1)}, bf16[1,448,768]{2,1,0:T(8,128)(2,1)}, bf16[448,768]{1,0:T(8,128)(2,1)}, bf16[448,768]{1,0:T(8,128)(2,1)}) custom-call(s32[1]{0:T(128)} %get-tuple-element.468.order, s32[4]{0:T(128)S(1)} %copy-done.27, bf16[448,768]{1,0:T(8,128)(2,1)} %copy-done.73, ...), custom_call_target="tpu_custom_call" | custom-call | flops 2113929216 | bytes 4816896 | tf_op jit(solution)/shard_map/feed_forward/pallas_call | solution.py:534
  126.1 6.5 %feed_forward.5 = (bf16[1,448,768]{2,1,0:T(8,128)(2,1)S(1)}, bf16[1,448,768]{2,1,0:T(8,128)(2,1)S(1)}, bf16[1,448,768]{2,1,0:T(8,128)(2,1)}, bf16[448,768]{1,0:T(8,128)(2,1)}, bf16[448,768]{1,0:T(8,128)(2,1)}) custom-call(s32[1]{0:T(128)} %get-tuple-element.280.order, s32[4]{0:T(128)S(1)} %copy-done.27, bf16[448,768]{1,0:T(8,128)(2,1)} %copy-done.72, ...), custom_call_target="tpu_custom_call" | custom-call | flops 2113929216 | bytes 4816896 | tf_op jit(solution)/shard_map/feed_forward/pallas_call | solution.py:534
  136.6 10.9 %feed_weight_grads.1 = (bf16[2,4,96,768]{3,2,1,0:T(8,128)(2,1)}, bf16[2,4,96,768]{3,2,1,0:T(8,128)(2,1)}) custom-call(s32[8]{0:T(128)S(1)} %shift-right-arithmetic_and_fusion.bits, bf16[448,768]{1,0:T(8,128)(2,1)S(1)} %copy-done.34, bf16[448,768]{1,0:T(8,128)(2,1)S(1)} %copy-done.36, bf16[448,768]{1,0:T(8,128)(2,1)} %copy-done.72, ...), custom_call_target="tpu_custom_call" | custom-call | flops 4227858432 | bytes 8257536 | tf_op jit(solution)/shard_map/feed_weight_grads/pallas_call | solution.py:793
  154.3 22.3 %cross_first_back.1 = (f32[448,768]{1,0:T(8,128)}, bf16[448,768]{1,0:T(8,128)(2,1)}, bf16[2,448,384]{2,1,0:T(8,128)(2,1)}, f32[1,768]{1,0:T(1,128)S(1)}, f32[2,4...) custom-call(s32[4]{0:T(128)S(1)} %iota_xor_fusion.order, s32[4]{0:T(128)S(1)} %copy-done.27, ...), custom_call_target="tpu_custom_call" | custom-call | flops 17666408448 | bytes 11796480 | tf_op jit(solution)/shard_map/cross_first_back/pallas_call | solution.py:633
  176.6 4.4 %all-to-all-start.2 = ((bf16[8,96,768]{2,1,0:T(8,128)(2,1)}), bf16[8,96,768]{2,1,0:T(8,128)(2,1)}, u32[]{:S(2)}, u32[]{:S(2)}) async-start(bf16[8,96,768]{2,1,0:T(8,128)(2,1)} %bitcast.80), calls=%async_computation.2 | async-start | bytes 2359296 | tf_op jit(solution)/shard_map/all_to_all | solution.py:1165
  188.8 23.2 %cross_second_back.1 = (bf16[2,448,384]{2,1,0:T(8,128)(2,1)}, bf16[1536,768]{1,0:T(8,128)(2,1)}, bf16[768,768]{1,0:T(8,128)(2,1)}, f32[448,768]{1,0:T(8,128)}, b...) custom-call(bf16[2,448,384]{2,1,0:T(8,128)(2,1)} %get-tuple-element., ...), custom_call_target="tpu_custom_call" | custom-call | flops 17666408448 | bytes 11796480 | tf_op jit(solution)/shard_map/cross_second_back/pallas_call | solution.py:705
  221.5 10.5 %head_weight_grads.1 = (bf16[2,768,768]{2,1,0:T(8,128)(2,1)}, bf16[2,768,768]{2,1,0:T(8,128)(2,1)}) custom-call(bf16[768,768]{1,0:T(8,128)(2,1)} %bitcast.6.encoded_ref.enc0, bf16[768,768]{1,0:T(8,128)(2,1)} %bitcast.5.encoded_ref.enc1, bf16[1536,768]{1,0:T(8,128)(2,1)} %get-tuple-element.304.dkv0, bf16[1536,768]{1,0:T(8,128)(2,1)} %get-tuple-element.314.dkv1, ...), custom_call_target="tpu_custom_call" | custom-call | flops 234042163200 | bytes 353894400 | tf_op jit(solution)/shard_map/head_weight_grads/pallas_call | solution.py:824
  232.7 4.5 %all-to-all-start.3 = ((bf16[8,96,768]{2,1,0:T(8,128)(2,1)}), bf16[8,96,768]{2,1,0:T(8,128)(2,1)}, u32[]{:S(2)}, u32[]{:S(2)}) async-start(bf16[8,96,768]{2,1,0:T(8,128)(2,1)} %bitcast.79), calls=%async_computation.3 | async-start | bytes 2359296 | tf_op jit(solution)/shard_map/all_to_all | solution.py:1165
  242.4 9.0 %self_backward.2 = (bf16[2,448,192]{2,1,0:T(8,128)(2,1)S(1)}, bf16[2,384,448]{2,1,0:T(8,128)(2,1)}, bf16[448,768]{1,0:T(8,128)(2,1)}, bf16[448,768]{1,0:T(8,128)(2,1)}) custom-call(s32[2]{0:T(128)S(1)} %copy-done.32, s32[4]{0:T(128)S(1)} %copy-done.27, bf16[2,3,448,192]{3,2,1,0:T(8,128)(2,1)} %get-tuple-element.344.qkv_ref, bf16[448,192]{1,0:T(8,128)(2,1)S(1)} %copy-done.21, ...), custom_call_target="tpu_custom_call" | custom-call | flops 2334 | bytes 5 | tf_op jit(solution)/shard_map/self_backward/pallas_call | solution.py:297
  260.0 9.0 %self_backward.3 = (bf16[2,448,192]{2,1,0:T(8,128)(2,1)S(1)}, bf16[2,384,448]{2,1,0:T(8,128)(2,1)}, bf16[448,768]{1,0:T(8,128)(2,1)}, bf16[448,768]{1,0:T(8,128)(2,1)}) custom-call(s32[2]{0:T(128)S(1)} %copy-done.30, s32[4]{0:T(128)S(1)} %copy-done.28, bf16[2,3,448,192]{3,2,1,0:T(8,128)(2,1)} %get-tuple-element.359.qkv_ref, bf16[448,192]{1,0:T(8,128)(2,1)S(1)} %copy-done.17, ...), custom_call_target="tpu_custom_call" | custom-call | flops 2334 | bytes 5 | tf_op jit(solution)/shard_map/self_backward/pallas_call | solution.py:297
  281.7 6.2 %self_weight_grads.1 = (bf16[4,96,768]{2,1,0:T(8,128)(2,1)S(1)}, bf16[4,96,768]{2,1,0:T(8,128)(2,1)}) custom-call(s32[8]{0:T(128)S(1)} %shift-right-arithmetic_and_fusion.bits, bf16[2,448,768]{2,1,0:T(8,128)(2,1)} %get-tuple-element.381.near, bf16[2,448,768]{2,1,0:T(8,128)(2,1)} %get-tuple-element.382.far, bf16[2,448,192]{2,1,0:T(8,128)(2,1)S(1)} %copy-done.42, ...), custom_call_target="tpu_custom_call" | custom-call | flops 79272345600 | bytes 275251200 | tf_op jit(solution)/shard_map/self_weight_grads/pallas_call | solution.py:877
  289.5 4.5 %collective-permute-done.41 = bf16[4,96,768]{2,1,0:T(8,128)(2,1)S(1)} collective-permute-done((bf16[4,96,768]{2,1,0:T(8,128)(2,1)}, bf16[4,96,768]{2,1,0:T(8,128)(2,1)S(1)}, u32[]{:S(2)}, u32[]{:S(2)}) %collective-permute-start.41) | collective-permute-done | bytes 589856 | tf_op jit(solution)/shard_map/ppermute | solution.py:79
  314.7 4.4 %collective-permute-done.45 = bf16[2,1,96,768]{3,2,0,1:T(8,128)(2,1)S(1)} collective-permute-done((bf16[2,1,96,768]{3,2,0,1:T(8,128)(2,1)S(1)}, bf16[2,1,96,768]{3,2,0,1:T(8,128)(2,1)S(1)}, u32[]{:S(2)}, u32[]{:S(2)}) %collective-permute-start.45) | collective-permute-done | bytes 294944 | tf_op jit(solution)/shard_map/ppermute | solution.py:79
  319.2 5.4 %collective-permute-done.47 = bf16[2,1,96,768]{3,2,0,1:T(8,128)(2,1)S(1)} collective-permute-done((bf16[2,1,96,768]{3,2,0,1:T(8,128)(2,1)S(1)}, bf16[2,1,96,768]{3,2,0,1:T(8,128)(2,1)S(1)}, u32[]{:S(2)}, u32[]{:S(2)}) %collective-permute-start.47) | collective-permute-done | bytes 294944 | tf_op jit(solution)/shard_map/ppermute | solution.py:79
  339.9 11.3 %collective-permute-done.53 = f32[4,768]{1,0:T(4,128)S(1)} collective-permute-done((f32[4,768]{1,0:T(4,128)S(1)}, f32[4,768]{1,0:T(4,128)S(1)}, u32[]{:S(2)}, u32[]{:S(2)}) %collective-permute-start.53) | collective-permute-done | bytes 12320 | tf_op jit(solution)/shard_map/ppermute | solution.py:79
  (309 shorter events, 143.6 us)
Async XLA Ops:
  4.6 37.8 %all-to-all-start.1 = ((bf16[8,96,768]{2,1,0:T(8,128)(2,1)}), bf16[8,96,768]{2,1,0:T(8,128)(2,1)}, u32[]{:S(2)}, u32[]{:S(2)}) async-start(bf16[8,96,768]{2,1,0:T(8,128)(2,1)} %encode.2), calls=%async_computation.1 | async-start | bytes 2359296 | tf_op jit(solution)/shard_map/all_to_all | solution.py:1089
  12.1 19.8 %collective-permute-start.3 = (bf16[384,768]{1,0:T(8,128)(2,1)S(1)}, bf16[384,768]{1,0:T(8,128)(2,1)S(1)}, u32[]{:S(2)}, u32[]{:S(2)}) collective-permute-start(bf16[384,768]{1,0:T(8,128)(2,1)S(1)} %pad_maximum_fusion.p0), channel_id=1, source_target_pairs={{0,2},{1,3},{2,0},{3,1},{4,6},{5,7},{6,4},{7,5},{8,10},{9,11},{10,... | collective-permute-start | bytes 1769480 | tf_op jit(solution)/shard_map/ppermute | solution.py:79
  13.7 18.2 %collective-permute-start.2 = (bf16[384,768]{1,0:T(8,128)(2,1)S(1)}, bf16[384,768]{1,0:T(8,128)(2,1)S(1)}, u32[]{:S(2)}, u32[]{:S(2)}) collective-permute-start(bf16[384,768]{1,0:T(8,128)(2,1)S(1)} %pad_maximum_fusion.p0), channel_id=1, source_target_pairs={{0,1},{1,0},{2,3},{3,2},{4,5},{5,4},{6,7},{7,6},{8,9},{9,8},{10,11... | collective-permute-start | bytes 1769480 | tf_op jit(solution)/shard_map/ppermute | solution.py:79
  42.4 35.5 %all-to-all-start = ((bf16[8,96,768]{2,1,0:T(8,128)(2,1)}), bf16[8,96,768]{2,1,0:T(8,128)(2,1)}, u32[]{:S(2)}, u32[]{:S(2)}) async-start(bf16[8,96,768]{2,1,0:T(8,128)(2,1)} %encode.3), calls=%async_computation | async-start | bytes 2359296 | tf_op jit(solution)/shard_map/all_to_all | solution.py:1089
  95.7 18.1 %collective-permute-start.13 = (bf16[448,768]{1,0:T(8,128)(2,1)}, bf16[448,768]{1,0:T(8,128)(2,1)S(1)}, u32[]{:S(2)}, u32[]{:S(2)}) collective-permute-start(bf16[448,768]{1,0:T(8,128)(2,1)} %get-tuple-element.276.refs_0_), channel_id=1, source_target_pairs={{0,2},{1,3},{2,0},{3,1},{4,6},{5,7},{6,4},{7,5},{8,10},{9,11},{10,... | collective-permute-start | bytes 2064392 | tf_op jit(solution)/shard_map/ppermute | solution.py:79
  135.9 17.5 %collective-permute-start.20 = (bf16[448,768]{1,0:T(8,128)(2,1)S(1)}, bf16[448,768]{1,0:T(8,128)(2,1)S(1)}, u32[]{:S(2)}, u32[]{:S(2)}) collective-permute-start(bf16[448,768]{1,0:T(8,128)(2,1)S(1)} %add_convert_fusion.3), channel_id=1, source_target_pairs={{0,2},{1,3},{2,0},{3,1},{4,6},{5,7},{6,4},{7,5},{8,10},{9,11},{10,... | collective-permute-start | bytes 2064392 | tf_op jit(solution)/shard_map/ppermute | solution.py:79
  147.5 36.9 %collective-permute-start.22 = (bf16[2,4,96,768]{3,2,1,0:T(8,128)(2,1)}, bf16[2,4,96,768]{3,2,1,0:T(8,128)(2,1)}, u32[]{:S(2)}, u32[]{:S(2)}) collective-permute-start(bf16[2,4,96,768]{3,2,1,0:T(8,128)(2,1)} %get-tuple-element.295), channel_id=1, source_target_pairs={{0,4},{4,0},{8,12},{12,8},{16,20},{20,16},{24,28},{28,24},{1,5},{5... | collective-permute-start | bytes 3538952 | tf_op jit(solution)/shard_map/ppermute | solution.py:79
  153.5 27.6 %collective-permute-start.21 = (bf16[448,768]{1,0:T(8,128)(2,1)}, bf16[448,768]{1,0:T(8,128)(2,1)}, u32[]{:S(2)}, u32[]{:S(2)}) collective-permute-start(bf16[448,768]{1,0:T(8,128)(2,1)} %add_convert_fusion.2), channel_id=1, source_target_pairs={{0,2},{1,3},{2,0},{3,1},{4,6},{5,7},{6,4},{7,5},{8,10},{9,11},{10,... | collective-permute-start | bytes 2064392 | tf_op jit(solution)/shard_map/ppermute | solution.py:79
  176.6 56.1 %all-to-all-start.2 = ((bf16[8,96,768]{2,1,0:T(8,128)(2,1)}), bf16[8,96,768]{2,1,0:T(8,128)(2,1)}, u32[]{:S(2)}, u32[]{:S(2)}) async-start(bf16[8,96,768]{2,1,0:T(8,128)(2,1)} %bitcast.80), calls=%async_computation.2 | async-start | bytes 2359296 | tf_op jit(solution)/shard_map/all_to_all | solution.py:1165
  183.1 31.7 %collective-permute-start.25 = (bf16[448,768]{1,0:T(8,128)(2,1)S(1)}, bf16[448,768]{1,0:T(8,128)(2,1)}, u32[]{:S(2)}, u32[]{:S(2)}) collective-permute-start(bf16[448,768]{1,0:T(8,128)(2,1)S(1)} %add_convert_fusion.1.a), channel_id=1, source_target_pairs={{0,2},{1,3},{2,0},{3,1},{4,6},{5,7},{6,4},{7,5},{8,10},{9,11},{10,... | collective-permute-start | bytes 2064392 | tf_op jit(solution)/shard_map/ppermute | solution.py:79
  184.4 30.5 %collective-permute-start.24 = (bf16[448,768]{1,0:T(8,128)(2,1)S(1)}, bf16[448,768]{1,0:T(8,128)(2,1)S(1)}, u32[]{:S(2)}, u32[]{:S(2)}) collective-permute-start(bf16[448,768]{1,0:T(8,128)(2,1)S(1)} %add_convert_fusion.1.a), channel_id=1, source_target_pairs={{0,1},{1,0},{2,3},{3,2},{4,5},{5,4},{6,7},{7,6},{8,9},{9,8},{10,11... | collective-permute-start | bytes 2064392 | tf_op jit(solution)/shard_map/ppermute | solution.py:79
  186.7 28.1 %collective-permute-start.23 = (bf16[4,1,96,768]{3,2,1,0:T(8,128)(2,1)S(1)}, bf16[4,1,96,768]{3,2,1,0:T(8,128)(2,1)S(1)}, u32[]{:S(2)}, u32[]{:S(2)}) collective-permute-start(bf16[4,1,96,768]{3,2,1,0:T(8,128)(2,1)S(1)} %get-tuple-element.320), channel_id=1, source_target_pairs={{0,8},{4,12},{8,0},{12,4},{16,24},{20,28},{24,16},{28,20},{1,9},{5... | collective-permute-start | bytes 1769480 | tf_op jit(solution)/shard_map/ppermute | solution.py:79
  232.7 18.7 %collective-permute-start.31 = (bf16[2,768,768]{2,1,0:T(8,128)(2,1)}, bf16[2,768,768]{2,1,0:T(8,128)(2,1)}, u32[]{:S(2)}, u32[]{:S(2)}) collective-permute-start(bf16[2,768,768]{2,1,0:T(8,128)(2,1)} %get-tuple-element.339), channel_id=1, source_target_pairs={{0,1},{1,0},{2,3},{3,2},{4,5},{5,4},{6,7},{7,6},{8,9},{9,8},{10,11... | collective-permute-start | bytes 7077896 | tf_op jit(solution)/shard_map/ppermute | solution.py:79
  232.7 37.6 %all-to-all-start.3 = ((bf16[8,96,768]{2,1,0:T(8,128)(2,1)}), bf16[8,96,768]{2,1,0:T(8,128)(2,1)}, u32[]{:S(2)}, u32[]{:S(2)}) async-start(bf16[8,96,768]{2,1,0:T(8,128)(2,1)} %bitcast.79), calls=%async_computation.3 | async-start | bytes 2359296 | tf_op jit(solution)/shard_map/all_to_all | solution.py:1165
  240.9 28.4 %collective-permute-start.35 = (bf16[8,96,768]{2,1,0:T(8,128)(2,1)S(1)}, bf16[8,96,768]{2,1,0:T(8,128)(2,1)S(1)}, u32[]{:S(2)}, u32[]{:S(2)}) collective-permute-start(bf16[8,96,768]{2,1,0:T(8,128)(2,1)S(1)} %get-tuple-element.424.a), channel_id=1, source_target_pairs={{0,2},{1,3},{2,0},{3,1},{4,6},{5,7},{6,4},{7,5},{8,10},{9,11},{10,... | collective-permute-start | bytes 3538952 | tf_op jit(solution)/shard_map/ppermute | solution.py:79
  241.9 28.5 %collective-permute-start.34 = (bf16[8,96,768]{2,1,0:T(8,128)(2,1)S(1)}, bf16[8,96,768]{2,1,0:T(8,128)(2,1)}, u32[]{:S(2)}, u32[]{:S(2)}) collective-permute-start(bf16[8,96,768]{2,1,0:T(8,128)(2,1)S(1)} %get-tuple-element.424.a), channel_id=1, source_target_pairs={{0,1},{1,0},{2,3},{3,2},{4,5},{5,4},{6,7},{7,6},{8,9},{9,8},{10,11... | collective-permute-start | bytes 3538952 | tf_op jit(solution)/shard_map/ppermute | solution.py:79
  273.3 20.7 %collective-permute-start.40 = (bf16[4,96,768]{2,1,0:T(8,128)(2,1)}, bf16[4,96,768]{2,1,0:T(8,128)(2,1)S(1)}, u32[]{:S(2)}, u32[]{:S(2)}) collective-permute-start(bf16[4,96,768]{2,1,0:T(8,128)(2,1)} %copy-done.40), channel_id=1, source_target_pairs={{0,4},{4,0},{8,12},{12,8},{16,20},{20,16},{24,28},{28,24},{1,5},{5... | collective-permute-start | bytes 1769480 | tf_op jit(solution)/shard_map/ppermute | solution.py:79
  287.9 21.3 %collective-permute-start.43 = (bf16[4,96,768]{2,1,0:T(8,128)(2,1)}, bf16[4,96,768]{2,1,0:T(8,128)(2,1)S(1)}, u32[]{:S(2)}, u32[]{:S(2)}) collective-permute-start(bf16[4,96,768]{2,1,0:T(8,128)(2,1)} %get-tuple-element.387), channel_id=1, source_target_pairs={{0,4},{4,0},{8,12},{12,8},{16,20},{20,16},{24,28},{28,24},{1,5},{5... | collective-permute-start | bytes 1769480 | tf_op jit(solution)/shard_map/ppermute | solution.py:79
  302.2 24.1 %collective-permute-start.50 = (bf16[448,768]{1,0:T(8,128)(2,1)S(1)}, bf16[448,768]{1,0:T(8,128)(2,1)S(1)}, u32[]{:S(2)}, u32[]{:S(2)}) collective-permute-start(bf16[448,768]{1,0:T(8,128)(2,1)S(1)} %get-tuple-element.433.a), channel_id=1, source_target_pairs={{0,2},{1,3},{2,0},{3,1},{4,6},{5,7},{6,4},{7,5},{8,10},{9,11},{10,... | collective-permute-start | bytes 2064392 | tf_op jit(solution)/shard_map/ppermute | solution.py:79
  303.3 23.0 %collective-permute-start.49 = (bf16[448,768]{1,0:T(8,128)(2,1)S(1)}, bf16[448,768]{1,0:T(8,128)(2,1)S(1)}, u32[]{:S(2)}, u32[]{:S(2)}) collective-permute-start(bf16[448,768]{1,0:T(8,128)(2,1)S(1)} %get-tuple-element.433.a), channel_id=1, source_target_pairs={{0,1},{1,0},{2,3},{3,2},{4,5},{5,4},{6,7},{7,6},{8,9},{9,8},{10,11... | collective-permute-start | bytes 2064392 | tf_op jit(solution)/shard_map/ppermute | solution.py:79
  326.3 27.0 %collective-permute-start.55 = (bf16[8,96,768]{2,1,0:T(8,128)(2,1)S(1)}, bf16[8,96,768]{2,1,0:T(8,128)(2,1)}, u32[]{:S(2)}, u32[]{:S(2)}) collective-permute-start(bf16[8,96,768]{2,1,0:T(8,128)(2,1)S(1)} %get-tuple-element.446.a), channel_id=1, source_target_pairs={{0,2},{1,3},{2,0},{3,1},{4,6},{5,7},{6,4},{7,5},{8,10},{9,11},{10,... | collective-permute-start | bytes 3538952 | tf_op jit(solution)/shard_map/ppermute | solution.py:79
  327.4 25.9 %collective-permute-start.54 = (bf16[8,96,768]{2,1,0:T(8,128)(2,1)S(1)}, bf16[8,96,768]{2,1,0:T(8,128)(2,1)S(1)}, u32[]{:S(2)}, u32[]{:S(2)}) collective-permute-start(bf16[8,96,768]{2,1,0:T(8,128)(2,1)S(1)} %get-tuple-element.446.a), channel_id=1, source_target_pairs={{0,1},{1,0},{2,3},{3,2},{4,5},{5,4},{6,7},{7,6},{8,9},{9,8},{10,11... | collective-permute-start | bytes 3538952 | tf_op jit(solution)/shard_map/ppermute | solution.py:79
  327.9 23.2 %collective-permute-start.52 = (bf16[3,1,96,768]{3,2,0,1:T(8,128)(2,1)}, bf16[3,1,96,768]{3,2,0,1:T(8,128)(2,1)S(1)}, u32[]{:S(2)}, u32[]{:S(2)}) collective-permute-start(bf16[3,1,96,768]{3,2,0,1:T(8,128)(2,1)} %bitcast.84), channel_id=1, source_target_pairs={{0,16},{4,20},{8,24},{12,28},{16,0},{20,4},{24,8},{28,12},{1,17},{... | collective-permute-start | bytes 1327112 | tf_op jit(solution)/shard_map/ppermute | solution.py:79
  330.3 20.8 %collective-permute-start.53 = (f32[4,768]{1,0:T(4,128)S(1)}, f32[4,768]{1,0:T(4,128)S(1)}, u32[]{:S(2)}, u32[]{:S(2)}) collective-permute-start(f32[4,768]{1,0:T(4,128)S(1)} %add.59), channel_id=1, source_target_pairs={{0,16},{4,20},{8,24},{12,28},{16,0},{20,4},{24,8},{28,12},{1,17},{... | collective-permute-start | bytes 36872 | tf_op jit(solution)/shard_map/ppermute | solution.py:79
  (117 other events, 1223.8 us)
